TPU v7x, 32 devices: a whole 2x2x4 slice. The times are simulated.
32 devices in a mesh: img: 4 (over y, core), cell: 8 (over z, x).
Axes of the slice: x: 2, y: 2, z: 4, core: 2. Of those that a mesh axis runs over, the one named last changes fastest.
Arguments:
- attributes: float32 [59, 262144], P(None, ('img', 'cell')), may hold values from -5 to 2, as said below
- camera: float32 [3, 3], replicated, may hold values from -6 to 5, as said below
- target: float32 [3, 128, 2048], P(None, 'img', 'cell'), may hold values from 0 to 1
- visible_index: int32 [32, 2048], P(('img', 'cell')), may hold values from 0 to 8191
- tile_lists: int32 [8, 128, 128], P('img', 'cell'), may hold values from 0 to 2047
- tile_len: int32 [8, 128], P('img', 'cell'), may hold values from 16 to 128
Outputs:
- gradient: float32 [59, 262144], P(None, ('img', 'cell'))
Inputs may be any that keep to these rules, and one draw needn't show every extreme that they name: `attributes`: rows 0 to 2 (positions) lie within [-1, 1]. `camera`: row 2, the eye, lies 4 or more from the anchor.
All inputs are finite; a program needn't handle non-finite values.
Results may differ from a plain program's by a relative error of at most 0.0003.
Values sent between devices are 32-bit elements; how exact they have to be, the bound alone decides.
No kernel may reach another device: no remote copies, remote signals or barrier semaphores. Data moves between devices by JAX's collectives and lax.ppermute only.
A program may use at most 64 MiB of HBM per device.

v0:
```python
import functools
import math

import jax
import jax.numpy as jnp
import numpy as np
from jax import lax
from jax.experimental import pallas as pl
from jax.experimental.pallas import tpu as pltpu
from jax.sharding import PartitionSpec as P

TILE = 16
LANES = 128
SUBS = 8
GROUP = 8
RIM = 5
HALO = 16
WEIGHT_SSIM = 0.2
SMOOTHING = 0.01
STAB_ONE = 0.0001
STAB_TWO = 0.0009
BLUR_SIGMA = 1.5
LOG2E = 1.4426950408889634
SH_ZERO = 0.28209479177387814
SH_ONE = 0.4886025119029199
SH_TWO = (
    1.0925484305920792,
    -1.0925484305920792,
    0.31539156525252005,
    -1.0925484305920792,
    0.5462742152960396,
)
SH_THREE = (
    -0.5900435899266435,
    2.890611442640554,
    -0.4570457994644658,
    0.3731763325901154,
    -0.4570457994644658,
    1.445305721320277,
    -0.5900435899266435,
)
F32 = jnp.float32
BF16 = jnp.bfloat16
JAC_ROWS = 51
VMEM_BYTES = 56 * 1024 * 1024


def harmonic_basis(unit_x, unit_y, unit_z):
    unit_xx = unit_x * unit_x
    unit_yy = unit_y * unit_y
    unit_zz = unit_z * unit_z
    return [
        -SH_ONE * unit_y,
        SH_ONE * unit_z,
        -SH_ONE * unit_x,
        SH_TWO[0] * unit_x * unit_y,
        SH_TWO[1] * unit_y * unit_z,
        SH_TWO[2] * (2.0 * unit_zz - unit_xx - unit_yy),
        SH_TWO[3] * unit_x * unit_z,
        SH_TWO[4] * (unit_xx - unit_yy),
        SH_THREE[0] * unit_y * (3.0 * unit_xx - unit_yy),
        SH_THREE[1] * unit_x * unit_y * unit_z,
        SH_THREE[2] * unit_y * (4.0 * unit_zz - unit_xx - unit_yy),
        SH_THREE[3] * unit_z * (2.0 * unit_zz - 3.0 * unit_xx - 3.0 * unit_yy),
        SH_THREE[4] * unit_x * (4.0 * unit_zz - unit_xx - unit_yy),
        SH_THREE[5] * unit_z * (unit_xx - unit_yy),
        SH_THREE[6] * unit_x * (unit_xx - 3.0 * unit_yy),
    ]


def three_pieces(value):
    first = value.astype(BF16)
    rest = value - first.astype(F32)
    second = rest.astype(BF16)
    third = (rest - second.astype(F32)).astype(BF16)
    return first, second, third


def two_pieces(value):
    first = value.astype(BF16)
    return first, (value - first.astype(F32)).astype(BF16)


def dot(left, right):
    return jnp.dot(left, right, preferred_element_type=F32)


def dot_nt(left, right):
    return lax.dot_general(left, right, (((1,), (1,)), ((), ())), preferred_element_type=F32)


def dot_full(left, right):
    return jnp.dot(left, right, preferred_element_type=F32, precision=lax.Precision.HIGHEST)


def iota(shape, dim):
    return lax.broadcasted_iota(jnp.int32, shape, dim)


def block_transpose(block):
    turn = (iota(block.shape, 0) - iota(block.shape, 1) // TILE) & (SUBS - 1)
    out = block
    for step in range(1, SUBS):
        moved = pltpu.roll(block, LANES - TILE * step, 1)
        moved = pltpu.roll(moved, step, 0)
        out = jnp.where(turn == step, moved, out)
    return out


def covariance(scale_rows, quat_rows, cam):
    scales = [jnp.exp(row) for row in scale_rows]
    quat_w = 1.5 + jnp.tanh(quat_rows[0])
    quat_x, quat_y, quat_z = quat_rows[1:]
    inverse = lax.rsqrt(quat_w * quat_w + quat_x * quat_x + quat_y * quat_y + quat_z * quat_z)
    quat_w, quat_x, quat_y, quat_z = (
        quat_w * inverse,
        quat_x * inverse,
        quat_y * inverse,
        quat_z * inverse,
    )
    rotation = [
        [
            1.0 - 2.0 * (quat_y * quat_y + quat_z * quat_z),
            2.0 * (quat_x * quat_y - quat_w * quat_z),
            2.0 * (quat_x * quat_z + quat_w * quat_y),
        ],
        [
            2.0 * (quat_x * quat_y + quat_w * quat_z),
            1.0 - 2.0 * (quat_x * quat_x + quat_z * quat_z),
            2.0 * (quat_y * quat_z - quat_w * quat_x),
        ],
        [
            2.0 * (quat_x * quat_z - quat_w * quat_y),
            2.0 * (quat_y * quat_z + quat_w * quat_x),
            1.0 - 2.0 * (quat_x * quat_x + quat_y * quat_y),
        ],
    ]
    axes = [
        [
            (
                cam[screen][0] * rotation[0][axis]
                + cam[screen][1] * rotation[1][axis]
                + cam[screen][2] * rotation[2][axis]
            )
            * scales[axis]
            for axis in range(3)
        ]
        for screen in range(2)
    ]
    first = axes[0][0] * axes[0][0] + axes[0][1] * axes[0][1] + axes[0][2] * axes[0][2] + 0.3
    mixed = axes[0][0] * axes[1][0] + axes[0][1] * axes[1][1] + axes[0][2] * axes[1][2]
    second = axes[1][0] * axes[1][0] + axes[1][1] * axes[1][1] + axes[1][2] * axes[1][2] + 0.3
    return first, mixed, second


def owner_kernel(attr_ref, cam_ref, table_ref, jac_ref, pack_ref, feat_ref):
    count, own = attr_ref.shape
    high = own // LANES
    cam = [[cam_ref[row, col] for col in range(3)] for row in range(3)]
    for first in range(0, count, SUBS):
        number = min(SUBS, count - first)
        for place in range(high):
            pack_ref[pl.ds(first * high + place, number, stride=high), :] = attr_ref[
                first : first + number, place * LANES : (place + 1) * LANES
            ]

    def block(index, carry):
        start = pl.multiple_of(index * SUBS, SUBS)

        def row(number):
            return pack_ref[pl.ds(number * high + start, SUBS), :]

        positions = [row(number) for number in range(3)]
        shape_rows = [row(3 + number) for number in range(7)]
        jac = []
        (cov_first, cov_mixed, cov_second), pull = jax.vjp(
            lambda *rows: covariance(rows[:3], rows[3:], cam), *shape_rows
        )
        one = jnp.ones_like(cov_first)
        zero = jnp.zeros_like(cov_first)
        jac += pull((one, zero, zero))
        jac += pull((zero, one, zero))
        jac += pull((zero, zero, one))
        inverse = 1.0 / (cov_first * cov_second - cov_mixed * cov_mixed)
        conic = [cov_second * inverse, -cov_mixed * inverse, cov_first * inverse]
        centers = []
        slopes = []
        for screen in range(2):
            angle = (
                cam[screen][0] * positions[0]
                + cam[screen][1] * positions[1]
                + cam[screen][2] * positions[2]
            ) / 3.0
            centers.append(7.0 * jnp.sin(angle))
            slopes.append((7.0 / 3.0) * jnp.cos(angle))
        raw = row(10)
        decay = jnp.exp(-raw)
        log_opacity = -jnp.log(1.0 + decay)
        harmonics = [[row(11 + 16 * channel + term) for term in range(16)] for channel in range(3)]

        def colours_of(pos_x, pos_y, pos_z):
            off_x = pos_x - cam[2][0]
            off_y = pos_y - cam[2][1]
            off_z = pos_z - cam[2][2]
            scale = lax.rsqrt(off_x * off_x + off_y * off_y + off_z * off_z)
            basis = harmonic_basis(off_x * scale, off_y * scale, off_z * scale)
            colours = []
            for channel in range(3):
                total = 0.5 + SH_ZERO * harmonics[channel][0]
                for term in range(1, 16):
                    total = total + basis[term - 1] * harmonics[channel][term]
                colours.append(total)
            return tuple(colours), basis

        colours, pull_colours, basis = jax.vjp(colours_of, *positions, has_aux=True)
        jac += pull_colours((one, zero, zero))
        jac += pull_colours((zero, one, zero))
        jac += pull_colours((zero, zero, one))
        jac += slopes
        jac.append(decay / (1.0 + decay))
        jac += basis
        jac += conic
        for number, value in enumerate(jac):
            jac_ref[pl.ds(number * high + start, SUBS), :] = value
        features = centers + conic + [log_opacity] + list(colours)
        for number in range(SUBS):
            feat_ref[pl.ds(start * SUBS + number, SUBS, stride=SUBS), :] = features[number]
        feat_ref[pl.ds(high * SUBS + start, SUBS), :] = features[SUBS]
        return carry

    lax.fori_loop(0, high // SUBS, block, 0)
    for number, piece in enumerate(three_pieces(feat_ref[...])):
        table_ref[:, number * LANES : (number + 1) * LANES] = piece


def fill_numbers(got_ref, row_ref):
    lane_low = iota((1, LANES), 1) < LANES // 2
    for pair in range(got_ref.shape[0] // 2):
        row_ref[:, pair * LANES : (pair + 1) * LANES] = jnp.where(
            lane_low, got_ref[2 * pair : 2 * pair + 1, :], got_ref[2 * pair + 1 : 2 * pair + 2, :]
        )


def reply_kernel(table_ref, got_ref, out_ref, row_ref, wide_ref):
    devices = got_ref.shape[0]
    high = table_ref.shape[0] // (SUBS + 1)
    chunk = 2 * LANES
    half = LANES // 2
    fill_numbers(got_ref, row_ref)

    def step(index, carry):
        numbers = row_ref[:, pl.ds(pl.multiple_of(index * chunk, chunk), chunk)]
        low = numbers & (LANES - 1)
        top = numbers >> 7
        hot = jnp.where(iota((LANES, chunk), 0) == low, 1.0, 0.0).astype(BF16)
        wide_ref[...] = dot(
            table_ref[:, : 2 * LANES], jnp.concatenate([hot, hot], axis=0)
        ) + dot(table_ref[:, 2 * LANES :], hot)
        spread = jnp.broadcast_to(top, (SUBS, chunk))
        picked = jnp.zeros((SUBS, chunk), F32)
        for place in range(high):
            picked = jnp.where(spread == place, wide_ref[place * SUBS : (place + 1) * SUBS, :], picked)
        last = jnp.sum(
            jnp.where(iota((high, chunk), 0) == top, wide_ref[high * SUBS :, :], 0.0),
            axis=0,
            keepdims=True,
        )
        lane_low = iota((SUBS, LANES), 1) < half
        for part in range(chunk // LANES):
            eight = picked[:, part * LANES : (part + 1) * LANES]
            ninth = jnp.broadcast_to(last[:, part * LANES : (part + 1) * LANES], (SUBS, LANES))
            peer = index * 4 + part * 2
            out_ref[peer] = jnp.where(lane_low, eight, pltpu.roll(ninth, half, 1))
            out_ref[peer + 1] = jnp.where(lane_low, pltpu.roll(eight, half, 1), ninth)
        return carry

    lax.fori_loop(0, devices // 4, step, 0)


def render_kernel(
    place_ref, arrived_ref, entry_ref, bias_ref, target_ref, mono_ref,
    image_ref, feat_ref, column_ref, alpha_ref, weight_ref, send_a_ref, send_b_ref,
    wide_ref, coef_ref,
):
    peers = arrived_ref.shape[0]
    entries = entry_ref.shape[1]
    rows = image_ref.shape[1]
    across = image_ref.shape[2] // LANES
    groups = (rows // TILE) * across
    length = entries // (groups * GROUP)
    half = LANES // 2
    chunk = 512

    table = arrived_ref[...].reshape(peers * SUBS, LANES)
    ninth = arrived_ref[:, 0, :]
    low = iota((peers * SUBS, LANES), 1) < half
    low9 = iota((peers, LANES), 1) < half
    one, two, three = [piece.astype(F32) for piece in three_pieces(table)]
    one9, two9, three9 = [piece.astype(F32) for piece in three_pieces(ninth)]
    left = jnp.concatenate(
        [
            jnp.where(low, one, pltpu.roll(two, half, 1)),
            jnp.where(low9, pltpu.roll(two9, half, 1), one9),
        ],
        axis=0,
    ).astype(BF16)
    left_rest = jnp.concatenate(
        [jnp.where(low, three, 0.0), jnp.where(low9, 0.0, three9)], axis=0
    ).astype(BF16)
    feat_ref[...] = jnp.zeros(feat_ref.shape, F32)
    coef_ref[...] = jnp.zeros(coef_ref.shape, F32)

    def gather(index, carry):
        start = pl.multiple_of(index * chunk, chunk)
        slot = entry_ref[:, pl.ds(start, chunk)]
        within = slot & (half - 1)
        owner = slot >> 6
        hot = jnp.where((iota((LANES, chunk), 0) & (half - 1)) == within, 1.0, 0.0).astype(BF16)
        wide_ref[...] = dot(left, hot) + dot(left_rest, hot)
        spread = jnp.broadcast_to(owner, (SUBS, chunk))
        picked = jnp.zeros((SUBS, chunk), F32)
        for place in range(peers):
            picked = jnp.where(spread == place, wide_ref[place * SUBS : (place + 1) * SUBS, :], picked)
        last = jnp.sum(
            jnp.where(iota((peers, chunk), 0) == owner, wide_ref[peers * SUBS :, :], 0.0),
            axis=0,
            keepdims=True,
        )
        feat_ref[0:SUBS, pl.ds(start, chunk)] = picked
        feat_ref[SUBS : SUBS + 1, pl.ds(start, chunk)] = last
        center_x = picked[0:1]
        center_y = picked[1:2]
        conic_xx = picked[2:3]
        conic_xy = picked[3:4]
        conic_yy = picked[4:5]
        lin_x = conic_xx * center_x + conic_xy * center_y
        lin_y = conic_xy * center_x + conic_yy * center_y
        constant = picked[5:6] - 0.5 * (center_x * lin_x + center_y * lin_y)
        coef_ref[0:1] = (-0.5 * LOG2E) * conic_xx
        coef_ref[1:2] = -LOG2E * conic_xy
        coef_ref[2:3] = (-0.5 * LOG2E) * conic_yy
        coef_ref[3:4] = LOG2E * lin_x
        coef_ref[4:5] = LOG2E * lin_y
        coef_ref[5:6] = LOG2E * constant + bias_ref[:, pl.ds(start, chunk)]
        for number, piece in enumerate(three_pieces(coef_ref[0:SUBS])):
            coef_ref[number * SUBS : (number + 1) * SUBS] = piece.astype(F32)
        coef_ref[24:25] = picked[6:7]
        coef_ref[25:26] = picked[7:8]
        coef_ref[26:27] = last
        columns = jnp.transpose(coef_ref[...])
        coef_ref[0:SUBS] = jnp.zeros((SUBS, chunk), F32)
        column_ref[pl.ds(start, chunk), :] = columns
        alpha_ref[pl.ds(start, chunk), :] = jnp.exp2(dot(columns.astype(BF16), mono_ref[...]))
        return carry

    lax.fori_loop(0, entries // chunk, gather, 0)

    pixels = TILE * TILE
    step_rows = length * GROUP

    def scan(number, carry):
        keeps, sums = carry
        new_keeps = []
        new_sums = []
        for group in range(groups):
            at = pl.ds(pl.multiple_of(group * step_rows + number * GROUP, GROUP), GROUP)
            weight = keeps[group] * alpha_ref[at, :]
            weight_ref[at, :] = weight
            new_keeps.append(keeps[group] - weight)
            columns = column_ref[at, :]
            new_sums.append(
                tuple(
                    sums[group][channel] + weight * columns[:, 24 + channel : 25 + channel]
                    for channel in range(3)
                )
            )
        return tuple(new_keeps), tuple(new_sums)

    zero = jnp.zeros((GROUP, pixels), F32)
    start_keeps = tuple(jnp.ones((GROUP, pixels), F32) for _ in range(groups))
    start_sums = tuple((zero, zero, zero) for _ in range(groups))
    _, sums = lax.fori_loop(0, length, scan, (start_keeps, start_sums), unroll=4)
    for group in range(groups):
        row = (group // across) * TILE
        col = (group % across) * LANES
        for channel in range(3):
            for part in range(2):
                image_ref[
                    channel, row + part * SUBS : row + (part + 1) * SUBS, col : col + LANES
                ] = block_transpose(sums[group][channel][:, part * LANES : (part + 1) * LANES])

    blocks = rows // SUBS
    lane_block = iota((SUBS, LANES), 1) // TILE
    even = place_ref[1] % 2 == 0
    for vector in range(6 * blocks // SUBS):
        at_left = jnp.zeros((SUBS, LANES), F32)
        at_right = jnp.zeros((SUBS, LANES), F32)
        for place in range(SUBS):
            number = vector * SUBS + place
            source = image_ref if number // blocks < 3 else target_ref
            channel = (number // blocks) % 3
            top = (number % blocks) * SUBS
            first = source[channel, top : top + SUBS, 0:LANES]
            final = source[channel, top : top + SUBS, (across - 1) * LANES :]
            if place:
                first = pltpu.roll(first, TILE * place, 1)
            if place != SUBS - 1:
                final = pltpu.roll(final, TILE * (place + 1), 1)
            at_left = jnp.where(lane_block == place, first, at_left)
            at_right = jnp.where(lane_block == place, final, at_right)
        send_a_ref[vector * SUBS : (vector + 1) * SUBS, :] = jnp.where(even, at_right, at_left)
        send_b_ref[vector * SUBS : (vector + 1) * SUBS, :] = jnp.where(even, at_left, at_right)


def strip_kernel(place_ref, got_a_ref, got_b_ref, image_ref, target_ref, side_ref, send_a_ref, send_b_ref):
    rows = image_ref.shape[1]
    cols = image_ref.shape[2]
    blocks = rows // SUBS
    lane_block = iota((SUBS, LANES), 1) // TILE
    even = place_ref[1] % 2 == 0
    for vector in range(6 * blocks // SUBS):
        got_a = got_a_ref[vector * SUBS : (vector + 1) * SUBS, :]
        got_b = got_b_ref[vector * SUBS : (vector + 1) * SUBS, :]
        from_right = jnp.where(even, got_a, got_b)
        from_left = jnp.where(even, got_b, got_a)
        for place in range(SUBS):
            number = vector * SUBS + place
            right = pltpu.roll(from_right, LANES - TILE * place, 1) if place else from_right
            left = from_left
            if place != SUBS - 1:
                left = pltpu.roll(from_left, LANES - TILE * (place + 1), 1)
            top = (number % blocks) * SUBS
            side_ref[number // blocks, top : top + SUBS, :] = jnp.where(
                lane_block == 0, right, jnp.where(lane_block == SUBS - 1, left, 0.0)
            )
    even_row = place_ref[0] % 2 == 0
    for number in range(6):
        source = image_ref if number < 3 else target_ref
        channel = number % 3
        top = source[channel, 0:HALO, :]
        bottom = source[channel, rows - HALO :, :]
        send_a_ref[number, :, 0:cols] = jnp.where(even_row, bottom, top)
        send_b_ref[number, :, 0:cols] = jnp.where(even_row, top, bottom)
        top = side_ref[number, 0:HALO, :]
        bottom = side_ref[number, rows - HALO :, :]
        send_a_ref[number, :, cols:] = jnp.where(even_row, bottom, top)
        send_b_ref[number, :, cols:] = jnp.where(even_row, top, bottom)


def back_kernel(
    place_ref, got_a_ref, got_b_ref, image_ref, target_ref, side_ref, entry_ref, feat_ref,
    column_ref, alpha_ref, weight_ref, down_ref, down_back_ref, across_ref, mono_ref,
    out_ref,
    raw_ref, vert_ref, blur_ref, coef_ref, grad_ref, pair_ref, right_ref, slope_ref, mask_ref, sum_ref,
):
    rows = image_ref.shape[1]
    cols = image_ref.shape[2]
    wide = cols + LANES
    entries = entry_ref.shape[1]
    across = cols // LANES
    groups = (rows // TILE) * across
    length = entries // (groups * GROUP)
    tall = rows + 2 * HALO
    mid = rows + 2 * SUBS
    peers = out_ref.shape[0]
    half = LANES // 2

    even_row = place_ref[0] % 2 == 0
    for number in range(6):
        source = image_ref if number < 3 else target_ref
        raw_ref[number, 0:rows, 0:cols] = source[number % 3]
        raw_ref[number, 0:rows, cols:] = side_ref[number]
        got_a = got_a_ref[number]
        got_b = got_b_ref[number]
        raw_ref[number, rows : rows + HALO, :] = jnp.where(even_row, got_a, got_b)
        raw_ref[number, rows + HALO :, :] = jnp.where(even_row, got_b, got_a)
    down = down_ref[...]
    for channel in range(3):
        shown = raw_ref[channel]
        wanted = raw_ref[3 + channel]
        for number, value in enumerate(
            [shown, wanted, shown * shown, wanted * wanted, shown * wanted]
        ):
            at = (channel * 5 + number) * mid
            vert_ref[at : at + mid, :] = dot_full(down, value)
    for part in range(3):
        at = part * 5 * mid
        blur_ref[at : at + 5 * mid, :] = dot_full(vert_ref[at : at + 5 * mid, :], across_ref[...])
    line = iota((mid, wide), 0) - SUBS + place_ref[0] * rows
    spot = iota((mid, wide), 1)
    spot = jnp.where(spot < cols + half, spot, spot - wide) + place_ref[1] * cols
    inside = (
        (line >= 0) & (line < place_ref[2] * rows) & (spot >= 0) & (spot < place_ref[3] * cols)
    )
    down_back = down_back_ref[...]
    for channel in range(3):
        at = channel * 5 * mid
        mean_r, mean_t, square_r, square_t, cross = [
            blur_ref[at + number * mid : at + (number + 1) * mid, :] for number in range(5)
        ]
        upper_one = 2.0 * mean_r * mean_t + STAB_ONE
        upper_two = 2.0 * (cross - mean_r * mean_t) + STAB_TWO
        lower_one = mean_r * mean_r + mean_t * mean_t + STAB_ONE
        lower_two = (square_r - mean_r * mean_r) + (square_t - mean_t * mean_t) + STAB_TWO
        inv_one = 1.0 / lower_one
        inv_two = 1.0 / lower_two
        inverse = inv_one * inv_two
        value = upper_one * upper_two * inverse
        on_mean = (
            2.0 * mean_t * (upper_two - upper_one) * inverse
            + 2.0 * mean_r * value * (inv_two - inv_one)
        )
        on_square = -value * inv_two
        on_cross = 2.0 * upper_one * inverse
        for number, part in enumerate([on_mean, on_square, on_cross]):
            part = jnp.where(inside, -WEIGHT_SSIM * part, 0.0)
            spot_at = (channel * 3 + number) * rows
            coef_ref[spot_at : spot_at + rows, :] = dot_full(down_back, part)
    for channel in range(3):
        at = channel * 3 * rows
        back = dot_full(coef_ref[at : at + 3 * rows, :], across_ref[:, 0:cols])
        shown = image_ref[channel]
        wanted = target_ref[channel]
        gap = shown - wanted
        grad_ref[channel] = (
            (1.0 - WEIGHT_SSIM) * gap * lax.rsqrt(gap * gap + SMOOTHING * SMOOTHING)
            + back[0:rows]
            + 2.0 * shown * back[rows : 2 * rows]
            + wanted * back[2 * rows :]
        )

    pixels = TILE * TILE
    step_rows = length * GROUP
    mono8 = mono_ref[0:SUBS, :].astype(F32)
    right_ref[...] = jnp.zeros(right_ref.shape, F32)
    right_ref[0:SUBS, 0:pixels] = mono8
    right_ref[0:SUBS, pixels : 2 * pixels] = mono8
    same = iota((SUBS, step_rows), 0) == (iota((SUBS, step_rows), 1) & (GROUP - 1))
    slope_ref[...] = jnp.zeros(slope_ref.shape, F32)

    for group in range(groups):
        row = (group // across) * TILE
        col = (group % across) * LANES
        slopes = []
        for channel in range(3):
            slope = jnp.concatenate(
                [
                    block_transpose(
                        grad_ref[channel, row + part * SUBS : row + (part + 1) * SUBS, col : col + LANES]
                    )
                    for part in range(2)
                ],
                axis=1,
            )
            slopes.append(slope)
            for number, piece in enumerate(two_pieces(slope)):
                at = 16 + 24 * number + SUBS * channel
                right_ref[at : at + SUBS, 2 * pixels : 3 * pixels] = piece.astype(F32)
                right_ref[at : at + SUBS, 3 * pixels :] = piece.astype(F32)

        def step(number, behind):
            at = (length // 2 - 1 - number) * 2 * GROUP
            source = pl.ds(pl.multiple_of(group * step_rows + at, 2 * GROUP), 2 * GROUP)
            alpha = alpha_ref[source, :]
            weight = weight_ref[source, :]
            columns = column_ref[source, :]
            parts = []
            for low in (GROUP, 0):
                ahead = (
                    columns[low : low + GROUP, 24:25] * slopes[0]
                    + columns[low : low + GROUP, 25:26] * slopes[1]
                    + columns[low : low + GROUP, 26:27] * slopes[2]
                )
                change = ahead - behind
                parts.append(weight[low : low + GROUP] * change)
                behind = behind + alpha[low : low + GROUP] * change
            target_at = pl.ds(pl.multiple_of(at, 2 * GROUP), 2 * GROUP)
            high, rest = two_pieces(jnp.concatenate([parts[1], parts[0]], axis=0))
            pair_ref[target_at, 0:pixels] = high
            pair_ref[target_at, pixels : 2 * pixels] = rest
            high, rest = two_pieces(weight)
            pair_ref[target_at, 2 * pixels : 3 * pixels] = high
            pair_ref[target_at, 3 * pixels :] = rest
            return behind

        lax.fori_loop(0, length // 2, step, jnp.zeros((GROUP, pixels), F32), unroll=4)
        moments = jnp.transpose(dot_nt(pair_ref[...], right_ref[...].astype(BF16)))
        here = slice(group * step_rows, (group + 1) * step_rows)
        on_xx = moments[0:1]
        on_xy = moments[1:2]
        on_yy = moments[2:3]
        on_x = moments[3:4]
        on_y = moments[4:5]
        on_one = moments[5:6]
        center_x = feat_ref[0:1, here]
        center_y = feat_ref[1:2, here]
        conic_xx = feat_ref[2:3, here]
        conic_xy = feat_ref[3:4, here]
        conic_yy = feat_ref[4:5, here]
        near_x = on_x - center_x * on_one
        near_y = on_y - center_y * on_one
        slope_ref[0:1, here] = conic_xx * near_x + conic_xy * near_y
        slope_ref[1:2, here] = conic_xy * near_x + conic_yy * near_y
        slope_ref[2:3, here] = -0.5 * (on_xx - center_x * (on_x + near_x))
        slope_ref[3:4, here] = -(on_xy - center_y * on_x - center_x * near_y)
        slope_ref[4:5, here] = -0.5 * (on_yy - center_y * (on_y + near_y))
        slope_ref[5:6, here] = on_one
        for channel in range(3):
            at = 16 + SUBS * channel
            both = moments[at : at + SUBS] + moments[at + 24 : at + 24 + SUBS]
            slope_ref[6 + channel : 7 + channel, here] = jnp.sum(
                jnp.where(same, both, 0.0), axis=0, keepdims=True
            )

    chunk = 512
    tops = peers * SUBS
    sum_ref[...] = jnp.zeros(sum_ref.shape, F32)
    pair_step = iota((2 * SUBS, chunk), 0) // SUBS

    def collect(index, carry):
        start = pl.multiple_of(index * chunk, chunk)
        slot = entry_ref[:, pl.ds(start, chunk)]
        within = slot & (half - 1)
        owner = slot >> 6
        hot = jnp.where((iota((LANES, chunk), 0) & (half - 1)) == within, 1.0, 0.0).astype(BF16)
        values = [
            piece.astype(F32) for piece in two_pieces(slope_ref[0:SUBS, pl.ds(start, chunk)])
        ]
        values = [jnp.concatenate([value, value], axis=0) for value in values]
        offset = jnp.broadcast_to(owner, (2 * SUBS, chunk)) - pair_step
        for place in range(peers // 2):
            hit = offset == 2 * place
            for number in range(2):
                at = number * (tops + peers) + place * 2 * SUBS
                mask_ref[at : at + 2 * SUBS, :] = jnp.where(hit, values[number], 0.0).astype(BF16)
        hit = iota((peers, chunk), 0) == owner
        for number, piece in enumerate(
            two_pieces(slope_ref[SUBS : SUBS + 1, pl.ds(start, chunk)])
        ):
            at = number * (tops + peers) + tops
            mask_ref[at : at + peers, :] = jnp.where(hit, piece.astype(F32), 0.0).astype(BF16)
        sum_ref[...] += dot_nt(mask_ref[...], hot)
        return carry

    lax.fori_loop(0, entries // chunk, collect, 0)
    lane_low = iota((SUBS, LANES), 1) < half
    for place in range(peers):
        at = place * SUBS
        eight = sum_ref[at : at + SUBS, :] + sum_ref[tops + peers + at : tops + peers + at + SUBS, :]
        at = tops + place
        ninth = sum_ref[at : at + 1, :] + sum_ref[tops + peers + at : tops + peers + at + 1, :]
        out_ref[place] = jnp.where(lane_low, eight, jnp.broadcast_to(ninth, (SUBS, LANES)))


def return_kernel(returned_ref, got_ref, jac_ref, cam_ref, grad_ref, row_ref, mask_ref, sum_ref, pack_ref):
    devices = got_ref.shape[0]
    count, own = grad_ref.shape
    high = own // LANES
    half = LANES // 2
    tops = high * SUBS
    part_rows = tops + high
    chunk = 4 * LANES
    cam = [[cam_ref[row, col] for col in range(3)] for row in range(3)]
    fill_numbers(got_ref, row_ref)
    sum_ref[...] = jnp.zeros(sum_ref.shape, F32)
    lane_low = iota((SUBS, LANES), 1) < half
    pair_step = iota((2 * SUBS, chunk), 0) // SUBS

    def collect(index, carry):
        numbers = row_ref[:, pl.ds(pl.multiple_of(index * chunk, chunk), chunk)]
        low = numbers & (LANES - 1)
        top = numbers >> 7
        hot = jnp.where(iota((LANES, chunk), 0) == low, 1.0, 0.0).astype(BF16)
        eights = []
        ninths = []
        for part in range(chunk // LANES):
            first = returned_ref[index * 8 + 2 * part]
            second = returned_ref[index * 8 + 2 * part + 1]
            eights.append(jnp.where(lane_low, first, pltpu.roll(second, half, 1)))
            ninths.append(jnp.where(lane_low, pltpu.roll(first, half, 1), second)[0:1])
        values = [piece.astype(F32) for piece in two_pieces(jnp.concatenate(eights, axis=1))]
        values = [jnp.concatenate([value, value], axis=0) for value in values]
        offset = jnp.broadcast_to(top, (2 * SUBS, chunk)) - pair_step
        for place in range(high // 2):
            hit = offset == 2 * place
            for number in range(2):
                at = number * part_rows + place * 2 * SUBS
                mask_ref[at : at + 2 * SUBS, :] = jnp.where(hit, values[number], 0.0).astype(BF16)
        hit = iota((high, chunk), 0) == top
        for number, piece in enumerate(two_pieces(jnp.concatenate(ninths, axis=1))):
            at = number * part_rows + tops
            mask_ref[at : at + high, :] = jnp.where(hit, piece.astype(F32), 0.0).astype(BF16)
        sum_ref[...] += dot_nt(mask_ref[...], hot)
        return carry

    lax.fori_loop(0, devices * half // chunk, collect, 0)

    def block(index, carry):
        start = pl.multiple_of(index * SUBS, SUBS)

        def jac(number):
            return jac_ref[pl.ds(number * high + start, SUBS), :]

        slopes = []
        for number in range(SUBS):
            at = start * SUBS + number
            slopes.append(
                sum_ref[pl.ds(at, SUBS, stride=SUBS), :]
                + sum_ref[pl.ds(part_rows + at, SUBS, stride=SUBS), :]
            )
        at = tops + start
        slopes.append(sum_ref[pl.ds(at, SUBS), :] + sum_ref[pl.ds(part_rows + at, SUBS), :])
        on_center = [slopes[0] * jac(30), slopes[1] * jac(31)]
        conic_xx = jac(48)
        conic_xy = jac(49)
        conic_yy = jac(50)
        on_xx, on_xy, on_yy = slopes[2:5]
        first_x = conic_xx * on_xx + conic_xy * on_xy
        first_y = conic_xy * on_xy + conic_yy * on_yy
        on_first = -(conic_xx * first_x + conic_xy * conic_xy * on_yy)
        on_second = -(conic_xy * conic_xy * on_xx + conic_yy * first_y)
        on_mixed = -(
            2.0 * conic_xx * conic_xy * on_xx
            + (conic_xx * conic_yy + conic_xy * conic_xy) * on_xy
            + 2.0 * conic_xy * conic_yy * on_yy
        )
        out = []
        for axis in range(3):
            out.append(
                cam[0][axis] * on_center[0]
                + cam[1][axis] * on_center[1]
                + slopes[6] * jac(21 + axis)
                + slopes[7] * jac(24 + axis)
                + slopes[8] * jac(27 + axis)
            )
        for number in range(7):
            out.append(
                on_first * jac(number) + on_mixed * jac(7 + number) + on_second * jac(14 + number)
            )
        out.append(slopes[5] * jac(32))
        for channel in range(3):
            out.append(SH_ZERO * slopes[6 + channel])
            for term in range(1, 16):
                out.append(slopes[6 + channel] * jac(32 + term))
        for number, value in enumerate(out):
            pack_ref[pl.ds(number * high + start, SUBS), :] = value
        return carry

    lax.fori_loop(0, high // SUBS, block, 0)
    for first in range(0, count, SUBS):
        number = min(SUBS, count - first)
        for place in range(high):
            grad_ref[first : first + number, place * LANES : (place + 1) * LANES] = pack_ref[
                pl.ds(first * high + place, number, stride=high), :
            ]


def band(outs, ins):
    taps = np.exp(-((np.arange(11) - 5.0) ** 2) / (2.0 * BLUR_SIGMA * BLUR_SIGMA))
    offset = np.asarray(ins)[None, :] - np.asarray(outs)[:, None]
    values = np.exp(-(offset**2) / (2.0 * BLUR_SIGMA * BLUR_SIGMA)) / taps.sum()
    return np.where(np.abs(offset) <= RIM, values, 0.0).astype(np.float32)


def monomials():
    pixel = np.arange(TILE * TILE)
    x = (pixel % TILE) - 7.5
    y = (pixel // TILE) - 7.5
    eight = np.stack([x * x, x * y, y * y, x, y, x * 0 + 1, x * 0, x * 0])
    return np.concatenate([eight, eight, eight, eight * 0]).astype(np.float32)


def call(body, out_shape, scratch, scalar_at, args, flops):
    in_specs = [
        pl.BlockSpec(memory_space=pltpu.SMEM if number in scalar_at else pltpu.VMEM)
        for number in range(len(args))
    ]
    return pl.pallas_call(
        body,
        out_shape=out_shape,
        in_specs=in_specs,
        out_specs=jax.tree.map(lambda _: pl.BlockSpec(memory_space=pltpu.VMEM), out_shape),
        scratch_shapes=scratch,
        compiler_params=pltpu.CompilerParams(vmem_limit_bytes=VMEM_BYTES),
        cost_estimate=pl.CostEstimate(flops=flops, bytes_accessed=1 << 20, transcendentals=0),
    )(*args)


def swap_pairs(count, first):
    pairs = []
    for low in range(first, count - 1, 2):
        pairs += [(low, low + 1), (low + 1, low)]
    return pairs


def swap(value_a, value_b, axis):
    count = lax.axis_size(axis)
    return (
        lax.ppermute(value_a, axis, swap_pairs(count, 0)),
        lax.ppermute(value_b, axis, swap_pairs(count, 1)),
    )


def exchange(payload):
    return lax.all_to_all(payload, ("img", "cell"), split_axis=0, concat_axis=0, tiled=True)


def shards(attributes, camera, target, visible_index, tile_lists, tile_len):
    img_count = lax.axis_size("img")
    cell_count = lax.axis_size("cell")
    devices = img_count * cell_count
    slots = visible_index.shape[1]
    per_owner = slots // devices
    count, own = attributes.shape
    high = own // LANES
    _, rows, cols = target.shape
    tiles_down, tiles_across, length = tile_lists.shape
    entries = tiles_down * tiles_across * length
    wide = cols + LANES
    mid = rows + 2 * SUBS
    tall = rows + 2 * HALO
    place = jnp.stack(
        [
            lax.axis_index("img"),
            lax.axis_index("cell"),
            jnp.int32(img_count),
            jnp.int32(cell_count),
        ]
    ).astype(jnp.int32)

    asked = visible_index.reshape(devices, per_owner)
    got = exchange(jnp.concatenate([asked, asked], axis=1))

    table, jac = call(
        owner_kernel,
        (
            jax.ShapeDtypeStruct((high * (SUBS + 1), 3 * LANES), BF16),
            jax.ShapeDtypeStruct((JAC_ROWS * high, LANES), F32),
        ),
        [pltpu.VMEM((count * high, LANES), F32), pltpu.VMEM((high * (SUBS + 1), LANES), F32)],
        (1,),
        (attributes, camera),
        1 << 24,
    )
    reply = call(
        reply_kernel,
        jax.ShapeDtypeStruct((devices, SUBS, LANES), F32),
        [pltpu.VMEM((1, slots), jnp.int32), pltpu.VMEM((high * (SUBS + 1), 2 * LANES), F32)],
        (),
        (table, got),
        1 << 24,
    )
    arrived = exchange(reply)

    order = (tiles_down, tiles_across // GROUP, GROUP, length)
    entry = tile_lists.reshape(order).transpose(0, 1, 3, 2).reshape(1, entries)
    live = jnp.arange(length, dtype=jnp.int32)[None, None, :, None] < tile_len.reshape(
        tiles_down, tiles_across // GROUP, 1, GROUP
    )
    bias = jnp.where(live, 0.0, -1e30).astype(F32).reshape(1, entries)
    mono = jnp.asarray(monomials()).astype(BF16)
    packed = 6 * rows // SUBS
    big = jax.ShapeDtypeStruct((entries, TILE * TILE), F32)
    strip = jax.ShapeDtypeStruct((packed, LANES), F32)
    image, feat, column, alpha, weight, send_a, send_b = call(
        render_kernel,
        (
            jax.ShapeDtypeStruct((3, rows, cols), F32),
            jax.ShapeDtypeStruct((2 * SUBS, entries), F32),
            jax.ShapeDtypeStruct((entries, 32), F32),
            big,
            big,
            strip,
            strip,
        ),
        [pltpu.VMEM((devices * (SUBS + 1), 512), F32), pltpu.VMEM((32, 512), F32)],
        (0,),
        (place, arrived, entry, bias, target, mono),
        1 << 26,
    )
    got_a, got_b = swap(send_a, send_b, "cell")
    edge = jax.ShapeDtypeStruct((6, HALO, wide), F32)
    side, send_a, send_b = call(
        strip_kernel,
        (jax.ShapeDtypeStruct((6, rows, LANES), F32), edge, edge),
        [],
        (0,),
        (place, got_a, got_b, image, target),
        1 << 20,
    )
    got_a, got_b = swap(send_a, send_b, "img")

    tall_at = np.arange(tall)
    tall_at = np.where(tall_at < rows + HALO, tall_at, tall_at - tall)
    mid_at = np.arange(mid) - SUBS
    wide_at = np.arange(wide)
    wide_at = np.where(wide_at < cols + LANES // 2, wide_at, wide_at - wide)
    down = jnp.asarray(band(mid_at, tall_at))
    down_back = jnp.asarray(band(np.arange(rows), mid_at))
    across = jnp.asarray(band(wide_at, wide_at))
    pixels = TILE * TILE
    group_rows = length * GROUP
    slot_grads = call(
        back_kernel,
        jax.ShapeDtypeStruct((devices, SUBS, LANES), F32),
        [
            pltpu.VMEM((6, tall, wide), F32),
            pltpu.VMEM((15 * mid, wide), F32),
            pltpu.VMEM((15 * mid, wide), F32),
            pltpu.VMEM((9 * rows, wide), F32),
            pltpu.VMEM((3, rows, cols), F32),
            pltpu.VMEM((group_rows, 4 * pixels), BF16),
            pltpu.VMEM((64, 4 * pixels), F32),
            pltpu.VMEM((2 * SUBS, entries), F32),
            pltpu.VMEM((2 * devices * (SUBS + 1), 512), BF16),
            pltpu.VMEM((2 * devices * (SUBS + 1), LANES), F32),
        ],
        (0,),
        (
            place, got_a, got_b, image, target, side, entry, feat, column, alpha, weight,
            down, down_back, across, mono,
        ),
        1 << 27,
    )
    returned = exchange(slot_grads)
    return call(
        return_kernel,
        jax.ShapeDtypeStruct((count, own), F32),
        [
            pltpu.VMEM((1, slots), jnp.int32),
            pltpu.VMEM((2 * high * (SUBS + 1), 4 * LANES), BF16),
            pltpu.VMEM((2 * high * (SUBS + 1), LANES), F32),
            pltpu.VMEM((count * high, LANES), F32),
        ],
        (3,),
        (returned, got, jac, camera),
        1 << 26,
    )


def solution(mesh):
    return jax.shard_map(
        shards,
        mesh=mesh,
        in_specs=(
            P(None, ("img", "cell")),
            P(),
            P(None, "img", "cell"),
            P(("img", "cell"), None),
            P("img", "cell", None),
            P("img", "cell"),
        ),
        out_specs=P(None, ("img", "cell")),
        check_vma=False,
    )
```

profile of v0, /device:TPU:0, one launch (start us, length us, event | category | flops | bytes accessed | tf_op | source)
XLA Modules:
  0.0 110.8 jit_solution(8804946007583185034)
XLA Ops:
  0.0 0.0 copy-start.4
  0.0 0.5 broadcast.25
  0.5 1.4 %reduce.3 = s32[2048]{0:T(1024)S(1)} reduce(s32[1,2048]{1,0:T(1,128)} %param.13, s32[]{:T(128)} %broadcast.25), dimensions={0}, to_apply=%param.13.reduce_sub_computation.3 | reduce | bytes 16388 | tf_op args[3]
  1.9 0.1 reshape.42
  2.0 0.7 pad_add_fusion
  2.6 7.3 %all-to-all-start = ((s32[32,1,128]{2,1,0:T(1,128)}), s32[32,1,128]{2,1,0:T(1,128)S(1)}, u32[]{:S(2)}, u32[]{:S(2)}) async-start(s32[32,1,128]{2,1,0:T(1,128)} %bitcast.2), calls=%async_computation | async-start | bytes 32768 | tf_op jit(solution)/shard_map/all_to_all | solution.py:805
  9.9 0.8 lt.24
  10.7 5.8 %shard_map.100 = (bf16[576,384]{1,0:T(8,128)(2,1)}, f32[3264,128]{1,0:T(8,128)}) custom-call(f32[59,8192]{1,0:T(8,128)} %attr_ref.1, f32[3,3]{1,0:T(4,128)} %cam_ref.3), custom_call_target="tpu_custom_call" | custom-call | flops 16777216 | bytes 1048576 | tf_op jit(solution)/shard_map/pallas_call | solution.py:778
  16.5 0.6 all-to-all-done
  17.0 0.0 copy-start.1
  17.1 0.6 copy-done.1
  17.6 5.0 %shard_map.101 = f32[32,8,128]{2,1,0:T(8,128)} custom-call(bf16[576,384]{1,0:T(8,128)(2,1)} %get-tuple-element.17.table_ref, s32[32,128]{1,0:T(8,128)} %bitcast.11), custom_call_target="tpu_custom_call" | custom-call | flops 16777216 | bytes 1048576 | tf_op jit(solution)/shard_map/pallas_call | solution.py:778
  22.6 5.3 %all-to-all-start.1 = ((f32[32,8,128]{2,1,0:T(8,128)}), f32[32,8,128]{2,1,0:T(8,128)S(1)}, u32[]{:S(2)}, u32[]{:S(2)}) async-start(f32[32,8,128]{2,1,0:T(8,128)} %shard_map.101), calls=%async_computation.1 | async-start | bytes 262144 | tf_op jit(solution)/shard_map/all_to_all | solution.py:805
  27.9 0.8 select_n.15.bias_ref
  28.7 0.0 copy-done.4
  28.7 0.1 copy.13
  28.8 0.8 reshape.44.entry_ref
  29.6 0.6 pad_add_fusion.1.place_ref
  30.2 5.4 %all-to-all-done.1.arrived_ref = f32[32,8,128]{2,1,0:T(8,128)S(1)} async-done(((f32[32,8,128]{2,1,0:T(8,128)}), f32[32,8,128]{2,1,0:T(8,128)S(1)}, u32[]{:S(2)}, u32[]{:S(2)}) %all-to-all-start.1) | async-done | bytes 131104 | tf_op jit(solution)/shard_map/all_to_all | solution.py:805
  35.6 0.0 copy-start
  35.6 0.7 copy-done
  36.3 15.5 %shard_map.102 = (f32[3,32,256]{2,1,0:T(8,128)}, f32[16,4096]{1,0:T(8,128)}, f32[4096,32]{1,0:T(8,128)}, f32[4096,256]{1,0:T(8,128)}, f32[4096,256]{1,0:T(8,128)}, /*index=5*/f32[24,128]{1,0:T(8,128)}, f32[24,128]{1,0:T(8,128)}) custom-call(s32[4]{0:T(128)} %pad_add_fusion.1.place_ref, f32[32,8,128]{2,1,0:T(8,128)} %copy-done, s32[1,4096]{1,0:T(1,128)} %reshape.44.entry_ref, ...), custom_call_target="tpu_custom_call" | custom-call | flops 67108864 | bytes 1048576 | tf_op jit(solution)/shard_map/pallas_call | solution.py:778
  51.8 1.2 %collective-permute-start = (f32[24,128]{1,0:T(8,128)}, f32[24,128]{1,0:T(8,128)S(1)}, u32[]{:S(2)}, u32[]{:S(2)}) collective-permute-start(f32[24,128]{1,0:T(8,128)} %get-tuple-element.18), channel_id=1, source_target_pairs={{0,1},{1,0},{2,3},{3,2},{4,5},{5,4},{6,7},{7,6},{8,9},{9,8},{10,11... | collective-permute-start | bytes 36872 | tf_op jit(solution)/shard_map/ppermute | solution.py:799
  53.0 0.7 collective-permute-start.1
  53.7 2.0 %collective-permute-done.got_a_ref = f32[24,128]{1,0:T(8,128)S(1)} collective-permute-done((f32[24,128]{1,0:T(8,128)}, f32[24,128]{1,0:T(8,128)S(1)}, u32[]{:S(2)}, u32[]{:S(2)}) %collective-permute-start) | collective-permute-done | bytes 12320 | tf_op jit(solution)/shard_map/ppermute | solution.py:799
  55.7 0.0 copy-start.5
  55.7 0.0 collective-permute-done.1.got_b_ref
  55.7 0.0 copy-start.6
  55.7 0.6 copy-done.5
  56.3 0.0 copy-done.6
  56.3 1.9 %shard_map.103 = (f32[6,32,128]{2,1,0:T(8,128)}, f32[6,16,384]{2,1,0:T(8,128)}, f32[6,16,384]{2,1,0:T(8,128)}) custom-call(s32[4]{0:T(128)} %pad_add_fusion.1.place_ref, f32[24,128]{1,0:T(8,128)} %copy-done.5, f32[24,128]{1,0:T(8,128)} %copy-done.6, f32[3,32,256]{2,1,0:T(8,128)} %get-tuple-element.20.image_ref, f32[3,32,256]{2,1,0:T(8,128)} %target_ref.5), custom_call_target="tpu_custom_call" | custom-call | flops 1048576 | bytes 1048576 | tf_op jit(solution)/shard_map/pallas_call | solution.py:778
  58.2 0.0 collective-permute-start.2
  58.2 0.8 collective-permute-start.3
  59.0 0.7 collective-permute-done.2.got_a_ref
  59.7 0.0 copy-start.2
  59.7 0.0 collective-permute-done.3.got_b_ref
  59.8 0.0 copy-start.3
  59.8 0.6 copy-done.2
  60.4 0.1 copy-done.3
  60.5 24.8 %shard_map.104 = f32[32,8,128]{2,1,0:T(8,128)} custom-call(s32[4]{0:T(128)} %pad_add_fusion.1.place_ref, f32[6,16,384]{2,1,0:T(8,128)} %copy-done.2, f32[6,16,384]{2,1,0:T(8,128)} %copy-done.3, f32[3,32,256]{2,1,0:T(8,128)} %get-tuple-element.20.image_ref, f32[3,32,256]{2,1,0:T(8,128)} %target_ref.5, f32[6,32,128]{2,1,0:T(8,128)} %get-tuple-element.23.side_ref, ...), custom_call_target="tpu_custom_call" | custom-call | flops 134217728 | bytes 1048576 | tf_op jit(solution)/shard_map/pallas_call | solution.py:778
  85.2 18.9 %all_to_all.21.returned_ref = f32[32,8,128]{2,1,0:T(8,128)} all-to-all(f32[32,8,128]{2,1,0:T(8,128)} %shard_map.104), channel_id=1, replica_groups=mesh['img'=4,'cell'=8] {'img','cell'}, dimensions={0} | all-to-all | bytes 262144 | tf_op jit(solution)/shard_map/all_to_all | solution.py:805
  104.2 6.6 %shard_map.105 = f32[59,8192]{1,0:T(8,128)} custom-call(f32[32,8,128]{2,1,0:T(8,128)} %all_to_all.21.returned_ref, s32[32,128]{1,0:T(8,128)} %bitcast.12, f32[3264,128]{1,0:T(8,128)} %get-tuple-element.28.jac_ref, f32[3,3]{1,0:T(4,128)} %cam_ref.3), custom_call_target="tpu_custom_call" | custom-call | flops 67108864 | bytes 1048576 | tf_op jit(solution)/shard_map/pallas_call | solution.py:778
  (1 shorter events, 0.0 us)
Async XLA Ops:
  0.0 28.7 %copy-start.4 = (s32[2,16,128]{2,1,0:T(8,128)S(1)}, s32[2,16,128]{2,1,0:T(8,128)}, u32[]{:S(2)}) copy-start(s32[2,16,128]{2,1,0:T(8,128)} %param.14) | copy-start | bytes 49156
  2.6 14.4 %all-to-all-start = ((s32[32,1,128]{2,1,0:T(1,128)}), s32[32,1,128]{2,1,0:T(1,128)S(1)}, u32[]{:S(2)}, u32[]{:S(2)}) async-start(s32[32,1,128]{2,1,0:T(1,128)} %bitcast.2), calls=%async_computation | async-start | bytes 32768 | tf_op jit(solution)/shard_map/all_to_all | solution.py:805
  17.0 0.6 copy-start.1
  22.6 13.0 %all-to-all-start.1 = ((f32[32,8,128]{2,1,0:T(8,128)}), f32[32,8,128]{2,1,0:T(8,128)S(1)}, u32[]{:S(2)}, u32[]{:S(2)}) async-start(f32[32,8,128]{2,1,0:T(8,128)} %shard_map.101), calls=%async_computation.1 | async-start | bytes 262144 | tf_op jit(solution)/shard_map/all_to_all | solution.py:805
  35.6 0.7 copy-start
  51.8 3.9 %collective-permute-start = (f32[24,128]{1,0:T(8,128)}, f32[24,128]{1,0:T(8,128)S(1)}, u32[]{:S(2)}, u32[]{:S(2)}) collective-permute-start(f32[24,128]{1,0:T(8,128)} %get-tuple-element.18), channel_id=1, source_target_pairs={{0,1},{1,0},{2,3},{3,2},{4,5},{5,4},{6,7},{7,6},{8,9},{9,8},{10,11... | collective-permute-start | bytes 36872 | tf_op jit(solution)/shard_map/ppermute | solution.py:799
  53.0 2.7 %collective-permute-start.1 = (f32[24,128]{1,0:T(8,128)}, f32[24,128]{1,0:T(8,128)S(1)}, u32[]{:S(2)}, u32[]{:S(2)}) collective-permute-start(f32[24,128]{1,0:T(8,128)} %get-tuple-element.19), channel_id=1, source_target_pairs={{1,2},{2,1},{3,4},{4,3},{5,6},{6,5},{9,10},{10,9},{11,12},{12,11},... | collective-permute-start | bytes 36872 | tf_op jit(solution)/shard_map/ppermute | solution.py:800
  55.7 0.6 copy-start.5
  55.7 0.6 copy-start.6
  58.2 1.6 %collective-permute-start.2 = (f32[6,16,384]{2,1,0:T(8,128)}, f32[6,16,384]{2,1,0:T(8,128)S(1)}, u32[]{:S(2)}, u32[]{:S(2)}) collective-permute-start(f32[6,16,384]{2,1,0:T(8,128)} %get-tuple-element.21), channel_id=1, source_target_pairs={{0,8},{8,0},{16,24},{24,16},{1,9},{9,1},{17,25},{25,17},{2,10},{10... | collective-permute-start | bytes 442376 | tf_op jit(solution)/shard_map/ppermute | solution.py:799
  58.2 1.6 %collective-permute-start.3 = (f32[6,16,384]{2,1,0:T(8,128)}, f32[6,16,384]{2,1,0:T(8,128)S(1)}, u32[]{:S(2)}, u32[]{:S(2)}) collective-permute-start(f32[6,16,384]{2,1,0:T(8,128)} %get-tuple-element.22), channel_id=1, source_target_pairs={{8,16},{16,8},{9,17},{17,9},{10,18},{18,10},{11,19},{19,11},{12,20... | collective-permute-start | bytes 442376 | tf_op jit(solution)/shard_map/ppermute | solution.py:800
  59.7 0.7 copy-start.2
  59.8 0.7 copy-start.3
where the time goes:
time: 111 us
  Pallas kernels  59.5 us (54%)
  blocking collectives  18.9 us (17%)
  starting transfers between devices  15.3 us (14%)
  waiting for transfers between devices  8.73 us (8%)
  local copies, waits for them, and re-layouts  5.56 us (5%)
  other arithmetic  2.69 us (2%)
    pallas_call x6, Pallas kernels, call(): pl.pallas_call(body, out_shape=out_shape, in_specs=in_specs, out_specs=ja...  59.5 us
    all_to_all x1, blocking collectives, exchange(): lax.all_to_all(payload, ('img', 'cell'), split_axis=0, concat_axis=0, til...  18.9 us
    all_to_all x2, starting transfers between devices, exchange(): lax.all_to_all(payload, ('img', 'cell'), split_axis=0, concat_axis=0, til...  12.6 us
    all_to_all x2, waiting for transfers between devices, exchange(): lax.all_to_all(payload, ('img', 'cell'), split_axis=0, concat_axis=0, til...  5.98 us
    unnamed x15, local copies, waits for them, and re-layouts  3.07 us
    ppermute x2, waiting for transfers between devices, swap(): lax.ppermute(value_a, axis, swap_pairs(count, 0))  2.75 us
  transfers between devices with their start and end apart: 6, of which 4 were waited for; matrix products, arithmetic and copies ran while one was open for 3% of the time, Pallas kernels for 5%

commit v1 on v0

--- a/solution.py
+++ b/solution.py
@@ -277,10 +277,21 @@
     lax.fori_loop(0, devices // 4, step, 0)
 
 
+def spread_colours(feat_ref, start, size):
+    same = iota((GROUP, size), 0) == (iota((GROUP, size), 1) & (GROUP - 1))
+    return jnp.concatenate(
+        [
+            jnp.where(same, feat_ref[6 + channel : 7 + channel, start : start + size], 0.0)
+            for channel in range(3)
+        ],
+        axis=0,
+    )
+
+
 def render_kernel(
     place_ref, arrived_ref, entry_ref, bias_ref, target_ref, mono_ref,
-    image_ref, feat_ref, column_ref, alpha_ref, weight_ref, send_a_ref, send_b_ref,
-    wide_ref, coef_ref,
+    image_ref, feat_ref, alpha_out, weight_out, send_a_ref, send_b_ref,
+    wide_ref, coef_ref, alpha_ref, weight_ref, alpha_sems, weight_sems,
 ):
     peers = arrived_ref.shape[0]
     entries = entry_ref.shape[1]
@@ -307,8 +318,13 @@
     left_rest = jnp.concatenate(
         [jnp.where(low, three, 0.0), jnp.where(low9, 0.0, three9)], axis=0
     ).astype(BF16)
+    left = jnp.concatenate([left, left_rest], axis=1)
     feat_ref[...] = jnp.zeros(feat_ref.shape, F32)
     coef_ref[...] = jnp.zeros(coef_ref.shape, F32)
+
+    def alpha_copy(index):
+        at = pl.ds(pl.multiple_of(index * chunk, chunk), chunk)
+        return pltpu.make_async_copy(alpha_ref.at[at], alpha_out.at[at], alpha_sems.at[index])
 
     def gather(index, carry):
         start = pl.multiple_of(index * chunk, chunk)
@@ -316,7 +332,7 @@
         within = slot & (half - 1)
         owner = slot >> 6
         hot = jnp.where((iota((LANES, chunk), 0) & (half - 1)) == within, 1.0, 0.0).astype(BF16)
-        wide_ref[...] = dot(left, hot) + dot(left_rest, hot)
+        wide_ref[...] = dot(left, jnp.concatenate([hot, hot], axis=0))
         spread = jnp.broadcast_to(owner, (SUBS, chunk))
         picked = jnp.zeros((SUBS, chunk), F32)
         for place in range(peers):
@@ -344,50 +360,61 @@
         coef_ref[5:6] = LOG2E * constant + bias_ref[:, pl.ds(start, chunk)]
         for number, piece in enumerate(three_pieces(coef_ref[0:SUBS])):
             coef_ref[number * SUBS : (number + 1) * SUBS] = piece.astype(F32)
-        coef_ref[24:25] = picked[6:7]
-        coef_ref[25:26] = picked[7:8]
-        coef_ref[26:27] = last
-        columns = jnp.transpose(coef_ref[...])
-        coef_ref[0:SUBS] = jnp.zeros((SUBS, chunk), F32)
-        column_ref[pl.ds(start, chunk), :] = columns
-        alpha_ref[pl.ds(start, chunk), :] = jnp.exp2(dot(columns.astype(BF16), mono_ref[...]))
+        columns = jnp.transpose(coef_ref[...]).astype(BF16)
+        alpha_ref[pl.ds(start, chunk), :] = jnp.exp2(dot(columns, mono_ref[...]))
+        alpha_copy(index).start()
         return carry
 
     lax.fori_loop(0, entries // chunk, gather, 0)
 
     pixels = TILE * TILE
     step_rows = length * GROUP
-
-    def scan(number, carry):
-        keeps, sums = carry
+    parts = 4
+    part_rows = step_rows // parts
+
+    def weight_copy(group, part):
+        at = pl.ds(group * step_rows + part * part_rows, part_rows)
+        return pltpu.make_async_copy(
+            weight_ref.at[at], weight_out.at[at], weight_sems.at[group * parts + part]
+        )
+
+    def scan(number, keeps):
         new_keeps = []
-        new_sums = []
         for group in range(groups):
-            at = pl.ds(pl.multiple_of(group * step_rows + number * GROUP, GROUP), GROUP)
-            weight = keeps[group] * alpha_ref[at, :]
-            weight_ref[at, :] = weight
-            new_keeps.append(keeps[group] - weight)
-            columns = column_ref[at, :]
-            new_sums.append(
-                tuple(
-                    sums[group][channel] + weight * columns[:, 24 + channel : 25 + channel]
-                    for channel in range(3)
-                )
+            at = pl.ds(
+                pl.multiple_of(group * step_rows + number * 2 * GROUP, 2 * GROUP), 2 * GROUP
             )
-        return tuple(new_keeps), tuple(new_sums)
-
-    zero = jnp.zeros((GROUP, pixels), F32)
-    start_keeps = tuple(jnp.ones((GROUP, pixels), F32) for _ in range(groups))
-    start_sums = tuple((zero, zero, zero) for _ in range(groups))
-    _, sums = lax.fori_loop(0, length, scan, (start_keeps, start_sums), unroll=4)
+            alpha = alpha_ref[at, :]
+            first = keeps[group] * alpha[0:GROUP]
+            keep = keeps[group] - first
+            second = keep * alpha[GROUP:]
+            new_keeps.append(keep - second)
+            high, rest = two_pieces(jnp.concatenate([first, second], axis=0))
+            weight_ref[at, 0:pixels] = high
+            weight_ref[at, pixels:] = rest
+        return tuple(new_keeps)
+
+    keeps = tuple(jnp.ones((GROUP, pixels), F32) for _ in range(groups))
+    steps = length // (2 * parts)
+    for part in range(parts):
+        keeps = lax.fori_loop(part * steps, (part + 1) * steps, scan, keeps, unroll=4)
+        for group in range(groups):
+            weight_copy(group, part).start()
     for group in range(groups):
+        here = slice(group * step_rows, (group + 1) * step_rows)
+        left = jnp.concatenate(
+            two_pieces(spread_colours(feat_ref, group * step_rows, step_rows)), axis=0
+        )
+        sums = dot(left, weight_ref[here, 0:pixels]) + dot(left, weight_ref[here, pixels:])
         row = (group // across) * TILE
         col = (group % across) * LANES
         for channel in range(3):
+            at = channel * GROUP
+            total = sums[at : at + GROUP] + sums[at + 3 * GROUP : at + 4 * GROUP]
             for part in range(2):
                 image_ref[
                     channel, row + part * SUBS : row + (part + 1) * SUBS, col : col + LANES
-                ] = block_transpose(sums[group][channel][:, part * LANES : (part + 1) * LANES])
+                ] = block_transpose(total[:, part * LANES : (part + 1) * LANES])
 
     blocks = rows // SUBS
     lane_block = iota((SUBS, LANES), 1) // TILE
@@ -410,6 +437,11 @@
             at_right = jnp.where(lane_block == place, final, at_right)
         send_a_ref[vector * SUBS : (vector + 1) * SUBS, :] = jnp.where(even, at_right, at_left)
         send_b_ref[vector * SUBS : (vector + 1) * SUBS, :] = jnp.where(even, at_left, at_right)
+    for index in range(entries // chunk):
+        alpha_copy(index).wait()
+    for group in range(groups):
+        for part in range(parts):
+            weight_copy(group, part).wait()
 
 
 def strip_kernel(place_ref, got_a_ref, got_b_ref, image_ref, target_ref, side_ref, send_a_ref, send_b_ref):
@@ -449,9 +481,10 @@
 
 def back_kernel(
     place_ref, got_a_ref, got_b_ref, image_ref, target_ref, side_ref, entry_ref, feat_ref,
-    column_ref, alpha_ref, weight_ref, down_ref, down_back_ref, across_ref, mono_ref,
+    alpha_in, weight_in, down_ref, down_back_ref, across_ref, mono_ref,
     out_ref,
-    raw_ref, vert_ref, blur_ref, coef_ref, grad_ref, pair_ref, right_ref, slope_ref, mask_ref, sum_ref,
+    raw_ref, vert_ref, blur_ref, coef_ref, grad_ref, alpha_ref, weight_ref, ahead_ref, pair_ref,
+    right_ref, slope_ref, mask_ref, sum_ref, sems,
 ):
     rows = image_ref.shape[1]
     cols = image_ref.shape[2]
@@ -465,6 +498,10 @@
     peers = out_ref.shape[0]
     half = LANES // 2
 
+    alpha_copy = pltpu.make_async_copy(alpha_in, alpha_ref, sems.at[0])
+    weight_copy = pltpu.make_async_copy(weight_in, weight_ref, sems.at[1])
+    alpha_copy.start()
+    weight_copy.start()
     even_row = place_ref[0] % 2 == 0
     for number in range(6):
         source = image_ref if number < 3 else target_ref
@@ -531,61 +568,72 @@
 
     pixels = TILE * TILE
     step_rows = length * GROUP
-    mono8 = mono_ref[0:SUBS, :].astype(F32)
-    right_ref[...] = jnp.zeros(right_ref.shape, F32)
-    right_ref[0:SUBS, 0:pixels] = mono8
-    right_ref[0:SUBS, pixels : 2 * pixels] = mono8
+    mono = mono_ref[0 : 2 * SUBS, :]
+    mono = jnp.concatenate([mono, mono], axis=1)
     same = iota((SUBS, step_rows), 0) == (iota((SUBS, step_rows), 1) & (GROUP - 1))
     slope_ref[...] = jnp.zeros(slope_ref.shape, F32)
 
     for group in range(groups):
         row = (group // across) * TILE
         col = (group % across) * LANES
+        start = group * step_rows
         slopes = []
         for channel in range(3):
-            slope = jnp.concatenate(
-                [
+            for part in range(2):
+                slopes.append(
                     block_transpose(
                         grad_ref[channel, row + part * SUBS : row + (part + 1) * SUBS, col : col + LANES]
                     )
-                    for part in range(2)
-                ],
-                axis=1,
-            )
-            slopes.append(slope)
-            for number, piece in enumerate(two_pieces(slope)):
-                at = 16 + 24 * number + SUBS * channel
-                right_ref[at : at + SUBS, 2 * pixels : 3 * pixels] = piece.astype(F32)
-                right_ref[at : at + SUBS, 3 * pixels :] = piece.astype(F32)
-
-        def step(number, behind):
-            at = (length // 2 - 1 - number) * 2 * GROUP
+                )
+        slopes = jnp.concatenate(
+            [jnp.concatenate(slopes[2 * channel : 2 * channel + 2], axis=1) for channel in range(3)],
+            axis=0,
+        )
+        high, rest = [piece.astype(F32) for piece in two_pieces(slopes)]
+        at = group * 6 * GROUP
+        both = jnp.concatenate([high, rest], axis=0)
+        right_ref[at : at + 6 * GROUP, 0:pixels] = both
+        right_ref[at : at + 6 * GROUP, pixels:] = both
+        top, low = [
+            piece.astype(F32)
+            for piece in two_pieces(spread_colours(feat_ref, start, step_rows))
+        ]
+        left = jnp.transpose(jnp.concatenate([top, low, top], axis=0)).astype(BF16)
+        ahead_ref[start : start + step_rows, :] = dot(
+            left, jnp.concatenate([high, high, rest], axis=0).astype(BF16)
+        )
+
+    alpha_copy.wait()
+    weight_copy.wait()
+
+    def step(number, behinds):
+        new_behinds = []
+        at = (length // 2 - 1 - number) * 2 * GROUP
+        for group in range(groups):
             source = pl.ds(pl.multiple_of(group * step_rows + at, 2 * GROUP), 2 * GROUP)
             alpha = alpha_ref[source, :]
-            weight = weight_ref[source, :]
-            columns = column_ref[source, :]
-            parts = []
-            for low in (GROUP, 0):
-                ahead = (
-                    columns[low : low + GROUP, 24:25] * slopes[0]
-                    + columns[low : low + GROUP, 25:26] * slopes[1]
-                    + columns[low : low + GROUP, 26:27] * slopes[2]
-                )
-                change = ahead - behind
-                parts.append(weight[low : low + GROUP] * change)
-                behind = behind + alpha[low : low + GROUP] * change
-            target_at = pl.ds(pl.multiple_of(at, 2 * GROUP), 2 * GROUP)
-            high, rest = two_pieces(jnp.concatenate([parts[1], parts[0]], axis=0))
-            pair_ref[target_at, 0:pixels] = high
-            pair_ref[target_at, pixels : 2 * pixels] = rest
-            high, rest = two_pieces(weight)
-            pair_ref[target_at, 2 * pixels : 3 * pixels] = high
-            pair_ref[target_at, 3 * pixels :] = rest
-            return behind
-
-        lax.fori_loop(0, length // 2, step, jnp.zeros((GROUP, pixels), F32), unroll=4)
-        moments = jnp.transpose(dot_nt(pair_ref[...], right_ref[...].astype(BF16)))
+            ahead = ahead_ref[source, :]
+            weight = weight_ref[source, 0:pixels].astype(F32) + weight_ref[source, pixels:].astype(F32)
+            behind = behinds[group]
+            second = ahead[GROUP:] - behind
+            behind = behind + alpha[GROUP:] * second
+            first = ahead[0:GROUP] - behind
+            new_behinds.append(behind + alpha[0:GROUP] * first)
+            high, rest = two_pieces(weight * jnp.concatenate([first, second], axis=0))
+            pair_ref[source, 0:pixels] = high
+            pair_ref[source, pixels:] = rest
+        return tuple(new_behinds)
+
+    zero = jnp.zeros((GROUP, pixels), F32)
+    lax.fori_loop(0, length // 2, step, tuple(zero for _ in range(groups)), unroll=4)
+
+    for group in range(groups):
         here = slice(group * step_rows, (group + 1) * step_rows)
+        at = group * 6 * GROUP
+        moments = jnp.transpose(dot_nt(pair_ref[here, :], mono))
+        tints = jnp.transpose(
+            dot_nt(weight_ref[here, :], right_ref[at : at + 6 * GROUP, :].astype(BF16))
+        )
         on_xx = moments[0:1]
         on_xy = moments[1:2]
         on_yy = moments[2:3]
@@ -606,8 +654,8 @@
         slope_ref[4:5, here] = -0.5 * (on_yy - center_y * (on_y + near_y))
         slope_ref[5:6, here] = on_one
         for channel in range(3):
-            at = 16 + SUBS * channel
-            both = moments[at : at + SUBS] + moments[at + 24 : at + 24 + SUBS]
+            at = SUBS * channel
+            both = tints[at : at + SUBS] + tints[at + 24 : at + 24 + SUBS]
             slope_ref[6 + channel : 7 + channel, here] = jnp.sum(
                 jnp.where(same, both, 0.0), axis=0, keepdims=True
             )
@@ -770,16 +818,29 @@
     return np.concatenate([eight, eight, eight, eight * 0]).astype(np.float32)
 
 
-def call(body, out_shape, scratch, scalar_at, args, flops):
+def call(body, out_shape, scratch, scalar_at, args, flops, outside=(), outs_outside=()):
     in_specs = [
-        pl.BlockSpec(memory_space=pltpu.SMEM if number in scalar_at else pltpu.VMEM)
+        pl.BlockSpec(
+            memory_space=pltpu.SMEM
+            if number in scalar_at
+            else pl.ANY
+            if number in outside
+            else pltpu.VMEM
+        )
         for number in range(len(args))
     ]
+    if isinstance(out_shape, tuple):
+        out_specs = tuple(
+            pl.BlockSpec(memory_space=pl.ANY if number in outs_outside else pltpu.VMEM)
+            for number in range(len(out_shape))
+        )
+    else:
+        out_specs = pl.BlockSpec(memory_space=pltpu.VMEM)
     return pl.pallas_call(
         body,
         out_shape=out_shape,
         in_specs=in_specs,
-        out_specs=jax.tree.map(lambda _: pl.BlockSpec(memory_space=pltpu.VMEM), out_shape),
+        out_specs=out_specs,
         scratch_shapes=scratch,
         compiler_params=pltpu.CompilerParams(vmem_limit_bytes=VMEM_BYTES),
         cost_estimate=pl.CostEstimate(flops=flops, bytes_accessed=1 << 20, transcendentals=0),
@@ -860,23 +921,32 @@
     bias = jnp.where(live, 0.0, -1e30).astype(F32).reshape(1, entries)
     mono = jnp.asarray(monomials()).astype(BF16)
     packed = 6 * rows // SUBS
-    big = jax.ShapeDtypeStruct((entries, TILE * TILE), F32)
+    pixels = TILE * TILE
+    group_rows = length * GROUP
+    groups = entries // group_rows
     strip = jax.ShapeDtypeStruct((packed, LANES), F32)
-    image, feat, column, alpha, weight, send_a, send_b = call(
+    image, feat, alpha, weight, send_a, send_b = call(
         render_kernel,
         (
             jax.ShapeDtypeStruct((3, rows, cols), F32),
             jax.ShapeDtypeStruct((2 * SUBS, entries), F32),
-            jax.ShapeDtypeStruct((entries, 32), F32),
-            big,
-            big,
+            jax.ShapeDtypeStruct((entries, pixels), F32),
+            jax.ShapeDtypeStruct((entries, 2 * pixels), BF16),
             strip,
             strip,
         ),
-        [pltpu.VMEM((devices * (SUBS + 1), 512), F32), pltpu.VMEM((32, 512), F32)],
+        [
+            pltpu.VMEM((devices * (SUBS + 1), 512), F32),
+            pltpu.VMEM((32, 512), F32),
+            pltpu.VMEM((entries, pixels), F32),
+            pltpu.VMEM((entries, 2 * pixels), BF16),
+            pltpu.SemaphoreType.DMA((entries // 512,)),
+            pltpu.SemaphoreType.DMA((4 * groups,)),
+        ],
         (0,),
         (place, arrived, entry, bias, target, mono),
         1 << 26,
+        outs_outside=(2, 3),
     )
     got_a, got_b = swap(send_a, send_b, "cell")
     edge = jax.ShapeDtypeStruct((6, HALO, wide), F32)
@@ -898,8 +968,6 @@
     down = jnp.asarray(band(mid_at, tall_at))
     down_back = jnp.asarray(band(np.arange(rows), mid_at))
     across = jnp.asarray(band(wide_at, wide_at))
-    pixels = TILE * TILE
-    group_rows = length * GROUP
     slot_grads = call(
         back_kernel,
         jax.ShapeDtypeStruct((devices, SUBS, LANES), F32),
@@ -909,18 +977,23 @@
             pltpu.VMEM((15 * mid, wide), F32),
             pltpu.VMEM((9 * rows, wide), F32),
             pltpu.VMEM((3, rows, cols), F32),
-            pltpu.VMEM((group_rows, 4 * pixels), BF16),
-            pltpu.VMEM((64, 4 * pixels), F32),
+            pltpu.VMEM((entries, pixels), F32),
+            pltpu.VMEM((entries, 2 * pixels), BF16),
+            pltpu.VMEM((entries, pixels), F32),
+            pltpu.VMEM((entries, 2 * pixels), BF16),
+            pltpu.VMEM((groups * 6 * GROUP, 2 * pixels), F32),
             pltpu.VMEM((2 * SUBS, entries), F32),
             pltpu.VMEM((2 * devices * (SUBS + 1), 512), BF16),
             pltpu.VMEM((2 * devices * (SUBS + 1), LANES), F32),
+            pltpu.SemaphoreType.DMA((2,)),
         ],
         (0,),
         (
-            place, got_a, got_b, image, target, side, entry, feat, column, alpha, weight,
+            place, got_a, got_b, image, target, side, entry, feat, alpha, weight,
             down, down_back, across, mono,
         ),
         1 << 27,
+        outside=(8, 9),
     )
     returned = exchange(slot_grads)
     return call(

time: 111 us -> 98.1 us (0.88)
  Pallas kernels: 59.5 us -> 46.2 us
    pallas_call x6, Pallas kernels: 59.5 us -> 46.2 us  [call(): pl.pallas_call(body, out_shape=out_shape, in_specs=in_specs, out_specs=ou...]
  transfers between devices with their start and end apart: 6 -> 6, of which waited for: 4 -> 4; matrix products, arithmetic and copies ran while one was open for 3% -> 3% of each run, Pallas kernels for 5% -> 6%
where the time goes in v1:
time: 98.1 us; the launch traced here: 97.6 us
  Pallas kernels  46.2 us (47%)
  blocking collectives  19 us (19%)
  starting transfers between devices  15.4 us (16%)
  waiting for transfers between devices  8.74 us (9%)
  local copies, waits for them, and re-layouts  5.56 us (6%)
  other arithmetic  2.68 us (3%)
    pallas_call x6, Pallas kernels, call(): pl.pallas_call(body, out_shape=out_shape, in_specs=in_specs, out_specs=ou...  46.2 us
    all_to_all x1, blocking collectives, exchange(): lax.all_to_all(payload, ('img', 'cell'), split_axis=0, concat_axis=0, til...  19 us
    all_to_all x2, starting transfers between devices, exchange(): lax.all_to_all(payload, ('img', 'cell'), split_axis=0, concat_axis=0, til...  12.6 us
    all_to_all x2, waiting for transfers between devices, exchange(): lax.all_to_all(payload, ('img', 'cell'), split_axis=0, concat_axis=0, til...  5.98 us
    unnamed x15, local copies, waits for them, and re-layouts  3.07 us
    ppermute x2, waiting for transfers between devices, swap(): lax.ppermute(value_a, axis, swap_pairs(count, 0))  2.75 us
  transfers between devices with their start and end apart: 6, of which 4 were waited for; matrix products, arithmetic and copies ran while one was open for 3% of the time, Pallas kernels for 6%

profile of v1, /device:TPU:0, one launch (start us, length us, event | category | flops | bytes accessed | tf_op | source)
XLA Modules:
  0.0 97.6 jit_solution(10820111684440305670)
XLA Ops:
  0.0 0.0 copy-start.4
  0.0 0.5 broadcast.25
  0.5 1.4 %reduce.3 = s32[2048]{0:T(1024)S(1)} reduce(s32[1,2048]{1,0:T(1,128)} %param.13, s32[]{:T(128)} %broadcast.25), dimensions={0}, to_apply=%param.13.reduce_sub_computation.3 | reduce | bytes 16388 | tf_op args[3]
  1.9 0.1 reshape.42
  2.0 0.7 pad_add_fusion
  2.6 7.3 %all-to-all-start = ((s32[32,1,128]{2,1,0:T(1,128)}), s32[32,1,128]{2,1,0:T(1,128)S(1)}, u32[]{:S(2)}, u32[]{:S(2)}) async-start(s32[32,1,128]{2,1,0:T(1,128)} %bitcast.2), calls=%async_computation | async-start | bytes 32768 | tf_op jit(solution)/shard_map/all_to_all | solution.py:866
  9.9 0.8 lt.24
  10.7 5.8 %shard_map.100 = (bf16[576,384]{1,0:T(8,128)(2,1)}, f32[3264,128]{1,0:T(8,128)}) custom-call(f32[59,8192]{1,0:T(8,128)} %attr_ref.1, f32[3,3]{1,0:T(4,128)} %cam_ref.3), custom_call_target="tpu_custom_call" | custom-call | flops 16777216 | bytes 1048576 | tf_op jit(solution)/shard_map/pallas_call | solution.py:839
  16.5 0.6 all-to-all-done
  17.0 0.0 copy-start.1
  17.1 0.6 copy-done.1
  17.6 4.9 %shard_map.101 = f32[32,8,128]{2,1,0:T(8,128)} custom-call(bf16[576,384]{1,0:T(8,128)(2,1)} %get-tuple-element.16.table_ref, s32[32,128]{1,0:T(8,128)} %bitcast.11), custom_call_target="tpu_custom_call" | custom-call | flops 16777216 | bytes 1048576 | tf_op jit(solution)/shard_map/pallas_call | solution.py:839
  22.6 5.3 %all-to-all-start.1 = ((f32[32,8,128]{2,1,0:T(8,128)}), f32[32,8,128]{2,1,0:T(8,128)S(1)}, u32[]{:S(2)}, u32[]{:S(2)}) async-start(f32[32,8,128]{2,1,0:T(8,128)} %shard_map.101), calls=%async_computation.1 | async-start | bytes 262144 | tf_op jit(solution)/shard_map/all_to_all | solution.py:866
  27.9 0.8 select_n.15.bias_ref
  28.7 0.0 copy-done.4
  28.7 0.1 copy.13
  28.8 0.8 reshape.44.entry_ref
  29.6 0.6 pad_add_fusion.1.place_ref
  30.2 5.4 %all-to-all-done.1.arrived_ref = f32[32,8,128]{2,1,0:T(8,128)S(1)} async-done(((f32[32,8,128]{2,1,0:T(8,128)}), f32[32,8,128]{2,1,0:T(8,128)S(1)}, u32[]{:S(2)}, u32[]{:S(2)}) %all-to-all-start.1) | async-done | bytes 131104 | tf_op jit(solution)/shard_map/all_to_all | solution.py:866
  35.6 0.0 copy-start
  35.6 0.6 copy-done
  36.3 9.8 %shard_map.102 = (f32[3,32,256]{2,1,0:T(8,128)}, f32[16,4096]{1,0:T(8,128)}, f32[4096,256]{1,0:T(8,128)}, bf16[4096,512]{1,0:T(8,128)(2,1)}, f32[24,128]{1,0:T(8,128)}, /*index=5*/f32[24,128]{1,0:T(8,128)}) custom-call(s32[4]{0:T(128)} %pad_add_fusion.1.place_ref, f32[32,8,128]{2,1,0:T(8,128)} %copy-done, s32[1,4096]{1,0:T(1,128)} %reshape.44.entry_ref, ...), custom_call_target="tpu_custom_call" | custom-call | flops 67108864 | bytes 1048576 | tf_op jit(solution)/shard_map/pallas_call | solution.py:839
  46.1 1.3 %collective-permute-start = (f32[24,128]{1,0:T(8,128)}, f32[24,128]{1,0:T(8,128)S(1)}, u32[]{:S(2)}, u32[]{:S(2)}) collective-permute-start(f32[24,128]{1,0:T(8,128)} %get-tuple-element.17), channel_id=1, source_target_pairs={{0,1},{1,0},{2,3},{3,2},{4,5},{5,4},{6,7},{7,6},{8,9},{9,8},{10,11... | collective-permute-start | bytes 36872 | tf_op jit(solution)/shard_map/ppermute | solution.py:860
  47.4 0.7 collective-permute-start.1
  48.1 2.0 %collective-permute-done.got_a_ref = f32[24,128]{1,0:T(8,128)S(1)} collective-permute-done((f32[24,128]{1,0:T(8,128)}, f32[24,128]{1,0:T(8,128)S(1)}, u32[]{:S(2)}, u32[]{:S(2)}) %collective-permute-start) | collective-permute-done | bytes 12320 | tf_op jit(solution)/shard_map/ppermute | solution.py:860
  50.1 0.0 copy-start.5
  50.1 0.0 collective-permute-done.1.got_b_ref
  50.1 0.0 copy-start.6
  50.1 0.6 copy-done.5
  50.7 0.0 copy-done.6
  50.7 1.9 %shard_map.103 = (f32[6,32,128]{2,1,0:T(8,128)}, f32[6,16,384]{2,1,0:T(8,128)}, f32[6,16,384]{2,1,0:T(8,128)}) custom-call(s32[4]{0:T(128)} %pad_add_fusion.1.place_ref, f32[24,128]{1,0:T(8,128)} %copy-done.5, f32[24,128]{1,0:T(8,128)} %copy-done.6, f32[3,32,256]{2,1,0:T(8,128)} %get-tuple-element.19.image_ref, f32[3,32,256]{2,1,0:T(8,128)} %target_ref.5), custom_call_target="tpu_custom_call" | custom-call | flops 1048576 | bytes 1048576 | tf_op jit(solution)/shard_map/pallas_call | solution.py:839
  52.6 0.0 collective-permute-start.2
  52.6 0.8 collective-permute-start.3
  53.4 0.7 collective-permute-done.2.got_a_ref
  54.1 0.0 copy-start.2
  54.1 0.0 collective-permute-done.3.got_b_ref
  54.2 0.0 copy-start.3
  54.2 0.7 copy-done.2
  54.8 0.0 copy-done.3
  54.9 17.2 %shard_map.104 = f32[32,8,128]{2,1,0:T(8,128)} custom-call(s32[4]{0:T(128)} %pad_add_fusion.1.place_ref, f32[6,16,384]{2,1,0:T(8,128)} %copy-done.2, f32[6,16,384]{2,1,0:T(8,128)} %copy-done.3, f32[3,32,256]{2,1,0:T(8,128)} %get-tuple-element.19.image_ref, f32[3,32,256]{2,1,0:T(8,128)} %target_ref.5, f32[6,32,128]{2,1,0:T(8,128)} %get-tuple-element.22.side_ref, ...), custom_call_target="tpu_custom_call" | custom-call | flops 134217728 | bytes 1048576 | tf_op jit(solution)/shard_map/pallas_call | solution.py:839
  72.0 19.0 %all_to_all.21.returned_ref = f32[32,8,128]{2,1,0:T(8,128)} all-to-all(f32[32,8,128]{2,1,0:T(8,128)} %shard_map.104), channel_id=1, replica_groups=mesh['img'=4,'cell'=8] {'img','cell'}, dimensions={0} | all-to-all | bytes 262144 | tf_op jit(solution)/shard_map/all_to_all | solution.py:866
  91.0 6.6 %shard_map.105 = f32[59,8192]{1,0:T(8,128)} custom-call(f32[32,8,128]{2,1,0:T(8,128)} %all_to_all.21.returned_ref, s32[32,128]{1,0:T(8,128)} %bitcast.12, f32[3264,128]{1,0:T(8,128)} %get-tuple-element.26.jac_ref, f32[3,3]{1,0:T(4,128)} %cam_ref.3), custom_call_target="tpu_custom_call" | custom-call | flops 67108864 | bytes 1048576 | tf_op jit(solution)/shard_map/pallas_call | solution.py:839
  (1 shorter events, 0.0 us)
Async XLA Ops:
  0.0 28.7 %copy-start.4 = (s32[2,16,128]{2,1,0:T(8,128)S(1)}, s32[2,16,128]{2,1,0:T(8,128)}, u32[]{:S(2)}) copy-start(s32[2,16,128]{2,1,0:T(8,128)} %param.14) | copy-start | bytes 49156
  2.6 14.4 %all-to-all-start = ((s32[32,1,128]{2,1,0:T(1,128)}), s32[32,1,128]{2,1,0:T(1,128)S(1)}, u32[]{:S(2)}, u32[]{:S(2)}) async-start(s32[32,1,128]{2,1,0:T(1,128)} %bitcast.2), calls=%async_computation | async-start | bytes 32768 | tf_op jit(solution)/shard_map/all_to_all | solution.py:866
  17.0 0.6 copy-start.1
  22.6 13.0 %all-to-all-start.1 = ((f32[32,8,128]{2,1,0:T(8,128)}), f32[32,8,128]{2,1,0:T(8,128)S(1)}, u32[]{:S(2)}, u32[]{:S(2)}) async-start(f32[32,8,128]{2,1,0:T(8,128)} %shard_map.101), calls=%async_computation.1 | async-start | bytes 262144 | tf_op jit(solution)/shard_map/all_to_all | solution.py:866
  35.6 0.7 copy-start
  46.1 4.0 %collective-permute-start = (f32[24,128]{1,0:T(8,128)}, f32[24,128]{1,0:T(8,128)S(1)}, u32[]{:S(2)}, u32[]{:S(2)}) collective-permute-start(f32[24,128]{1,0:T(8,128)} %get-tuple-element.17), channel_id=1, source_target_pairs={{0,1},{1,0},{2,3},{3,2},{4,5},{5,4},{6,7},{7,6},{8,9},{9,8},{10,11... | collective-permute-start | bytes 36872 | tf_op jit(solution)/shard_map/ppermute | solution.py:860
  47.4 2.7 %collective-permute-start.1 = (f32[24,128]{1,0:T(8,128)}, f32[24,128]{1,0:T(8,128)S(1)}, u32[]{:S(2)}, u32[]{:S(2)}) collective-permute-start(f32[24,128]{1,0:T(8,128)} %get-tuple-element.18), channel_id=1, source_target_pairs={{1,2},{2,1},{3,4},{4,3},{5,6},{6,5},{9,10},{10,9},{11,12},{12,11},... | collective-permute-start | bytes 36872 | tf_op jit(solution)/shard_map/ppermute | solution.py:861
  50.1 0.6 copy-start.5
  50.1 0.6 copy-start.6
  52.6 1.6 %collective-permute-start.2 = (f32[6,16,384]{2,1,0:T(8,128)}, f32[6,16,384]{2,1,0:T(8,128)S(1)}, u32[]{:S(2)}, u32[]{:S(2)}) collective-permute-start(f32[6,16,384]{2,1,0:T(8,128)} %get-tuple-element.20), channel_id=1, source_target_pairs={{0,8},{8,0},{16,24},{24,16},{1,9},{9,1},{17,25},{25,17},{2,10},{10... | collective-permute-start | bytes 442376 | tf_op jit(solution)/shard_map/ppermute | solution.py:860
  52.6 1.6 %collective-permute-start.3 = (f32[6,16,384]{2,1,0:T(8,128)}, f32[6,16,384]{2,1,0:T(8,128)S(1)}, u32[]{:S(2)}, u32[]{:S(2)}) collective-permute-start(f32[6,16,384]{2,1,0:T(8,128)} %get-tuple-element.21), channel_id=1, source_target_pairs={{8,16},{16,8},{9,17},{17,9},{10,18},{18,10},{11,19},{19,11},{12,20... | collective-permute-start | bytes 442376 | tf_op jit(solution)/shard_map/ppermute | solution.py:861
  54.1 0.7 copy-start.2
  54.2 0.7 copy-start.3

commit v2 on v1

--- a/solution.py
+++ b/solution.py
@@ -229,39 +229,56 @@
         return carry
 
     lax.fori_loop(0, high // SUBS, block, 0)
-    for number, piece in enumerate(three_pieces(feat_ref[...])):
+    for number, piece in enumerate(two_pieces(feat_ref[...])):
         table_ref[:, number * LANES : (number + 1) * LANES] = piece
 
 
-def fill_numbers(got_ref, row_ref):
+def ask_kernel(index_ref, out_ref):
+    for pair in range(out_ref.shape[0] // 2):
+        numbers = index_ref[:, pair * LANES : (pair + 1) * LANES]
+        out_ref[2 * pair : 2 * pair + 2, :] = jnp.broadcast_to(numbers, (2, LANES))
+
+
+def fill_numbers(place_ref, got_ref, row_ref):
     lane_low = iota((1, LANES), 1) < LANES // 2
+    odd = (place_ref[0] * place_ref[3] + place_ref[1]) % 2 == 1
     for pair in range(got_ref.shape[0] // 2):
+        first = got_ref[2 * pair : 2 * pair + 1, :]
+        second = got_ref[2 * pair + 1 : 2 * pair + 2, :]
         row_ref[:, pair * LANES : (pair + 1) * LANES] = jnp.where(
-            lane_low, got_ref[2 * pair : 2 * pair + 1, :], got_ref[2 * pair + 1 : 2 * pair + 2, :]
-        )
-
-
-def reply_kernel(table_ref, got_ref, out_ref, row_ref, wide_ref):
+            odd,
+            jnp.where(lane_low, pltpu.roll(first, LANES // 2, 1), second),
+            jnp.where(lane_low, first, pltpu.roll(second, LANES // 2, 1)),
+        )
+
+
+def reply_kernel(place_ref, table_ref, got_in, out_ref, row_ref, wide_ref, got_ref, sems):
+    got_copy = pltpu.make_async_copy(got_in, got_ref, sems.at[0])
+    got_copy.start()
+    got_copy.wait()
     devices = got_ref.shape[0]
     high = table_ref.shape[0] // (SUBS + 1)
     chunk = 2 * LANES
     half = LANES // 2
-    fill_numbers(got_ref, row_ref)
-
-    def step(index, carry):
+    fill_numbers(place_ref, got_ref, row_ref)
+
+    def look(index, slot):
         numbers = row_ref[:, pl.ds(pl.multiple_of(index * chunk, chunk), chunk)]
         low = numbers & (LANES - 1)
         top = numbers >> 7
         hot = jnp.where(iota((LANES, chunk), 0) == low, 1.0, 0.0).astype(BF16)
-        wide_ref[...] = dot(
-            table_ref[:, : 2 * LANES], jnp.concatenate([hot, hot], axis=0)
-        ) + dot(table_ref[:, 2 * LANES :], hot)
+        wide_ref[slot] = dot(table_ref[...], jnp.concatenate([hot, hot], axis=0))
+        return top
+
+    def pick(index, slot, top):
         spread = jnp.broadcast_to(top, (SUBS, chunk))
         picked = jnp.zeros((SUBS, chunk), F32)
         for place in range(high):
-            picked = jnp.where(spread == place, wide_ref[place * SUBS : (place + 1) * SUBS, :], picked)
+            picked = jnp.where(
+                spread == place, wide_ref[slot, place * SUBS : (place + 1) * SUBS, :], picked
+            )
         last = jnp.sum(
-            jnp.where(iota((high, chunk), 0) == top, wide_ref[high * SUBS :, :], 0.0),
+            jnp.where(iota((high, chunk), 0) == top, wide_ref[slot, high * SUBS :, :], 0.0),
             axis=0,
             keepdims=True,
         )
@@ -272,9 +289,14 @@
             peer = index * 4 + part * 2
             out_ref[peer] = jnp.where(lane_low, eight, pltpu.roll(ninth, half, 1))
             out_ref[peer + 1] = jnp.where(lane_low, pltpu.roll(eight, half, 1), ninth)
+
+    def step(index, carry):
+        tops = [look(2 * index + slot, slot) for slot in range(2)]
+        for slot in range(2):
+            pick(2 * index + slot, slot, tops[slot])
         return carry
 
-    lax.fori_loop(0, devices // 4, step, 0)
+    lax.fori_loop(0, devices // 8, step, 0)
 
 
 def spread_colours(feat_ref, start, size):
@@ -289,10 +311,13 @@
 
 
 def render_kernel(
-    place_ref, arrived_ref, entry_ref, bias_ref, target_ref, mono_ref,
+    place_ref, arrived_in, entry_ref, bias_ref, target_ref, mono_ref,
     image_ref, feat_ref, alpha_out, weight_out, send_a_ref, send_b_ref,
-    wide_ref, coef_ref, alpha_ref, weight_ref, alpha_sems, weight_sems,
+    wide_ref, coef_ref, alpha_ref, weight_ref, arrived_ref, alpha_sems, weight_sems, sems,
 ):
+    arrived_copy = pltpu.make_async_copy(arrived_in, arrived_ref, sems.at[0])
+    arrived_copy.start()
+    arrived_copy.wait()
     peers = arrived_ref.shape[0]
     entries = entry_ref.shape[1]
     rows = image_ref.shape[1]
@@ -326,19 +351,23 @@
         at = pl.ds(pl.multiple_of(index * chunk, chunk), chunk)
         return pltpu.make_async_copy(alpha_ref.at[at], alpha_out.at[at], alpha_sems.at[index])
 
-    def gather(index, carry):
+    def look(index, slot_number):
         start = pl.multiple_of(index * chunk, chunk)
         slot = entry_ref[:, pl.ds(start, chunk)]
         within = slot & (half - 1)
         owner = slot >> 6
         hot = jnp.where((iota((LANES, chunk), 0) & (half - 1)) == within, 1.0, 0.0).astype(BF16)
-        wide_ref[...] = dot(left, jnp.concatenate([hot, hot], axis=0))
+        wide_ref[slot_number] = dot(left, jnp.concatenate([hot, hot], axis=0))
+        return owner
+
+    def gather(index, slot_number, owner):
+        start = pl.multiple_of(index * chunk, chunk)
         spread = jnp.broadcast_to(owner, (SUBS, chunk))
         picked = jnp.zeros((SUBS, chunk), F32)
         for place in range(peers):
-            picked = jnp.where(spread == place, wide_ref[place * SUBS : (place + 1) * SUBS, :], picked)
+            picked = jnp.where(spread == place, wide_ref[slot_number, place * SUBS : (place + 1) * SUBS, :], picked)
         last = jnp.sum(
-            jnp.where(iota((peers, chunk), 0) == owner, wide_ref[peers * SUBS :, :], 0.0),
+            jnp.where(iota((peers, chunk), 0) == owner, wide_ref[slot_number, peers * SUBS :, :], 0.0),
             axis=0,
             keepdims=True,
         )
@@ -352,20 +381,25 @@
         lin_x = conic_xx * center_x + conic_xy * center_y
         lin_y = conic_xy * center_x + conic_yy * center_y
         constant = picked[5:6] - 0.5 * (center_x * lin_x + center_y * lin_y)
-        coef_ref[0:1] = (-0.5 * LOG2E) * conic_xx
-        coef_ref[1:2] = -LOG2E * conic_xy
-        coef_ref[2:3] = (-0.5 * LOG2E) * conic_yy
-        coef_ref[3:4] = LOG2E * lin_x
-        coef_ref[4:5] = LOG2E * lin_y
-        coef_ref[5:6] = LOG2E * constant + bias_ref[:, pl.ds(start, chunk)]
-        for number, piece in enumerate(three_pieces(coef_ref[0:SUBS])):
-            coef_ref[number * SUBS : (number + 1) * SUBS] = piece.astype(F32)
-        columns = jnp.transpose(coef_ref[...]).astype(BF16)
+        coef_ref[slot_number, 0:1] = (-0.5 * LOG2E) * conic_xx
+        coef_ref[slot_number, 1:2] = -LOG2E * conic_xy
+        coef_ref[slot_number, 2:3] = (-0.5 * LOG2E) * conic_yy
+        coef_ref[slot_number, 3:4] = LOG2E * lin_x
+        coef_ref[slot_number, 4:5] = LOG2E * lin_y
+        coef_ref[slot_number, 5:6] = LOG2E * constant + bias_ref[:, pl.ds(start, chunk)]
+        for number, piece in enumerate(three_pieces(coef_ref[slot_number, 0:SUBS])):
+            coef_ref[slot_number, number * SUBS : (number + 1) * SUBS] = piece.astype(F32)
+        columns = jnp.transpose(coef_ref[slot_number]).astype(BF16)
         alpha_ref[pl.ds(start, chunk), :] = jnp.exp2(dot(columns, mono_ref[...]))
         alpha_copy(index).start()
+
+    def gather_two(index, carry):
+        owners = [look(2 * index + number, number) for number in range(2)]
+        for number in range(2):
+            gather(2 * index + number, number, owners[number])
         return carry
 
-    lax.fori_loop(0, entries // chunk, gather, 0)
+    lax.fori_loop(0, entries // (2 * chunk), gather_two, 0)
 
     pixels = TILE * TILE
     step_rows = length * GROUP
@@ -444,7 +478,23 @@
             weight_copy(group, part).wait()
 
 
-def strip_kernel(place_ref, got_a_ref, got_b_ref, image_ref, target_ref, side_ref, send_a_ref, send_b_ref):
+def lane_shift(block, shift, axis=1):
+    shift %= block.shape[axis]
+    return pltpu.roll(block, shift, axis) if shift else block
+
+
+def strip_kernel(
+    place_ref, got_a_in, got_b_in, image_ref, target_ref, side_ref, send_a_ref, send_b_ref,
+    got_a_ref, got_b_ref, sems,
+):
+    copies = [
+        pltpu.make_async_copy(got_a_in, got_a_ref, sems.at[0]),
+        pltpu.make_async_copy(got_b_in, got_b_ref, sems.at[1]),
+    ]
+    for copy in copies:
+        copy.start()
+    for copy in copies:
+        copy.wait()
     rows = image_ref.shape[1]
     cols = image_ref.shape[2]
     blocks = rows // SUBS
@@ -457,34 +507,63 @@
         from_left = jnp.where(even, got_b, got_a)
         for place in range(SUBS):
             number = vector * SUBS + place
-            right = pltpu.roll(from_right, LANES - TILE * place, 1) if place else from_right
-            left = from_left
-            if place != SUBS - 1:
-                left = pltpu.roll(from_left, LANES - TILE * (place + 1), 1)
+            right = lane_shift(from_right, -TILE * place)
+            left = lane_shift(from_left, -TILE * (place + 1))
             top = (number % blocks) * SUBS
             side_ref[number // blocks, top : top + SUBS, :] = jnp.where(
                 lane_block == 0, right, jnp.where(lane_block == SUBS - 1, left, 0.0)
             )
+
+    def packed(main, rest, shift):
+        wide_sub = iota((SUBS, cols), 0) // 2
+        side_sub = iota((SUBS, LANES), 0) // 2
+        wides = []
+        sides = []
+        for number in range(6):
+            source = image_ref if number < 3 else target_ref
+            wides.append(source[number % 3, main : main + SUBS, :])
+            sides.append(side_ref[number, main : main + SUBS, :])
+        for first in (0, 4):
+            wide = jnp.zeros((SUBS, cols), F32)
+            side = jnp.zeros((SUBS, LANES), F32)
+            for number in range(first, min(first + 4, 6)):
+                source = image_ref if number < 3 else target_ref
+                turn = 2 * (number - first) - shift
+                block = lane_shift(source[number % 3, rest : rest + SUBS, :], turn, 0)
+                wide = jnp.where(wide_sub == number - first, block, wide)
+                block = lane_shift(side_ref[number, rest : rest + SUBS, :], turn, 0)
+                side = jnp.where(side_sub == number - first, block, side)
+            wides.append(wide)
+            sides.append(side)
+        lane_part = iota((SUBS, LANES), 1) // (2 * TILE)
+        last = []
+        for first in (0, 4):
+            total = jnp.zeros((SUBS, LANES), F32)
+            for part in range(4):
+                moved = lane_shift(sides[first + part], TILE + 2 * TILE * part)
+                total = jnp.where(lane_part == part, moved, total)
+            last.append(total)
+        return wides, last
+
     even_row = place_ref[0] % 2 == 0
-    for number in range(6):
-        source = image_ref if number < 3 else target_ref
-        channel = number % 3
-        top = source[channel, 0:HALO, :]
-        bottom = source[channel, rows - HALO :, :]
-        send_a_ref[number, :, 0:cols] = jnp.where(even_row, bottom, top)
-        send_b_ref[number, :, 0:cols] = jnp.where(even_row, top, bottom)
-        top = side_ref[number, 0:HALO, :]
-        bottom = side_ref[number, rows - HALO :, :]
-        send_a_ref[number, :, cols:] = jnp.where(even_row, bottom, top)
-        send_b_ref[number, :, cols:] = jnp.where(even_row, top, bottom)
+    top, top_last = packed(0, SUBS, 0)
+    bottom, bottom_last = packed(rows - SUBS, rows - 2 * SUBS, 6)
+    for number in range(SUBS):
+        here = slice(number * SUBS, (number + 1) * SUBS)
+        send_a_ref[here, :] = jnp.where(even_row, bottom[number], top[number])
+        send_b_ref[here, :] = jnp.where(even_row, top[number], bottom[number])
+    for number in range(2):
+        here = slice(number * LANES, (number + 1) * LANES)
+        send_a_ref[SUBS * SUBS :, here] = jnp.where(even_row, bottom_last[number], top_last[number])
+        send_b_ref[SUBS * SUBS :, here] = jnp.where(even_row, top_last[number], bottom_last[number])
 
 
 def back_kernel(
-    place_ref, got_a_ref, got_b_ref, image_ref, target_ref, side_ref, entry_ref, feat_ref,
+    place_ref, got_a_in, got_b_in, image_ref, target_ref, side_ref, entry_ref, feat_ref,
     alpha_in, weight_in, down_ref, down_back_ref, across_ref, mono_ref,
     out_ref,
     raw_ref, vert_ref, blur_ref, coef_ref, grad_ref, alpha_ref, weight_ref, ahead_ref, pair_ref,
-    right_ref, slope_ref, mask_ref, sum_ref, sems,
+    right_ref, slope_ref, mask_ref, sum_ref, got_a_ref, got_b_ref, sems,
 ):
     rows = image_ref.shape[1]
     cols = image_ref.shape[2]
@@ -500,29 +579,63 @@
 
     alpha_copy = pltpu.make_async_copy(alpha_in, alpha_ref, sems.at[0])
     weight_copy = pltpu.make_async_copy(weight_in, weight_ref, sems.at[1])
+    got_copies = [
+        pltpu.make_async_copy(got_a_in, got_a_ref, sems.at[2]),
+        pltpu.make_async_copy(got_b_in, got_b_ref, sems.at[3]),
+    ]
+    for copy in got_copies:
+        copy.start()
     alpha_copy.start()
     weight_copy.start()
+    for copy in got_copies:
+        copy.wait()
     even_row = place_ref[0] % 2 == 0
     for number in range(6):
         source = image_ref if number < 3 else target_ref
         raw_ref[number, 0:rows, 0:cols] = source[number % 3]
         raw_ref[number, 0:rows, cols:] = side_ref[number]
-        got_a = got_a_ref[number]
-        got_b = got_b_ref[number]
-        raw_ref[number, rows : rows + HALO, :] = jnp.where(even_row, got_a, got_b)
-        raw_ref[number, rows + HALO :, :] = jnp.where(even_row, got_b, got_a)
+    lane_block = iota((SUBS, LANES), 1) // TILE
+    border = (lane_block == 0) | (lane_block == SUBS - 1)
+    for below in (True, False):
+        def got(rows_here, cols_here):
+            got_a = got_a_ref[rows_here, cols_here]
+            got_b = got_b_ref[rows_here, cols_here]
+            return jnp.where(even_row, got_a, got_b) if below else jnp.where(even_row, got_b, got_a)
+
+        main_at = rows if below else tall - SUBS
+        rest_at = rows + SUBS if below else tall - 2 * SUBS
+        goal = 0 if below else 3
+        wide_keep = iota((SUBS, cols), 0) // 2 == goal
+        side_keep = iota((SUBS, LANES), 0) // 2 == goal
+        wides = [got(slice(number * SUBS, (number + 1) * SUBS), slice(0, cols)) for number in range(SUBS)]
+        lasts = [
+            got(slice(SUBS * SUBS, (SUBS + 1) * SUBS), slice(number * LANES, (number + 1) * LANES))
+            for number in range(2)
+        ]
+        sides = [
+            jnp.where(border, lane_shift(lasts[number // 4], -TILE - 2 * TILE * (number % 4)), 0.0)
+            for number in range(SUBS)
+        ]
+        for number in range(6):
+            raw_ref[number, main_at : main_at + SUBS, 0:cols] = wides[number]
+            raw_ref[number, main_at : main_at + SUBS, cols:] = sides[number]
+            turn = 2 * (goal - number % 4)
+            block = lane_shift(wides[6 + number // 4], turn, 0)
+            raw_ref[number, rest_at : rest_at + SUBS, 0:cols] = jnp.where(wide_keep, block, 0.0)
+            block = lane_shift(sides[6 + number // 4], turn, 0)
+            raw_ref[number, rest_at : rest_at + SUBS, cols:] = jnp.where(side_keep, block, 0.0)
     down = down_ref[...]
     for channel in range(3):
         shown = raw_ref[channel]
         wanted = raw_ref[3 + channel]
         for number, value in enumerate(
-            [shown, wanted, shown * shown, wanted * wanted, shown * wanted]
+            [shown, wanted, shown * shown + wanted * wanted, shown * wanted]
         ):
-            at = (channel * 5 + number) * mid
+            at = (channel * 4 + number) * mid
             vert_ref[at : at + mid, :] = dot_full(down, value)
     for part in range(3):
-        at = part * 5 * mid
-        blur_ref[at : at + 5 * mid, :] = dot_full(vert_ref[at : at + 5 * mid, :], across_ref[...])
+        at = part * 4 * mid
+        blur_ref[at : at + 4 * mid, :] = dot_full(vert_ref[at : at + 4 * mid, :], across_ref[...])
     line = iota((mid, wide), 0) - SUBS + place_ref[0] * rows
     spot = iota((mid, wide), 1)
     spot = jnp.where(spot < cols + half, spot, spot - wide) + place_ref[1] * cols
@@ -531,14 +644,14 @@
     )
     down_back = down_back_ref[...]
     for channel in range(3):
-        at = channel * 5 * mid
-        mean_r, mean_t, square_r, square_t, cross = [
-            blur_ref[at + number * mid : at + (number + 1) * mid, :] for number in range(5)
+        at = channel * 4 * mid
+        mean_r, mean_t, squares, cross = [
+            blur_ref[at + number * mid : at + (number + 1) * mid, :] for number in range(4)
         ]
         upper_one = 2.0 * mean_r * mean_t + STAB_ONE
         upper_two = 2.0 * (cross - mean_r * mean_t) + STAB_TWO
         lower_one = mean_r * mean_r + mean_t * mean_t + STAB_ONE
-        lower_two = (square_r - mean_r * mean_r) + (square_t - mean_t * mean_t) + STAB_TWO
+        lower_two = squares - mean_r * mean_r - mean_t * mean_t + STAB_TWO
         inv_one = 1.0 / lower_one
         inv_two = 1.0 / lower_two
         inverse = inv_one * inv_two
@@ -630,10 +743,8 @@
     for group in range(groups):
         here = slice(group * step_rows, (group + 1) * step_rows)
         at = group * 6 * GROUP
-        moments = jnp.transpose(dot_nt(pair_ref[here, :], mono))
-        tints = jnp.transpose(
-            dot_nt(weight_ref[here, :], right_ref[at : at + 6 * GROUP, :].astype(BF16))
-        )
+        moments = dot_nt(mono, pair_ref[here, :])
+        tints = dot_nt(right_ref[at : at + 6 * GROUP, :].astype(BF16), weight_ref[here, :])
         on_xx = moments[0:1]
         on_xy = moments[1:2]
         on_yy = moments[2:3]
@@ -700,7 +811,7 @@
         out_ref[place] = jnp.where(lane_low, eight, jnp.broadcast_to(ninth, (SUBS, LANES)))
 
 
-def return_kernel(returned_ref, got_ref, jac_ref, cam_ref, grad_ref, row_ref, mask_ref, sum_ref, pack_ref):
+def return_kernel(place_ref, returned_ref, got_ref, jac_ref, cam_ref, grad_ref, row_ref, mask_ref, sum_ref, pack_ref):
     devices = got_ref.shape[0]
     count, own = grad_ref.shape
     high = own // LANES
@@ -709,7 +820,7 @@
     part_rows = tops + high
     chunk = 4 * LANES
     cam = [[cam_ref[row, col] for col in range(3)] for row in range(3)]
-    fill_numbers(got_ref, row_ref)
+    fill_numbers(place_ref, got_ref, row_ref)
     sum_ref[...] = jnp.zeros(sum_ref.shape, F32)
     lane_low = iota((SUBS, LANES), 1) < half
     pair_step = iota((2 * SUBS, chunk), 0) // SUBS
@@ -871,7 +982,6 @@
     cell_count = lax.axis_size("cell")
     devices = img_count * cell_count
     slots = visible_index.shape[1]
-    per_owner = slots // devices
     count, own = attributes.shape
     high = own // LANES
     _, rows, cols = target.shape
@@ -889,13 +999,21 @@
         ]
     ).astype(jnp.int32)
 
-    asked = visible_index.reshape(devices, per_owner)
-    got = exchange(jnp.concatenate([asked, asked], axis=1))
+    assert 2 * (slots // devices) == LANES
+    asked = call(
+        ask_kernel,
+        jax.ShapeDtypeStruct((devices, LANES), jnp.int32),
+        [],
+        (),
+        (visible_index,),
+        1 << 14,
+    )
+    got = exchange(asked)
 
     table, jac = call(
         owner_kernel,
         (
-            jax.ShapeDtypeStruct((high * (SUBS + 1), 3 * LANES), BF16),
+            jax.ShapeDtypeStruct((high * (SUBS + 1), 2 * LANES), BF16),
             jax.ShapeDtypeStruct((JAC_ROWS * high, LANES), F32),
         ),
         [pltpu.VMEM((count * high, LANES), F32), pltpu.VMEM((high * (SUBS + 1), LANES), F32)],
@@ -906,10 +1024,16 @@
     reply = call(
         reply_kernel,
         jax.ShapeDtypeStruct((devices, SUBS, LANES), F32),
-        [pltpu.VMEM((1, slots), jnp.int32), pltpu.VMEM((high * (SUBS + 1), 2 * LANES), F32)],
-        (),
-        (table, got),
+        [
+            pltpu.VMEM((1, slots), jnp.int32),
+            pltpu.VMEM((2, high * (SUBS + 1), 2 * LANES), F32),
+            pltpu.VMEM((devices, LANES), jnp.int32),
+            pltpu.SemaphoreType.DMA((1,)),
+        ],
+        (0,),
+        (place, table, got),
         1 << 24,
+        outside=(2,),
     )
     arrived = exchange(reply)
 
@@ -936,27 +1060,35 @@
             strip,
         ),
         [
-            pltpu.VMEM((devices * (SUBS + 1), 512), F32),
-            pltpu.VMEM((32, 512), F32),
+            pltpu.VMEM((2, devices * (SUBS + 1), 512), F32),
+            pltpu.VMEM((2, 32, 512), F32),
             pltpu.VMEM((entries, pixels), F32),
             pltpu.VMEM((entries, 2 * pixels), BF16),
+            pltpu.VMEM((devices, SUBS, LANES), F32),
             pltpu.SemaphoreType.DMA((entries // 512,)),
             pltpu.SemaphoreType.DMA((4 * groups,)),
+            pltpu.SemaphoreType.DMA((1,)),
         ],
         (0,),
         (place, arrived, entry, bias, target, mono),
         1 << 26,
+        outside=(1,),
         outs_outside=(2, 3),
     )
     got_a, got_b = swap(send_a, send_b, "cell")
-    edge = jax.ShapeDtypeStruct((6, HALO, wide), F32)
+    edge = jax.ShapeDtypeStruct(((SUBS + 1) * SUBS, cols), F32)
     side, send_a, send_b = call(
         strip_kernel,
         (jax.ShapeDtypeStruct((6, rows, LANES), F32), edge, edge),
-        [],
+        [
+            pltpu.VMEM((packed, LANES), F32),
+            pltpu.VMEM((packed, LANES), F32),
+            pltpu.SemaphoreType.DMA((2,)),
+        ],
         (0,),
         (place, got_a, got_b, image, target),
         1 << 20,
+        outside=(1, 2),
     )
     got_a, got_b = swap(send_a, send_b, "img")
 
@@ -973,8 +1105,8 @@
         jax.ShapeDtypeStruct((devices, SUBS, LANES), F32),
         [
             pltpu.VMEM((6, tall, wide), F32),
-            pltpu.VMEM((15 * mid, wide), F32),
-            pltpu.VMEM((15 * mid, wide), F32),
+            pltpu.VMEM((12 * mid, wide), F32),
+            pltpu.VMEM((12 * mid, wide), F32),
             pltpu.VMEM((9 * rows, wide), F32),
             pltpu.VMEM((3, rows, cols), F32),
             pltpu.VMEM((entries, pixels), F32),
@@ -985,7 +1117,9 @@
             pltpu.VMEM((2 * SUBS, entries), F32),
             pltpu.VMEM((2 * devices * (SUBS + 1), 512), BF16),
             pltpu.VMEM((2 * devices * (SUBS + 1), LANES), F32),
-            pltpu.SemaphoreType.DMA((2,)),
+            pltpu.VMEM(((SUBS + 1) * SUBS, cols), F32),
+            pltpu.VMEM(((SUBS + 1) * SUBS, cols), F32),
+            pltpu.SemaphoreType.DMA((4,)),
         ],
         (0,),
         (
@@ -993,7 +1127,7 @@
             down, down_back, across, mono,
         ),
         1 << 27,
-        outside=(8, 9),
+        outside=(1, 2, 8, 9),
     )
     returned = exchange(slot_grads)
     return call(
@@ -1005,8 +1139,8 @@
             pltpu.VMEM((2 * high * (SUBS + 1), LANES), F32),
             pltpu.VMEM((count * high, LANES), F32),
         ],
-        (3,),
-        (returned, got, jac, camera),
+        (0, 4),
+        (place, returned, got, jac, camera),
         1 << 26,
     )
 

time: 98.1 us -> 92.2 us (0.940)
  Pallas kernels: 46.2 us -> 43.7 us
  other arithmetic: 2.68 us -> 0.64 us
  local copies, waits for them, and re-layouts: 5.56 us -> 4.26 us
    pallas_call x6 -> x7, Pallas kernels: 46.2 us -> 43.7 us  [call(): pl.pallas_call(body, out_shape=out_shape, in_specs=in_specs, out_specs=ou...]
    unnamed x1 -> x0, other arithmetic: 1.36 us -> none
    unnamed x15 -> x16, local copies, waits for them, and re-layouts: 3.07 us -> 2.51 us
where the time goes in v2:
time: 92.2 us; the launch traced here: 91.5 us
  Pallas kernels  43.7 us (47%)
  blocking collectives  18.3 us (20%)
  starting transfers between devices  15.1 us (16%)
  waiting for transfers between devices  9.5 us (10%)
  local copies, waits for them, and re-layouts  4.26 us (5%)
    pallas_call x7, Pallas kernels, call(): pl.pallas_call(body, out_shape=out_shape, in_specs=in_specs, out_specs=ou...  43.7 us
    all_to_all x1, blocking collectives, exchange(): lax.all_to_all(payload, ('img', 'cell'), split_axis=0, concat_axis=0, til...  18.3 us
    all_to_all x2, starting transfers between devices, exchange(): lax.all_to_all(payload, ('img', 'cell'), split_axis=0, concat_axis=0, til...  12.4 us
    all_to_all x2, waiting for transfers between devices, exchange(): lax.all_to_all(payload, ('img', 'cell'), split_axis=0, concat_axis=0, til...  6.68 us
    ppermute x2, waiting for transfers between devices, swap(): lax.ppermute(value_a, axis, swap_pairs(count, 0))  2.81 us
    unnamed x16, local copies, waits for them, and re-layouts  2.51 us
  transfers between devices with their start and end apart: 6, of which 4 were waited for; matrix products, arithmetic and copies ran while one was open for 3% of the time, Pallas kernels for 6%

profile of v2, /device:TPU:0, one launch (start us, length us, event | category | flops | bytes accessed | tf_op | source)
XLA Modules:
  0.0 91.5 jit_solution(12582573547695471397)
XLA Ops:
  0.0 0.0 copy-start.7
  0.0 0.0 copy-start.4
  0.0 1.3 %shard_map.101 = s32[32,128]{1,0:T(8,128)} custom-call(s32[1,2048]{1,0:T(1,128)} %index_ref.1), custom_call_target="tpu_custom_call" | custom-call | flops 16384 | bytes 1048576 | tf_op jit(solution)/shard_map/pallas_call | solution.py:950
  1.3 7.3 %all-to-all-start = ((s32[32,1,128]{2,1,0:T(1,128)}), s32[32,1,128]{2,1,0:T(1,128)S(1)}, u32[]{:S(2)}, u32[]{:S(2)}) async-start(s32[32,1,128]{2,1,0:T(1,128)} %bitcast.15), calls=%async_computation | async-start | bytes 32768 | tf_op jit(solution)/shard_map/all_to_all | solution.py:977
  8.6 0.6 pad_add_fusion.place_ref
  9.3 5.8 %shard_map.100 = (bf16[576,256]{1,0:T(8,128)(2,1)}, f32[3264,128]{1,0:T(8,128)}) custom-call(f32[59,8192]{1,0:T(8,128)} %attr_ref.1, f32[3,3]{1,0:T(4,128)} %cam_ref.3), custom_call_target="tpu_custom_call" | custom-call | flops 16777216 | bytes 1048576 | tf_op jit(solution)/shard_map/pallas_call | solution.py:950
  15.0 0.7 all-to-all-done
  15.7 0.0 copy-start.1
  15.8 0.6 copy-done.1
  16.4 4.1 %shard_map.102 = f32[32,8,128]{2,1,0:T(8,128)} custom-call(s32[4]{0:T(128)} %pad_add_fusion.place_ref, bf16[576,256]{1,0:T(8,128)(2,1)} %get-tuple-element.16.table_ref, s32[32,128]{1,0:T(8,128)} %bitcast.13), custom_call_target="tpu_custom_call" | custom-call | flops 16777216 | bytes 1048576 | tf_op jit(solution)/shard_map/pallas_call | solution.py:950
  20.4 5.1 %all-to-all-start.1 = ((f32[32,8,128]{2,1,0:T(8,128)}), f32[32,8,128]{2,1,0:T(8,128)S(1)}, u32[]{:S(2)}, u32[]{:S(2)}) async-start(f32[32,8,128]{2,1,0:T(8,128)} %shard_map.102), calls=%async_computation.1 | async-start | bytes 262144 | tf_op jit(solution)/shard_map/all_to_all | solution.py:977
  25.5 0.0 copy-done.7
  25.6 0.1 lt.24
  25.7 0.8 select_n.15.bias_ref
  26.4 0.0 copy-done.4
  26.4 0.1 copy.14
  26.6 0.8 reshape.40.entry_ref
  27.3 5.9 %all-to-all-done.1.arrived_in = f32[32,8,128]{2,1,0:T(8,128)S(1)} async-done(((f32[32,8,128]{2,1,0:T(8,128)}), f32[32,8,128]{2,1,0:T(8,128)S(1)}, u32[]{:S(2)}, u32[]{:S(2)}) %all-to-all-start.1) | async-done | bytes 131104 | tf_op jit(solution)/shard_map/all_to_all | solution.py:977
  33.3 0.0 copy-start
  33.3 0.7 copy-done
  33.9 8.5 %shard_map.103 = (f32[3,32,256]{2,1,0:T(8,128)}, f32[16,4096]{1,0:T(8,128)}, f32[4096,256]{1,0:T(8,128)}, bf16[4096,512]{1,0:T(8,128)(2,1)}, f32[24,128]{1,0:T(8,128)}, /*index=5*/f32[24,128]{1,0:T(8,128)}) custom-call(s32[4]{0:T(128)} %pad_add_fusion.place_ref, f32[32,8,128]{2,1,0:T(8,128)} %copy-done, s32[1,4096]{1,0:T(1,128)} %reshape.40.entry_ref, ...), custom_call_target="tpu_custom_call" | custom-call | flops 67108864 | bytes 1048576 | tf_op jit(solution)/shard_map/pallas_call | solution.py:950
  42.4 1.3 %collective-permute-start = (f32[24,128]{1,0:T(8,128)}, f32[24,128]{1,0:T(8,128)S(1)}, u32[]{:S(2)}, u32[]{:S(2)}) collective-permute-start(f32[24,128]{1,0:T(8,128)} %get-tuple-element.17), channel_id=1, source_target_pairs={{0,1},{1,0},{2,3},{3,2},{4,5},{5,4},{6,7},{7,6},{8,9},{9,8},{10,11... | collective-permute-start | bytes 36872 | tf_op jit(solution)/shard_map/ppermute | solution.py:971
  43.7 0.7 collective-permute-start.1
  44.4 2.0 %collective-permute-done.got_a_in = f32[24,128]{1,0:T(8,128)S(1)} collective-permute-done((f32[24,128]{1,0:T(8,128)}, f32[24,128]{1,0:T(8,128)S(1)}, u32[]{:S(2)}, u32[]{:S(2)}) %collective-permute-start) | collective-permute-done | bytes 12320 | tf_op jit(solution)/shard_map/ppermute | solution.py:971
  46.4 0.0 copy-start.5
  46.4 0.0 collective-permute-done.1.got_b_in
  46.4 0.0 copy-start.6
  46.4 0.6 copy-done.5
  47.0 0.0 copy-done.6
  47.0 2.6 %shard_map.104 = (f32[6,32,128]{2,1,0:T(8,128)}, f32[72,256]{1,0:T(8,128)}, f32[72,256]{1,0:T(8,128)}) custom-call(s32[4]{0:T(128)} %pad_add_fusion.place_ref, f32[24,128]{1,0:T(8,128)} %copy-done.5, f32[24,128]{1,0:T(8,128)} %copy-done.6, f32[3,32,256]{2,1,0:T(8,128)} %get-tuple-element.19.image_ref, f32[3,32,256]{2,1,0:T(8,128)} %target_ref.5), custom_call_target="tpu_custom_call" | custom-call | flops 1048576 | bytes 1048576 | tf_op jit(solution)/shard_map/pallas_call | solution.py:950
  49.6 0.1 collective-permute-start.2
  49.7 0.7 collective-permute-start.3
  50.3 0.8 collective-permute-done.2.got_a_in
  51.1 0.0 copy-start.2
  51.1 0.0 collective-permute-done.3.got_b_in
  51.1 0.0 copy-start.3
  51.1 0.6 copy-done.2
  51.8 0.0 copy-done.3
  51.8 14.8 %shard_map.105 = f32[32,8,128]{2,1,0:T(8,128)} custom-call(s32[4]{0:T(128)} %pad_add_fusion.place_ref, f32[72,256]{1,0:T(8,128)} %copy-done.2, f32[72,256]{1,0:T(8,128)} %copy-done.3, f32[3,32,256]{2,1,0:T(8,128)} %get-tuple-element.19.image_ref, f32[3,32,256]{2,1,0:T(8,128)} %target_ref.5, f32[6,32,128]{2,1,0:T(8,128)} %get-tuple-element.22.side_ref, ...), custom_call_target="tpu_custom_call" | custom-call | flops 134217728 | bytes 1048576 | tf_op jit(solution)/shard_map/pallas_call | solution.py:950
  66.6 18.3 %all_to_all.21.returned_ref = f32[32,8,128]{2,1,0:T(8,128)} all-to-all(f32[32,8,128]{2,1,0:T(8,128)} %shard_map.105), channel_id=1, replica_groups=mesh['img'=4,'cell'=8] {'img','cell'}, dimensions={0} | all-to-all | bytes 262144 | tf_op jit(solution)/shard_map/all_to_all | solution.py:977
  84.9 6.6 %shard_map.106 = f32[59,8192]{1,0:T(8,128)} custom-call(s32[4]{0:T(128)} %pad_add_fusion.place_ref, f32[32,8,128]{2,1,0:T(8,128)} %all_to_all.21.returned_ref, s32[32,128]{1,0:T(8,128)} %bitcast.14, f32[3264,128]{1,0:T(8,128)} %get-tuple-element.26.jac_ref, f32[3,3]{1,0:T(4,128)} %cam_ref.3), custom_call_target="tpu_custom_call" | custom-call | flops 67108864 | bytes 1048576 | tf_op jit(solution)/shard_map/pallas_call | solution.py:950
  (1 shorter events, 0.0 us)
Async XLA Ops:
  0.0 25.5 %copy-start.7 = (s32[2,16]{1,0:T(2,128)S(1)}, s32[2,16]{1,0:T(2,128)}, u32[]{:S(2)}) copy-start(s32[2,16]{1,0:T(2,128)} %param.15) | copy-start | bytes 388
  0.0 26.4 %copy-start.4 = (s32[2,16,128]{2,1,0:T(8,128)S(1)}, s32[2,16,128]{2,1,0:T(8,128)}, u32[]{:S(2)}) copy-start(s32[2,16,128]{2,1,0:T(8,128)} %param.14) | copy-start | bytes 49156
  1.3 14.4 %all-to-all-start = ((s32[32,1,128]{2,1,0:T(1,128)}), s32[32,1,128]{2,1,0:T(1,128)S(1)}, u32[]{:S(2)}, u32[]{:S(2)}) async-start(s32[32,1,128]{2,1,0:T(1,128)} %bitcast.15), calls=%async_computation | async-start | bytes 32768 | tf_op jit(solution)/shard_map/all_to_all | solution.py:977
  15.7 0.6 copy-start.1
  20.4 12.8 %all-to-all-start.1 = ((f32[32,8,128]{2,1,0:T(8,128)}), f32[32,8,128]{2,1,0:T(8,128)S(1)}, u32[]{:S(2)}, u32[]{:S(2)}) async-start(f32[32,8,128]{2,1,0:T(8,128)} %shard_map.102), calls=%async_computation.1 | async-start | bytes 262144 | tf_op jit(solution)/shard_map/all_to_all | solution.py:977
  33.3 0.7 copy-start
  42.4 4.0 %collective-permute-start = (f32[24,128]{1,0:T(8,128)}, f32[24,128]{1,0:T(8,128)S(1)}, u32[]{:S(2)}, u32[]{:S(2)}) collective-permute-start(f32[24,128]{1,0:T(8,128)} %get-tuple-element.17), channel_id=1, source_target_pairs={{0,1},{1,0},{2,3},{3,2},{4,5},{5,4},{6,7},{7,6},{8,9},{9,8},{10,11... | collective-permute-start | bytes 36872 | tf_op jit(solution)/shard_map/ppermute | solution.py:971
  43.7 2.7 %collective-permute-start.1 = (f32[24,128]{1,0:T(8,128)}, f32[24,128]{1,0:T(8,128)S(1)}, u32[]{:S(2)}, u32[]{:S(2)}) collective-permute-start(f32[24,128]{1,0:T(8,128)} %get-tuple-element.18), channel_id=1, source_target_pairs={{1,2},{2,1},{3,4},{4,3},{5,6},{6,5},{9,10},{10,9},{11,12},{12,11},... | collective-permute-start | bytes 36872 | tf_op jit(solution)/shard_map/ppermute | solution.py:972
  46.4 0.6 copy-start.5
  46.4 0.6 copy-start.6
  49.6 1.5 %collective-permute-start.2 = (f32[72,256]{1,0:T(8,128)}, f32[72,256]{1,0:T(8,128)S(1)}, u32[]{:S(2)}, u32[]{:S(2)}) collective-permute-start(f32[72,256]{1,0:T(8,128)} %get-tuple-element.20), channel_id=1, source_target_pairs={{0,8},{8,0},{16,24},{24,16},{1,9},{9,1},{17,25},{25,17},{2,10},{10... | collective-permute-start | bytes 221192 | tf_op jit(solution)/shard_map/ppermute | solution.py:971
  49.7 1.5 %collective-permute-start.3 = (f32[72,256]{1,0:T(8,128)}, f32[72,256]{1,0:T(8,128)S(1)}, u32[]{:S(2)}, u32[]{:S(2)}) collective-permute-start(f32[72,256]{1,0:T(8,128)} %get-tuple-element.21), channel_id=1, source_target_pairs={{8,16},{16,8},{9,17},{17,9},{10,18},{18,10},{11,19},{19,11},{12,20... | collective-permute-start | bytes 221192 | tf_op jit(solution)/shard_map/ppermute | solution.py:972
  51.1 0.6 copy-start.2
  51.1 0.7 copy-start.3

commit v3 on v2

--- a/solution.py
+++ b/solution.py
@@ -42,7 +42,7 @@
 F32 = jnp.float32
 BF16 = jnp.bfloat16
 JAC_ROWS = 51
-VMEM_BYTES = 56 * 1024 * 1024
+MIB = 1024 * 1024
 
 
 def harmonic_basis(unit_x, unit_y, unit_z):
@@ -811,7 +811,12 @@
         out_ref[place] = jnp.where(lane_low, eight, jnp.broadcast_to(ninth, (SUBS, LANES)))
 
 
-def return_kernel(place_ref, returned_ref, got_ref, jac_ref, cam_ref, grad_ref, row_ref, mask_ref, sum_ref, pack_ref):
+def return_kernel(
+    place_ref, returned_ref, got_ref, jac_in, cam_ref, grad_out,
+    row_ref, mask_ref, sum_ref, pack_ref, jac_ref, grad_ref, sems, jac_sems,
+):
+    jac_copy = pltpu.make_async_copy(jac_in, jac_ref, jac_sems.at[0])
+    jac_copy.start()
     devices = got_ref.shape[0]
     count, own = grad_ref.shape
     high = own // LANES
@@ -853,6 +858,11 @@
         return carry
 
     lax.fori_loop(0, devices * half // chunk, collect, 0)
+    jac_copy.wait()
+
+    def grad_copy(index):
+        at = pl.ds(pl.multiple_of(index * SUBS * LANES, SUBS * LANES), SUBS * LANES)
+        return pltpu.make_async_copy(grad_ref.at[:, at], grad_out.at[:, at], sems.at[index])
 
     def block(index, carry):
         start = pl.multiple_of(index * SUBS, SUBS)
@@ -902,16 +912,20 @@
             for term in range(1, 16):
                 out.append(slopes[6 + channel] * jac(32 + term))
         for number, value in enumerate(out):
-            pack_ref[pl.ds(number * high + start, SUBS), :] = value
+            pack_ref[number * SUBS : (number + 1) * SUBS, :] = value
+        for first in range(0, count, SUBS):
+            number = min(SUBS, count - first)
+            for place in range(SUBS):
+                at = pl.ds(pl.multiple_of((start + place) * LANES, LANES), LANES)
+                grad_ref[first : first + number, at] = pack_ref[
+                    pl.ds(first * SUBS + place, number, stride=SUBS), :
+                ]
+        grad_copy(index).start()
         return carry
 
     lax.fori_loop(0, high // SUBS, block, 0)
-    for first in range(0, count, SUBS):
-        number = min(SUBS, count - first)
-        for place in range(high):
-            grad_ref[first : first + number, place * LANES : (place + 1) * LANES] = pack_ref[
-                pl.ds(first * high + place, number, stride=high), :
-            ]
+    for index in range(high // SUBS):
+        grad_copy(index).wait()
 
 
 def band(outs, ins):
@@ -929,7 +943,7 @@
     return np.concatenate([eight, eight, eight, eight * 0]).astype(np.float32)
 
 
-def call(body, out_shape, scratch, scalar_at, args, flops, outside=(), outs_outside=()):
+def call(body, out_shape, scratch, scalar_at, args, flops, vmem, outside=(), outs_outside=()):
     in_specs = [
         pl.BlockSpec(
             memory_space=pltpu.SMEM
@@ -946,14 +960,14 @@
             for number in range(len(out_shape))
         )
     else:
-        out_specs = pl.BlockSpec(memory_space=pltpu.VMEM)
+        out_specs = pl.BlockSpec(memory_space=pl.ANY if outs_outside else pltpu.VMEM)
     return pl.pallas_call(
         body,
         out_shape=out_shape,
         in_specs=in_specs,
         out_specs=out_specs,
         scratch_shapes=scratch,
-        compiler_params=pltpu.CompilerParams(vmem_limit_bytes=VMEM_BYTES),
+        compiler_params=pltpu.CompilerParams(vmem_limit_bytes=vmem * MIB),
         cost_estimate=pl.CostEstimate(flops=flops, bytes_accessed=1 << 20, transcendentals=0),
     )(*args)
 
@@ -1007,6 +1021,7 @@
         (),
         (visible_index,),
         1 << 14,
+        2,
     )
     got = exchange(asked)
 
@@ -1020,6 +1035,7 @@
         (1,),
         (attributes, camera),
         1 << 24,
+        12,
     )
     reply = call(
         reply_kernel,
@@ -1033,6 +1049,7 @@
         (0,),
         (place, table, got),
         1 << 24,
+        2 + slots // 128,
         outside=(2,),
     )
     arrived = exchange(reply)
@@ -1072,6 +1089,7 @@
         (0,),
         (place, arrived, entry, bias, target, mono),
         1 << 26,
+        16 + devices // 8,
         outside=(1,),
         outs_outside=(2, 3),
     )
@@ -1088,6 +1106,7 @@
         (0,),
         (place, got_a, got_b, image, target),
         1 << 20,
+        4,
         outside=(1, 2),
     )
     got_a, got_b = swap(send_a, send_b, "img")
@@ -1127,6 +1146,7 @@
             down, down_back, across, mono,
         ),
         1 << 27,
+        32 + devices // 8,
         outside=(1, 2, 8, 9),
     )
     returned = exchange(slot_grads)
@@ -1137,11 +1157,18 @@
             pltpu.VMEM((1, slots), jnp.int32),
             pltpu.VMEM((2 * high * (SUBS + 1), 4 * LANES), BF16),
             pltpu.VMEM((2 * high * (SUBS + 1), LANES), F32),
-            pltpu.VMEM((count * high, LANES), F32),
+            pltpu.VMEM((count * SUBS, LANES), F32),
+            pltpu.VMEM((JAC_ROWS * high, LANES), F32),
+            pltpu.VMEM((count, own), F32),
+            pltpu.SemaphoreType.DMA((high // SUBS,)),
+            pltpu.SemaphoreType.DMA((1,)),
         ],
         (0, 4),
         (place, returned, got, jac, camera),
         1 << 26,
+        12,
+        outside=(3,),
+        outs_outside=(0,),
     )
 
 

time: 92.2 us -> 81 us (0.88)
  Pallas kernels: 43.7 us -> 33.3 us
  waiting for transfers between devices: 9.5 us -> 10.5 us
    pallas_call x7, Pallas kernels: 43.7 us -> 33.3 us  [call(): pl.pallas_call(body, out_shape=out_shape, in_specs=in_specs, out_specs=ou...]
    all_to_all x2, waiting for transfers between devices: 6.68 us -> 8.29 us  [exchange(): lax.all_to_all(payload, ('img', 'cell'), split_axis=0, concat_axis=0, til...]
    unnamed x16 -> x22, local copies, waits for them, and re-layouts: 2.51 us -> 3.02 us
  transfers between devices with their start and end apart: 6 -> 6, of which waited for: 4 -> 4; matrix products, arithmetic and copies ran while one was open for 3% -> 1% of each run, Pallas kernels for 6% -> 4%
where the time goes in v3:
time: 81 us; the launch traced here: 80.7 us
  Pallas kernels  33.3 us (41%)
  blocking collectives  18 us (22%)
  starting transfers between devices  14.9 us (18%)
  waiting for transfers between devices  10.5 us (13%)
  local copies, waits for them, and re-layouts  3.56 us (4%)
    pallas_call x7, Pallas kernels, call(): pl.pallas_call(body, out_shape=out_shape, in_specs=in_specs, out_specs=ou...  33.3 us
    all_to_all x1, blocking collectives, exchange(): lax.all_to_all(payload, ('img', 'cell'), split_axis=0, concat_axis=0, til...  18 us
    all_to_all x2, starting transfers between devices, exchange(): lax.all_to_all(payload, ('img', 'cell'), split_axis=0, concat_axis=0, til...  12 us
    all_to_all x2, waiting for transfers between devices, exchange(): lax.all_to_all(payload, ('img', 'cell'), split_axis=0, concat_axis=0, til...  8.29 us
    unnamed x22, local copies, waits for them, and re-layouts  3.02 us
    ppermute x2, waiting for transfers between devices, swap(): lax.ppermute(value_a, axis, swap_pairs(count, 0))  2.21 us
  transfers between devices with their start and end apart: 6, of which 4 were waited for; matrix products, arithmetic and copies ran while one was open for 1% of the time, Pallas kernels for 4%

profile of v3, /device:TPU:0, one launch (start us, length us, event | category | flops | bytes accessed | tf_op | source)
XLA Modules:
  0.0 80.7 jit_solution(10292093547472472292)
XLA Ops:
  0.0 0.0 copy-start.3
  0.0 0.0 copy-start.8
  0.0 0.7 copy-done.8
  0.7 0.0 copy-start.10
  0.7 0.0 copy-start.9
  0.7 0.6 shard_map.101
  1.3 7.3 %all-to-all-start = ((s32[32,1,128]{2,1,0:T(1,128)}), s32[32,1,128]{2,1,0:T(1,128)S(1)}, u32[]{:S(2)}, u32[]{:S(2)}) async-start(s32[32,1,128]{2,1,0:T(1,128)} %bitcast.3), calls=%async_computation | async-start | bytes 32768 | tf_op jit(solution)/shard_map/all_to_all | solution.py:991
  8.6 0.1 pad_add_fusion.place_ref
  8.7 0.0 copy-start
  8.7 1.6 %copy-done = f32[59,8192]{1,0:T(8,128)S(1)} copy-done((f32[59,8192]{1,0:T(8,128)S(1)}, f32[59,8192]{1,0:T(8,128)}, u32[]{:S(2)}) %copy-start) | copy-done | bytes 1933336
  10.3 0.0 copy-start.6
  10.3 0.7 copy-done.6
  11.0 0.0 copy-start.1
  11.0 0.0 copy-start.2
  11.0 0.0 copy-start.4
  11.0 0.0 copy-start.5
  11.0 3.5 %shard_map.100 = (bf16[576,256]{1,0:T(8,128)(2,1)S(1)}, f32[3264,128]{1,0:T(8,128)S(1)}) custom-call(f32[59,8192]{1,0:T(8,128)S(1)} %copy-done, f32[3,3]{1,0:T(4,128)S(1)} %copy-done.6), custom_call_target="tpu_custom_call" | custom-call | flops 16777216 | bytes 1048576 | tf_op jit(solution)/shard_map/pallas_call | solution.py:964
  14.5 1.2 %all-to-all-done = s32[32,1,128]{2,1,0:T(1,128)S(1)} async-done(((s32[32,1,128]{2,1,0:T(1,128)}), s32[32,1,128]{2,1,0:T(1,128)S(1)}, u32[]{:S(2)}, u32[]{:S(2)}) %all-to-all-start) | async-done | bytes 16416 | tf_op jit(solution)/shard_map/all_to_all | solution.py:991
  15.7 2.9 %shard_map.102 = f32[32,8,128]{2,1,0:T(8,128)} custom-call(s32[4]{0:T(128)S(1)} %pad_add_fusion.place_ref, bf16[576,256]{1,0:T(8,128)(2,1)S(1)} %get-tuple-element.16.table_ref, s32[32,128]{1,0:T(8,128)S(1)} %bitcast.12), custom_call_target="tpu_custom_call" | custom-call | flops 16777216 | bytes 1048576 | tf_op jit(solution)/shard_map/pallas_call | solution.py:964
  18.6 4.7 %all-to-all-start.1 = ((f32[32,8,128]{2,1,0:T(8,128)}), f32[32,8,128]{2,1,0:T(8,128)S(1)}, u32[]{:S(2)}, u32[]{:S(2)}) async-start(f32[32,8,128]{2,1,0:T(8,128)} %shard_map.102), calls=%async_computation.1 | async-start | bytes 262144 | tf_op jit(solution)/shard_map/all_to_all | solution.py:991
  23.3 0.0 copy-done.10
  23.3 0.1 lt.24
  23.4 0.2 select_n.15.bias_ref
  23.6 0.0 copy-done.9
  23.6 0.1 copy.14
  23.8 0.2 reshape.40.entry_ref
  23.9 7.1 %all-to-all-done.1.arrived_in = f32[32,8,128]{2,1,0:T(8,128)S(1)} async-done(((f32[32,8,128]{2,1,0:T(8,128)}), f32[32,8,128]{2,1,0:T(8,128)S(1)}, u32[]{:S(2)}, u32[]{:S(2)}) %all-to-all-start.1) | async-done | bytes 131104 | tf_op jit(solution)/shard_map/all_to_all | solution.py:991
  31.1 0.0 copy-done.3
  31.1 0.0 copy-done.1
  31.1 7.7 %shard_map.103 = (f32[3,32,256]{2,1,0:T(8,128)S(1)}, f32[16,4096]{1,0:T(8,128)S(1)}, f32[4096,256]{1,0:T(8,128)S(1)}, bf16[4096,512]{1,0:T(8,128)(2,1)S(1)}, f32...) custom-call(s32[4]{0:T(128)S(1)} %pad_add_fusion.place_ref, f32[32,8,128]{2,1,0:T(8,128)S(1)} %all-to-all-done.1.arrived_in, ...), custom_call_target="tpu_custom_call" | custom-call | flops 67108864 | bytes 1048576 | tf_op jit(solution)/shard_map/pallas_call | solution.py:964
  38.8 1.3 %collective-permute-start = (f32[24,128]{1,0:T(8,128)S(1)}, f32[24,128]{1,0:T(8,128)S(1)}, u32[]{:S(2)}, u32[]{:S(2)}) collective-permute-start(f32[24,128]{1,0:T(8,128)S(1)} %get-tuple-element.17), channel_id=1, source_target_pairs={{0,1},{1,0},{2,3},{3,2},{4,5},{5,4},{6,7},{7,6},{8,9},{9,8},{10,11... | collective-permute-start | bytes 36872 | tf_op jit(solution)/shard_map/ppermute | solution.py:985
  40.1 0.7 collective-permute-start.1
  40.7 1.8 %collective-permute-done.got_a_in = f32[24,128]{1,0:T(8,128)S(1)} collective-permute-done((f32[24,128]{1,0:T(8,128)S(1)}, f32[24,128]{1,0:T(8,128)S(1)}, u32[]{:S(2)}, u32[]{:S(2)}) %collective-permute-start) | collective-permute-done | bytes 12320 | tf_op jit(solution)/shard_map/ppermute | solution.py:985
  42.5 0.0 collective-permute-done.1.got_b_in
  42.5 0.8 shard_map.104
  43.3 0.1 collective-permute-start.2
  43.4 0.8 %collective-permute-start.3 = (f32[72,256]{1,0:T(8,128)S(1)}, f32[72,256]{1,0:T(8,128)S(1)}, u32[]{:S(2)}, u32[]{:S(2)}) collective-permute-start(f32[72,256]{1,0:T(8,128)S(1)} %get-tuple-element.21), channel_id=1, source_target_pairs={{8,16},{16,8},{9,17},{17,9},{10,18},{18,10},{11,19},{19,11},{12,20... | collective-permute-start | bytes 221192 | tf_op jit(solution)/shard_map/ppermute | solution.py:986
  44.3 0.4 collective-permute-done.2.got_a_in
  44.7 0.0 collective-permute-done.3.got_b_in
  44.7 0.0 copy-done.2
  44.7 0.0 copy-done.4
  44.7 0.0 copy-done.5
  44.7 0.0 copy-start.7
  44.7 13.3 %shard_map.105 = f32[32,8,128]{2,1,0:T(8,128)S(1)} custom-call(s32[4]{0:T(128)S(1)} %pad_add_fusion.place_ref, f32[72,256]{1,0:T(8,128)S(1)} %collective-permute-done.2.got_a_in, f32[72,256]{1,0:T(8,128)S(1)} %collective-permute-done.3.got_b_in, f32[3,32,256]{2,1,0:T(8,128)S(1)} %get-tuple-element.19.image_ref, f32[3,32,256]{2,1,0:T(8,128)S(1)} %copy-done.1, ...), custom_call_target="tpu_custom_call" | custom-call | flops 134217728 | bytes 1048576 | tf_op jit(solution)/shard_map/pallas_call | solution.py:964
  58.0 18.0 %all_to_all.21.returned_ref = f32[32,8,128]{2,1,0:T(8,128)S(1)} all-to-all(f32[32,8,128]{2,1,0:T(8,128)S(1)} %shard_map.105), channel_id=1, replica_groups=mesh['img'=4,'cell'=8] {'img','cell'}, dimensions={0} | all-to-all | bytes 262144 | tf_op jit(solution)/shard_map/all_to_all | solution.py:991
  76.0 0.0 copy-done.7
  76.0 4.5 %shard_map.106 = f32[59,8192]{1,0:T(8,128)} custom-call(s32[4]{0:T(128)S(1)} %pad_add_fusion.place_ref, f32[32,8,128]{2,1,0:T(8,128)S(1)} %all_to_all.21.returned_ref, s32[32,128]{1,0:T(8,128)S(1)} %bitcast.13, f32[3264,128]{1,0:T(8,128)S(1)} %get-tuple-element.26.jac_in, f32[3,3]{1,0:T(4,128)S(1)} %copy-done.7), custom_call_target="tpu_custom_call" | custom-call | flops 67108864 | bytes 1048576 | tf_op jit(solution)/shard_map/pallas_call | solution.py:964
  (1 shorter events, 0.0 us)
Async XLA Ops:
  0.0 31.1 %copy-start.3 = (bf16[32,256]{1,0:T(8,128)(2,1)S(1)}, bf16[32,256]{1,0:T(8,128)(2,1)}, u32[]{:S(2)}) copy-start(bf16[32,256]{1,0:T(8,128)(2,1)} %constant.31.mono_ref) | copy-start | bytes 49156
  0.0 0.7 copy-start.8
  0.7 22.6 %copy-start.10 = (s32[2,16]{1,0:T(2,128)S(1)}, s32[2,16]{1,0:T(2,128)}, u32[]{:S(2)}) copy-start(s32[2,16]{1,0:T(2,128)} %param.15) | copy-start | bytes 388
  0.7 22.9 %copy-start.9 = (s32[2,16,128]{2,1,0:T(8,128)S(1)}, s32[2,16,128]{2,1,0:T(8,128)}, u32[]{:S(2)}) copy-start(s32[2,16,128]{2,1,0:T(8,128)} %param.14) | copy-start | bytes 49156
  1.3 14.3 %all-to-all-start = ((s32[32,1,128]{2,1,0:T(1,128)}), s32[32,1,128]{2,1,0:T(1,128)S(1)}, u32[]{:S(2)}, u32[]{:S(2)}) async-start(s32[32,1,128]{2,1,0:T(1,128)} %bitcast.3), calls=%async_computation | async-start | bytes 32768 | tf_op jit(solution)/shard_map/all_to_all | solution.py:991
  8.7 1.6 %copy-start = (f32[59,8192]{1,0:T(8,128)S(1)}, f32[59,8192]{1,0:T(8,128)}, u32[]{:S(2)}) copy-start(f32[59,8192]{1,0:T(8,128)} %attr_ref.1) | copy-start | bytes 5799940
  10.3 0.7 copy-start.6
  11.0 20.1 %copy-start.1 = (f32[3,32,256]{2,1,0:T(8,128)S(1)}, f32[3,32,256]{2,1,0:T(8,128)}, u32[]{:S(2)}) copy-start(f32[3,32,256]{2,1,0:T(8,128)} %target_ref.5) | copy-start | bytes 294916
  11.0 33.7 %copy-start.2 = (f32[384,384]{1,0:T(8,128)S(1)}, f32[384,384]{1,0:T(8,128)}, u32[]{:S(2)}) copy-start(f32[384,384]{1,0:T(8,128)} %constant.27.clone.across_ref) | copy-start | bytes 1769476
  11.0 33.7 %copy-start.4 = (f32[48,64]{1,0:T(8,128)S(1)}, f32[48,64]{1,0:T(8,128)}, u32[]{:S(2)}) copy-start(f32[48,64]{1,0:T(8,128)} %constant.25.clone.down_ref) | copy-start | bytes 36868
  11.0 33.7 %copy-start.5 = (f32[32,48]{1,0:T(8,128)S(1)}, f32[32,48]{1,0:T(8,128)}, u32[]{:S(2)}) copy-start(f32[32,48]{1,0:T(8,128)} %constant.26.clone.down_back_ref) | copy-start | bytes 18436
  18.6 12.4 %all-to-all-start.1 = ((f32[32,8,128]{2,1,0:T(8,128)}), f32[32,8,128]{2,1,0:T(8,128)S(1)}, u32[]{:S(2)}, u32[]{:S(2)}) async-start(f32[32,8,128]{2,1,0:T(8,128)} %shard_map.102), calls=%async_computation.1 | async-start | bytes 262144 | tf_op jit(solution)/shard_map/all_to_all | solution.py:991
  38.8 3.8 %collective-permute-start = (f32[24,128]{1,0:T(8,128)S(1)}, f32[24,128]{1,0:T(8,128)S(1)}, u32[]{:S(2)}, u32[]{:S(2)}) collective-permute-start(f32[24,128]{1,0:T(8,128)S(1)} %get-tuple-element.17), channel_id=1, source_target_pairs={{0,1},{1,0},{2,3},{3,2},{4,5},{5,4},{6,7},{7,6},{8,9},{9,8},{10,11... | collective-permute-start | bytes 36872 | tf_op jit(solution)/shard_map/ppermute | solution.py:985
  40.1 2.5 %collective-permute-start.1 = (f32[24,128]{1,0:T(8,128)S(1)}, f32[24,128]{1,0:T(8,128)S(1)}, u32[]{:S(2)}, u32[]{:S(2)}) collective-permute-start(f32[24,128]{1,0:T(8,128)S(1)} %get-tuple-element.18), channel_id=1, source_target_pairs={{1,2},{2,1},{3,4},{4,3},{5,6},{6,5},{9,10},{10,9},{11,12},{12,11},... | collective-permute-start | bytes 36872 | tf_op jit(solution)/shard_map/ppermute | solution.py:986
  43.3 1.3 %collective-permute-start.2 = (f32[72,256]{1,0:T(8,128)S(1)}, f32[72,256]{1,0:T(8,128)S(1)}, u32[]{:S(2)}, u32[]{:S(2)}) collective-permute-start(f32[72,256]{1,0:T(8,128)S(1)} %get-tuple-element.20), channel_id=1, source_target_pairs={{0,8},{8,0},{16,24},{24,16},{1,9},{9,1},{17,25},{25,17},{2,10},{10... | collective-permute-start | bytes 221192 | tf_op jit(solution)/shard_map/ppermute | solution.py:985
  43.4 1.3 %collective-permute-start.3 = (f32[72,256]{1,0:T(8,128)S(1)}, f32[72,256]{1,0:T(8,128)S(1)}, u32[]{:S(2)}, u32[]{:S(2)}) collective-permute-start(f32[72,256]{1,0:T(8,128)S(1)} %get-tuple-element.21), channel_id=1, source_target_pairs={{8,16},{16,8},{9,17},{17,9},{10,18},{18,10},{11,19},{19,11},{12,20... | collective-permute-start | bytes 221192 | tf_op jit(solution)/shard_map/ppermute | solution.py:986
  44.7 31.3 %copy-start.7 = (f32[3,3]{1,0:T(4,128)S(1)}, f32[3,3]{1,0:T(4,128)}, u32[]{:S(2)}) copy-start(f32[3,3]{1,0:T(4,128)} %cam_ref.3) | copy-start | bytes 112

commit v4 on v3

--- a/solution.py
+++ b/solution.py
@@ -1,8 +1,6 @@
-import functools
-import math
-
 import jax
 import jax.numpy as jnp
+import ml_dtypes
 import numpy as np
 from jax import lax
 from jax.experimental import pallas as pl
@@ -312,8 +310,8 @@
 
 def render_kernel(
     place_ref, arrived_in, entry_ref, bias_ref, target_ref, mono_ref,
-    image_ref, feat_ref, alpha_out, weight_out, send_a_ref, send_b_ref,
-    wide_ref, coef_ref, alpha_ref, weight_ref, arrived_ref, alpha_sems, weight_sems, sems,
+    image_ref, feat_ref, alpha_ref, weight_ref, send_a_ref, send_b_ref,
+    wide_ref, coef_ref, arrived_ref, sems,
 ):
     arrived_copy = pltpu.make_async_copy(arrived_in, arrived_ref, sems.at[0])
     arrived_copy.start()
@@ -346,10 +344,6 @@
     left = jnp.concatenate([left, left_rest], axis=1)
     feat_ref[...] = jnp.zeros(feat_ref.shape, F32)
     coef_ref[...] = jnp.zeros(coef_ref.shape, F32)
-
-    def alpha_copy(index):
-        at = pl.ds(pl.multiple_of(index * chunk, chunk), chunk)
-        return pltpu.make_async_copy(alpha_ref.at[at], alpha_out.at[at], alpha_sems.at[index])
 
     def look(index, slot_number):
         start = pl.multiple_of(index * chunk, chunk)
@@ -391,7 +385,6 @@
             coef_ref[slot_number, number * SUBS : (number + 1) * SUBS] = piece.astype(F32)
         columns = jnp.transpose(coef_ref[slot_number]).astype(BF16)
         alpha_ref[pl.ds(start, chunk), :] = jnp.exp2(dot(columns, mono_ref[...]))
-        alpha_copy(index).start()
 
     def gather_two(index, carry):
         owners = [look(2 * index + number, number) for number in range(2)]
@@ -403,14 +396,6 @@
 
     pixels = TILE * TILE
     step_rows = length * GROUP
-    parts = 4
-    part_rows = step_rows // parts
-
-    def weight_copy(group, part):
-        at = pl.ds(group * step_rows + part * part_rows, part_rows)
-        return pltpu.make_async_copy(
-            weight_ref.at[at], weight_out.at[at], weight_sems.at[group * parts + part]
-        )
 
     def scan(number, keeps):
         new_keeps = []
@@ -429,11 +414,7 @@
         return tuple(new_keeps)
 
     keeps = tuple(jnp.ones((GROUP, pixels), F32) for _ in range(groups))
-    steps = length // (2 * parts)
-    for part in range(parts):
-        keeps = lax.fori_loop(part * steps, (part + 1) * steps, scan, keeps, unroll=4)
-        for group in range(groups):
-            weight_copy(group, part).start()
+    lax.fori_loop(0, length // 2, scan, keeps, unroll=4)
     for group in range(groups):
         here = slice(group * step_rows, (group + 1) * step_rows)
         left = jnp.concatenate(
@@ -471,11 +452,6 @@
             at_right = jnp.where(lane_block == place, final, at_right)
         send_a_ref[vector * SUBS : (vector + 1) * SUBS, :] = jnp.where(even, at_right, at_left)
         send_b_ref[vector * SUBS : (vector + 1) * SUBS, :] = jnp.where(even, at_left, at_right)
-    for index in range(entries // chunk):
-        alpha_copy(index).wait()
-    for group in range(groups):
-        for part in range(parts):
-            weight_copy(group, part).wait()
 
 
 def lane_shift(block, shift, axis=1):
@@ -560,9 +536,9 @@
 
 def back_kernel(
     place_ref, got_a_in, got_b_in, image_ref, target_ref, side_ref, entry_ref, feat_ref,
-    alpha_in, weight_in, down_ref, down_back_ref, across_ref, mono_ref,
+    alpha_ref, weight_ref, down_ref, down_back_ref, across_ref, across_back_ref, mono_ref,
     out_ref,
-    raw_ref, vert_ref, blur_ref, coef_ref, grad_ref, alpha_ref, weight_ref, ahead_ref, pair_ref,
+    raw_ref, vert_ref, blur_ref, coef_ref, grad_ref, ahead_ref, pair_ref,
     right_ref, slope_ref, mask_ref, sum_ref, got_a_ref, got_b_ref, sems,
 ):
     rows = image_ref.shape[1]
@@ -577,16 +553,12 @@
     peers = out_ref.shape[0]
     half = LANES // 2
 
-    alpha_copy = pltpu.make_async_copy(alpha_in, alpha_ref, sems.at[0])
-    weight_copy = pltpu.make_async_copy(weight_in, weight_ref, sems.at[1])
     got_copies = [
-        pltpu.make_async_copy(got_a_in, got_a_ref, sems.at[2]),
-        pltpu.make_async_copy(got_b_in, got_b_ref, sems.at[3]),
+        pltpu.make_async_copy(got_a_in, got_a_ref, sems.at[0]),
+        pltpu.make_async_copy(got_b_in, got_b_ref, sems.at[1]),
     ]
     for copy in got_copies:
         copy.start()
-    alpha_copy.start()
-    weight_copy.start()
     for copy in got_copies:
         copy.wait()
     even_row = place_ref[0] % 2 == 0
@@ -665,10 +637,14 @@
         for number, part in enumerate([on_mean, on_square, on_cross]):
             part = jnp.where(inside, -WEIGHT_SSIM * part, 0.0)
             spot_at = (channel * 3 + number) * rows
-            coef_ref[spot_at : spot_at + rows, :] = dot_full(down_back, part)
+            high, rest = two_pieces(part)
+            coef_ref[spot_at : spot_at + rows, :] = dot(
+                down_back, jnp.concatenate([high, rest, high], axis=0)
+            )
     for channel in range(3):
         at = channel * 3 * rows
-        back = dot_full(coef_ref[at : at + 3 * rows, :], across_ref[:, 0:cols])
+        high, rest = two_pieces(coef_ref[at : at + 3 * rows, :])
+        back = dot(jnp.concatenate([high, rest, high], axis=1), across_back_ref[...])
         shown = image_ref[channel]
         wanted = target_ref[channel]
         gap = shown - wanted
@@ -715,9 +691,6 @@
         ahead_ref[start : start + step_rows, :] = dot(
             left, jnp.concatenate([high, high, rest], axis=0).astype(BF16)
         )
-
-    alpha_copy.wait()
-    weight_copy.wait()
 
     def step(number, behinds):
         new_behinds = []
@@ -776,7 +749,7 @@
     sum_ref[...] = jnp.zeros(sum_ref.shape, F32)
     pair_step = iota((2 * SUBS, chunk), 0) // SUBS
 
-    def collect(index, carry):
+    def collect(index, part):
         start = pl.multiple_of(index * chunk, chunk)
         slot = entry_ref[:, pl.ds(start, chunk)]
         within = slot & (half - 1)
@@ -791,17 +764,20 @@
             hit = offset == 2 * place
             for number in range(2):
                 at = number * (tops + peers) + place * 2 * SUBS
-                mask_ref[at : at + 2 * SUBS, :] = jnp.where(hit, values[number], 0.0).astype(BF16)
+                mask_ref[part, at : at + 2 * SUBS, :] = jnp.where(hit, values[number], 0.0).astype(BF16)
         hit = iota((peers, chunk), 0) == owner
         for number, piece in enumerate(
             two_pieces(slope_ref[SUBS : SUBS + 1, pl.ds(start, chunk)])
         ):
             at = number * (tops + peers) + tops
-            mask_ref[at : at + peers, :] = jnp.where(hit, piece.astype(F32), 0.0).astype(BF16)
-        sum_ref[...] += dot_nt(mask_ref[...], hot)
+            mask_ref[part, at : at + peers, :] = jnp.where(hit, piece.astype(F32), 0.0).astype(BF16)
+        return dot_nt(mask_ref[part], hot)
+
+    def collect_two(index, carry):
+        sum_ref[...] += collect(2 * index, 0) + collect(2 * index + 1, 1)
         return carry
 
-    lax.fori_loop(0, entries // chunk, collect, 0)
+    lax.fori_loop(0, entries // (2 * chunk), collect_two, 0)
     lane_low = iota((SUBS, LANES), 1) < half
     for place in range(peers):
         at = place * SUBS
@@ -830,16 +806,16 @@
     lane_low = iota((SUBS, LANES), 1) < half
     pair_step = iota((2 * SUBS, chunk), 0) // SUBS
 
-    def collect(index, carry):
+    def collect(index, part):
         numbers = row_ref[:, pl.ds(pl.multiple_of(index * chunk, chunk), chunk)]
         low = numbers & (LANES - 1)
         top = numbers >> 7
         hot = jnp.where(iota((LANES, chunk), 0) == low, 1.0, 0.0).astype(BF16)
         eights = []
         ninths = []
-        for part in range(chunk // LANES):
-            first = returned_ref[index * 8 + 2 * part]
-            second = returned_ref[index * 8 + 2 * part + 1]
+        for pair in range(chunk // LANES):
+            first = returned_ref[index * 8 + 2 * pair]
+            second = returned_ref[index * 8 + 2 * pair + 1]
             eights.append(jnp.where(lane_low, first, pltpu.roll(second, half, 1)))
             ninths.append(jnp.where(lane_low, pltpu.roll(first, half, 1), second)[0:1])
         values = [piece.astype(F32) for piece in two_pieces(jnp.concatenate(eights, axis=1))]
@@ -849,15 +825,18 @@
             hit = offset == 2 * place
             for number in range(2):
                 at = number * part_rows + place * 2 * SUBS
-                mask_ref[at : at + 2 * SUBS, :] = jnp.where(hit, values[number], 0.0).astype(BF16)
+                mask_ref[part, at : at + 2 * SUBS, :] = jnp.where(hit, values[number], 0.0).astype(BF16)
         hit = iota((high, chunk), 0) == top
         for number, piece in enumerate(two_pieces(jnp.concatenate(ninths, axis=1))):
             at = number * part_rows + tops
-            mask_ref[at : at + high, :] = jnp.where(hit, piece.astype(F32), 0.0).astype(BF16)
-        sum_ref[...] += dot_nt(mask_ref[...], hot)
+            mask_ref[part, at : at + high, :] = jnp.where(hit, piece.astype(F32), 0.0).astype(BF16)
+        return dot_nt(mask_ref[part], hot)
+
+    def collect_two(index, carry):
+        sum_ref[...] += collect(2 * index, 0) + collect(2 * index + 1, 1)
         return carry
 
-    lax.fori_loop(0, devices * half // chunk, collect, 0)
+    lax.fori_loop(0, devices * half // (2 * chunk), collect_two, 0)
     jac_copy.wait()
 
     def grad_copy(index):
@@ -935,6 +914,12 @@
     return np.where(np.abs(offset) <= RIM, values, 0.0).astype(np.float32)
 
 
+def band_pieces(values):
+    high = values.astype(ml_dtypes.bfloat16)
+    rest = (values - high.astype(np.float32)).astype(ml_dtypes.bfloat16)
+    return [high, high, rest]
+
+
 def monomials():
     pixel = np.arange(TILE * TILE)
     x = (pixel % TILE) - 7.5
@@ -981,10 +966,9 @@
 
 def swap(value_a, value_b, axis):
     count = lax.axis_size(axis)
-    return (
-        lax.ppermute(value_a, axis, swap_pairs(count, 0)),
-        lax.ppermute(value_b, axis, swap_pairs(count, 1)),
-    )
+    got_b = lax.ppermute(value_b, axis, swap_pairs(count, 1))
+    got_a = lax.ppermute(value_a, axis, swap_pairs(count, 0))
+    return got_a, got_b
 
 
 def exchange(payload):
@@ -1079,11 +1063,7 @@
         [
             pltpu.VMEM((2, devices * (SUBS + 1), 512), F32),
             pltpu.VMEM((2, 32, 512), F32),
-            pltpu.VMEM((entries, pixels), F32),
-            pltpu.VMEM((entries, 2 * pixels), BF16),
             pltpu.VMEM((devices, SUBS, LANES), F32),
-            pltpu.SemaphoreType.DMA((entries // 512,)),
-            pltpu.SemaphoreType.DMA((4 * groups,)),
             pltpu.SemaphoreType.DMA((1,)),
         ],
         (0,),
@@ -1091,7 +1071,6 @@
         1 << 26,
         16 + devices // 8,
         outside=(1,),
-        outs_outside=(2, 3),
     )
     got_a, got_b = swap(send_a, send_b, "cell")
     edge = jax.ShapeDtypeStruct(((SUBS + 1) * SUBS, cols), F32)
@@ -1117,8 +1096,9 @@
     wide_at = np.arange(wide)
     wide_at = np.where(wide_at < cols + LANES // 2, wide_at, wide_at - wide)
     down = jnp.asarray(band(mid_at, tall_at))
-    down_back = jnp.asarray(band(np.arange(rows), mid_at))
+    down_back = jnp.asarray(np.concatenate(band_pieces(band(np.arange(rows), mid_at)), axis=1))
     across = jnp.asarray(band(wide_at, wide_at))
+    across_back = jnp.asarray(np.concatenate(band_pieces(band(wide_at, np.arange(cols))), axis=0))
     slot_grads = call(
         back_kernel,
         jax.ShapeDtypeStruct((devices, SUBS, LANES), F32),
@@ -1130,24 +1110,22 @@
             pltpu.VMEM((3, rows, cols), F32),
             pltpu.VMEM((entries, pixels), F32),
             pltpu.VMEM((entries, 2 * pixels), BF16),
-            pltpu.VMEM((entries, pixels), F32),
-            pltpu.VMEM((entries, 2 * pixels), BF16),
             pltpu.VMEM((groups * 6 * GROUP, 2 * pixels), F32),
             pltpu.VMEM((2 * SUBS, entries), F32),
-            pltpu.VMEM((2 * devices * (SUBS + 1), 512), BF16),
+            pltpu.VMEM((2, 2 * devices * (SUBS + 1), 512), BF16),
             pltpu.VMEM((2 * devices * (SUBS + 1), LANES), F32),
             pltpu.VMEM(((SUBS + 1) * SUBS, cols), F32),
             pltpu.VMEM(((SUBS + 1) * SUBS, cols), F32),
-            pltpu.SemaphoreType.DMA((4,)),
+            pltpu.SemaphoreType.DMA((2,)),
         ],
         (0,),
         (
             place, got_a, got_b, image, target, side, entry, feat, alpha, weight,
-            down, down_back, across, mono,
+            down, down_back, across, across_back, mono,
         ),
         1 << 27,
         32 + devices // 8,
-        outside=(1, 2, 8, 9),
+        outside=(1, 2),
     )
     returned = exchange(slot_grads)
     return call(
@@ -1155,7 +1133,7 @@
         jax.ShapeDtypeStruct((count, own), F32),
         [
             pltpu.VMEM((1, slots), jnp.int32),
-            pltpu.VMEM((2 * high * (SUBS + 1), 4 * LANES), BF16),
+            pltpu.VMEM((2, 2 * high * (SUBS + 1), 4 * LANES), BF16),
             pltpu.VMEM((2 * high * (SUBS + 1), LANES), F32),
             pltpu.VMEM((count * SUBS, LANES), F32),
             pltpu.VMEM((JAC_ROWS * high, LANES), F32),

time: 81 us -> 76.5 us (0.944)
  Pallas kernels: 33.3 us -> 29 us
    pallas_call x7, Pallas kernels: 33.3 us -> 29 us  [call(): pl.pallas_call(body, out_shape=out_shape, in_specs=in_specs, out_specs=ou...]
    unnamed x22 -> x24, local copies, waits for them, and re-layouts: 3.02 us -> 3.02 us
  transfers between devices with their start and end apart: 6 -> 6, of which waited for: 4 -> 4; matrix products, arithmetic and copies ran while one was open for 1% -> 1% of each run, Pallas kernels for 4% -> 5%
where the time goes in v4:
time: 76.5 us; the launch traced here: 76.2 us
  Pallas kernels  29 us (38%)
  blocking collectives  18 us (24%)
  starting transfers between devices  14.7 us (19%)
  waiting for transfers between devices  10.7 us (14%)
  local copies, waits for them, and re-layouts  3.56 us (5%)
    pallas_call x7, Pallas kernels, call(): pl.pallas_call(body, out_shape=out_shape, in_specs=in_specs, out_specs=ou...  29 us
    all_to_all x1, blocking collectives, exchange(): lax.all_to_all(payload, ('img', 'cell'), split_axis=0, concat_axis=0, til...  18 us
    all_to_all x2, starting transfers between devices, exchange(): lax.all_to_all(payload, ('img', 'cell'), split_axis=0, concat_axis=0, til...  12 us
    all_to_all x2, waiting for transfers between devices, exchange(): lax.all_to_all(payload, ('img', 'cell'), split_axis=0, concat_axis=0, til...  8.27 us
    unnamed x24, local copies, waits for them, and re-layouts  3.02 us
    ppermute x2, waiting for transfers between devices, swap(): got_a = lax.ppermute(value_a, axis, swap_pairs(count, 0))  2.39 us
  transfers between devices with their start and end apart: 6, of which 4 were waited for; matrix products, arithmetic and copies ran while one was open for 1% of the time, Pallas kernels for 5%

profile of v4, /device:TPU:0, one launch (start us, length us, event | category | flops | bytes accessed | tf_op | source)
XLA Modules:
  0.0 76.2 jit_solution(4246533026295419137)
XLA Ops:
  0.0 0.0 copy-start.4
  0.0 0.0 copy-start.9
  0.0 0.7 copy-done.9
  0.7 0.0 copy-start.11
  0.7 0.0 copy-start.10
  0.7 0.6 shard_map.110
  1.3 7.3 %all-to-all-start = ((s32[32,1,128]{2,1,0:T(1,128)}), s32[32,1,128]{2,1,0:T(1,128)S(1)}, u32[]{:S(2)}, u32[]{:S(2)}) async-start(s32[32,1,128]{2,1,0:T(1,128)} %bitcast.3), calls=%async_computation | async-start | bytes 32768 | tf_op jit(solution)/shard_map/all_to_all | solution.py:975
  8.6 0.1 pad_add_fusion.place_ref
  8.7 0.0 copy-start
  8.7 1.6 %copy-done = f32[59,8192]{1,0:T(8,128)S(1)} copy-done((f32[59,8192]{1,0:T(8,128)S(1)}, f32[59,8192]{1,0:T(8,128)}, u32[]{:S(2)}) %copy-start) | copy-done | bytes 1933336
  10.3 0.0 copy-start.7
  10.3 0.7 copy-done.7
  11.0 0.0 copy-start.1
  11.0 0.0 copy-start.2
  11.0 0.0 copy-start.3
  11.0 0.0 copy-start.5
  11.0 0.0 copy-start.6
  11.0 3.5 %shard_map.109 = (bf16[576,256]{1,0:T(8,128)(2,1)S(1)}, f32[3264,128]{1,0:T(8,128)S(1)}) custom-call(f32[59,8192]{1,0:T(8,128)S(1)} %copy-done, f32[3,3]{1,0:T(4,128)S(1)} %copy-done.7), custom_call_target="tpu_custom_call" | custom-call | flops 16777216 | bytes 1048576 | tf_op jit(solution)/shard_map/pallas_call | solution.py:949
  14.5 1.1 %all-to-all-done = s32[32,1,128]{2,1,0:T(1,128)S(1)} async-done(((s32[32,1,128]{2,1,0:T(1,128)}), s32[32,1,128]{2,1,0:T(1,128)S(1)}, u32[]{:S(2)}, u32[]{:S(2)}) %all-to-all-start) | async-done | bytes 16416 | tf_op jit(solution)/shard_map/all_to_all | solution.py:975
  15.7 2.9 %shard_map.111 = f32[32,8,128]{2,1,0:T(8,128)} custom-call(s32[4]{0:T(128)S(1)} %pad_add_fusion.place_ref, bf16[576,256]{1,0:T(8,128)(2,1)S(1)} %get-tuple-element.16.table_ref, s32[32,128]{1,0:T(8,128)S(1)} %bitcast.12), custom_call_target="tpu_custom_call" | custom-call | flops 16777216 | bytes 1048576 | tf_op jit(solution)/shard_map/pallas_call | solution.py:949
  18.6 4.7 %all-to-all-start.1 = ((f32[32,8,128]{2,1,0:T(8,128)}), f32[32,8,128]{2,1,0:T(8,128)S(1)}, u32[]{:S(2)}, u32[]{:S(2)}) async-start(f32[32,8,128]{2,1,0:T(8,128)} %shard_map.111), calls=%async_computation.1 | async-start | bytes 262144 | tf_op jit(solution)/shard_map/all_to_all | solution.py:975
  23.3 0.0 copy-done.11
  23.3 0.1 lt.24
  23.5 0.2 select_n.15.bias_ref
  23.6 0.0 copy-done.10
  23.6 0.1 copy.15
  23.8 0.2 reshape.40.entry_ref
  23.9 7.1 %all-to-all-done.1.arrived_in = f32[32,8,128]{2,1,0:T(8,128)S(1)} async-done(((f32[32,8,128]{2,1,0:T(8,128)}), f32[32,8,128]{2,1,0:T(8,128)S(1)}, u32[]{:S(2)}, u32[]{:S(2)}) %all-to-all-start.1) | async-done | bytes 131104 | tf_op jit(solution)/shard_map/all_to_all | solution.py:975
  31.1 0.0 copy-done.4
  31.1 0.0 copy-done.1
  31.1 5.8 %shard_map.112 = (f32[3,32,256]{2,1,0:T(8,128)S(1)}, f32[16,4096]{1,0:T(8,128)S(1)}, f32[4096,256]{1,0:T(8,128)S(1)}, bf16[4096,512]{1,0:T(8,128)(2,1)S(1)}, f32...) custom-call(s32[4]{0:T(128)S(1)} %pad_add_fusion.place_ref, f32[32,8,128]{2,1,0:T(8,128)S(1)} %all-to-all-done.1.arrived_in, ...), custom_call_target="tpu_custom_call" | custom-call | flops 67108864 | bytes 1048576 | tf_op jit(solution)/shard_map/pallas_call | solution.py:949
  36.9 1.3 %collective-permute-start = (f32[24,128]{1,0:T(8,128)S(1)}, f32[24,128]{1,0:T(8,128)S(1)}, u32[]{:S(2)}, u32[]{:S(2)}) collective-permute-start(f32[24,128]{1,0:T(8,128)S(1)} %get-tuple-element.17), channel_id=1, source_target_pairs={{0,1},{1,0},{2,3},{3,2},{4,5},{5,4},{6,7},{7,6},{8,9},{9,8},{10,11... | collective-permute-start | bytes 36872 | tf_op jit(solution)/shard_map/ppermute | solution.py:970
  38.2 0.7 collective-permute-start.1
  38.9 1.8 %collective-permute-done.got_a_in = f32[24,128]{1,0:T(8,128)S(1)} collective-permute-done((f32[24,128]{1,0:T(8,128)S(1)}, f32[24,128]{1,0:T(8,128)S(1)}, u32[]{:S(2)}, u32[]{:S(2)}) %collective-permute-start) | collective-permute-done | bytes 12320 | tf_op jit(solution)/shard_map/ppermute | solution.py:970
  40.7 0.0 collective-permute-done.1.got_b_in
  40.7 0.8 %shard_map.113 = (f32[6,32,128]{2,1,0:T(8,128)S(1)}, f32[72,256]{1,0:T(8,128)S(1)}, f32[72,256]{1,0:T(8,128)S(1)}) custom-call(s32[4]{0:T(128)S(1)} %pad_add_fusion.place_ref, f32[24,128]{1,0:T(8,128)S(1)} %collective-permute-done.got_a_in, f32[24,128]{1,0:T(8,128)S(1)} %collective-permute-done.1.got_b_in, f32[3,32,256]{2,1,0:T(8,128)S(1)} %get-tuple-element.19.image_ref, ...), custom_call_target="tpu_custom_call" | custom-call | flops 1048576 | bytes 1048576 | tf_op jit(solution)/shard_map/pallas_call | solution.py:949
  41.5 0.1 collective-permute-start.2
  41.5 0.7 collective-permute-start.3
  42.2 0.6 collective-permute-done.2.got_a_in
  42.8 0.0 collective-permute-done.3.got_b_in
  42.8 0.0 copy-done.2
  42.8 0.0 copy-done.3
  42.8 0.0 copy-done.5
  42.8 0.0 copy-done.6
  42.8 0.0 copy-start.8
  42.8 11.2 %shard_map.114 = f32[32,8,128]{2,1,0:T(8,128)S(1)} custom-call(s32[4]{0:T(128)S(1)} %pad_add_fusion.place_ref, f32[72,256]{1,0:T(8,128)S(1)} %collective-permute-done.2.got_a_in, f32[72,256]{1,0:T(8,128)S(1)} %collective-permute-done.3.got_b_in, f32[3,32,256]{2,1,0:T(8,128)S(1)} %get-tuple-element.19.image_ref, f32[3,32,256]{2,1,0:T(8,128)S(1)} %copy-done.1, ...), custom_call_target="tpu_custom_call" | custom-call | flops 134217728 | bytes 1048576 | tf_op jit(solution)/shard_map/pallas_call | solution.py:949
  54.1 18.0 %all_to_all.21.returned_ref = f32[32,8,128]{2,1,0:T(8,128)S(1)} all-to-all(f32[32,8,128]{2,1,0:T(8,128)S(1)} %shard_map.114), channel_id=1, replica_groups=mesh['img'=4,'cell'=8] {'img','cell'}, dimensions={0} | all-to-all | bytes 262144 | tf_op jit(solution)/shard_map/all_to_all | solution.py:975
  72.1 0.0 copy-done.8
  72.1 4.1 %shard_map.115 = f32[59,8192]{1,0:T(8,128)} custom-call(s32[4]{0:T(128)S(1)} %pad_add_fusion.place_ref, f32[32,8,128]{2,1,0:T(8,128)S(1)} %all_to_all.21.returned_ref, s32[32,128]{1,0:T(8,128)S(1)} %bitcast.13, f32[3264,128]{1,0:T(8,128)S(1)} %get-tuple-element.26.jac_in, f32[3,3]{1,0:T(4,128)S(1)} %copy-done.8), custom_call_target="tpu_custom_call" | custom-call | flops 67108864 | bytes 1048576 | tf_op jit(solution)/shard_map/pallas_call | solution.py:949
  (1 shorter events, 0.0 us)
Async XLA Ops:
  0.0 31.1 %copy-start.4 = (bf16[32,256]{1,0:T(8,128)(2,1)S(1)}, bf16[32,256]{1,0:T(8,128)(2,1)}, u32[]{:S(2)}) copy-start(bf16[32,256]{1,0:T(8,128)(2,1)} %constant.34.mono_ref) | copy-start | bytes 49156
  0.0 0.7 copy-start.9
  0.7 22.6 %copy-start.11 = (s32[2,16]{1,0:T(2,128)S(1)}, s32[2,16]{1,0:T(2,128)}, u32[]{:S(2)}) copy-start(s32[2,16]{1,0:T(2,128)} %param.16) | copy-start | bytes 388
  0.7 22.9 %copy-start.10 = (s32[2,16,128]{2,1,0:T(8,128)S(1)}, s32[2,16,128]{2,1,0:T(8,128)}, u32[]{:S(2)}) copy-start(s32[2,16,128]{2,1,0:T(8,128)} %param.15) | copy-start | bytes 49156
  1.3 14.3 %all-to-all-start = ((s32[32,1,128]{2,1,0:T(1,128)}), s32[32,1,128]{2,1,0:T(1,128)S(1)}, u32[]{:S(2)}, u32[]{:S(2)}) async-start(s32[32,1,128]{2,1,0:T(1,128)} %bitcast.3), calls=%async_computation | async-start | bytes 32768 | tf_op jit(solution)/shard_map/all_to_all | solution.py:975
  8.7 1.6 %copy-start = (f32[59,8192]{1,0:T(8,128)S(1)}, f32[59,8192]{1,0:T(8,128)}, u32[]{:S(2)}) copy-start(f32[59,8192]{1,0:T(8,128)} %attr_ref.1) | copy-start | bytes 5799940
  10.3 0.7 copy-start.7
  11.0 20.1 %copy-start.1 = (f32[3,32,256]{2,1,0:T(8,128)S(1)}, f32[3,32,256]{2,1,0:T(8,128)}, u32[]{:S(2)}) copy-start(f32[3,32,256]{2,1,0:T(8,128)} %target_ref.5) | copy-start | bytes 294916
  11.0 31.8 %copy-start.2 = (bf16[1152,256]{1,0:T(8,128)(2,1)S(1)}, bf16[1152,256]{1,0:T(8,128)(2,1)}, u32[]{:S(2)}) copy-start(bf16[1152,256]{1,0:T(8,128)(2,1)} %constant.30.clone.across_back_ref) | copy-start | bytes 1769476
  11.0 31.8 %copy-start.3 = (f32[384,384]{1,0:T(8,128)S(1)}, f32[384,384]{1,0:T(8,128)}, u32[]{:S(2)}) copy-start(f32[384,384]{1,0:T(8,128)} %constant.29.clone.across_ref) | copy-start | bytes 1769476
  11.0 31.8 %copy-start.5 = (f32[48,64]{1,0:T(8,128)S(1)}, f32[48,64]{1,0:T(8,128)}, u32[]{:S(2)}) copy-start(f32[48,64]{1,0:T(8,128)} %constant.27.clone.down_ref) | copy-start | bytes 36868
  11.0 31.8 %copy-start.6 = (bf16[32,144]{1,0:T(8,128)(2,1)S(1)}, bf16[32,144]{1,0:T(8,128)(2,1)}, u32[]{:S(2)}) copy-start(bf16[32,144]{1,0:T(8,128)(2,1)} %constant.28.clone.down_back_ref) | copy-start | bytes 27652
  18.6 12.4 %all-to-all-start.1 = ((f32[32,8,128]{2,1,0:T(8,128)}), f32[32,8,128]{2,1,0:T(8,128)S(1)}, u32[]{:S(2)}, u32[]{:S(2)}) async-start(f32[32,8,128]{2,1,0:T(8,128)} %shard_map.111), calls=%async_computation.1 | async-start | bytes 262144 | tf_op jit(solution)/shard_map/all_to_all | solution.py:975
  36.9 3.8 %collective-permute-start = (f32[24,128]{1,0:T(8,128)S(1)}, f32[24,128]{1,0:T(8,128)S(1)}, u32[]{:S(2)}, u32[]{:S(2)}) collective-permute-start(f32[24,128]{1,0:T(8,128)S(1)} %get-tuple-element.17), channel_id=1, source_target_pairs={{0,1},{1,0},{2,3},{3,2},{4,5},{5,4},{6,7},{7,6},{8,9},{9,8},{10,11... | collective-permute-start | bytes 36872 | tf_op jit(solution)/shard_map/ppermute | solution.py:970
  38.2 2.5 %collective-permute-start.1 = (f32[24,128]{1,0:T(8,128)S(1)}, f32[24,128]{1,0:T(8,128)S(1)}, u32[]{:S(2)}, u32[]{:S(2)}) collective-permute-start(f32[24,128]{1,0:T(8,128)S(1)} %get-tuple-element.18), channel_id=1, source_target_pairs={{1,2},{2,1},{3,4},{4,3},{5,6},{6,5},{9,10},{10,9},{11,12},{12,11},... | collective-permute-start | bytes 36872 | tf_op jit(solution)/shard_map/ppermute | solution.py:969
  41.5 1.3 %collective-permute-start.2 = (f32[72,256]{1,0:T(8,128)S(1)}, f32[72,256]{1,0:T(8,128)S(1)}, u32[]{:S(2)}, u32[]{:S(2)}) collective-permute-start(f32[72,256]{1,0:T(8,128)S(1)} %get-tuple-element.20), channel_id=1, source_target_pairs={{0,8},{8,0},{16,24},{24,16},{1,9},{9,1},{17,25},{25,17},{2,10},{10... | collective-permute-start | bytes 221192 | tf_op jit(solution)/shard_map/ppermute | solution.py:970
  41.5 1.3 %collective-permute-start.3 = (f32[72,256]{1,0:T(8,128)S(1)}, f32[72,256]{1,0:T(8,128)S(1)}, u32[]{:S(2)}, u32[]{:S(2)}) collective-permute-start(f32[72,256]{1,0:T(8,128)S(1)} %get-tuple-element.21), channel_id=1, source_target_pairs={{8,16},{16,8},{9,17},{17,9},{10,18},{18,10},{11,19},{19,11},{12,20... | collective-permute-start | bytes 221192 | tf_op jit(solution)/shard_map/ppermute | solution.py:969
  42.8 29.3 %copy-start.8 = (f32[3,3]{1,0:T(4,128)S(1)}, f32[3,3]{1,0:T(4,128)}, u32[]{:S(2)}) copy-start(f32[3,3]{1,0:T(4,128)} %cam_ref.3) | copy-start | bytes 112

commit v5 on v4

--- a/solution.py
+++ b/solution.py
@@ -37,6 +37,7 @@
     1.445305721320277,
     -0.5900435899266435,
 )
+UNROLL = 4
 F32 = jnp.float32
 BF16 = jnp.bfloat16
 JAC_ROWS = 51
@@ -289,12 +290,12 @@
             out_ref[peer + 1] = jnp.where(lane_low, pltpu.roll(eight, half, 1), ninth)
 
     def step(index, carry):
-        tops = [look(2 * index + slot, slot) for slot in range(2)]
-        for slot in range(2):
-            pick(2 * index + slot, slot, tops[slot])
+        tops = [look(UNROLL * index + slot, slot) for slot in range(UNROLL)]
+        for slot in range(UNROLL):
+            pick(UNROLL * index + slot, slot, tops[slot])
         return carry
 
-    lax.fori_loop(0, devices // 8, step, 0)
+    lax.fori_loop(0, devices // (4 * UNROLL), step, 0)
 
 
 def spread_colours(feat_ref, start, size):
@@ -386,13 +387,13 @@
         columns = jnp.transpose(coef_ref[slot_number]).astype(BF16)
         alpha_ref[pl.ds(start, chunk), :] = jnp.exp2(dot(columns, mono_ref[...]))
 
-    def gather_two(index, carry):
-        owners = [look(2 * index + number, number) for number in range(2)]
-        for number in range(2):
-            gather(2 * index + number, number, owners[number])
+    def gather_some(index, carry):
+        owners = [look(UNROLL * index + number, number) for number in range(UNROLL)]
+        for number in range(UNROLL):
+            gather(UNROLL * index + number, number, owners[number])
         return carry
 
-    lax.fori_loop(0, entries // (2 * chunk), gather_two, 0)
+    lax.fori_loop(0, entries // (UNROLL * chunk), gather_some, 0)
 
     pixels = TILE * TILE
     step_rows = length * GROUP
@@ -605,9 +606,7 @@
         ):
             at = (channel * 4 + number) * mid
             vert_ref[at : at + mid, :] = dot_full(down, value)
-    for part in range(3):
-        at = part * 4 * mid
-        blur_ref[at : at + 4 * mid, :] = dot_full(vert_ref[at : at + 4 * mid, :], across_ref[...])
+    blur_ref[...] = dot_full(vert_ref[...], across_ref[...])
     line = iota((mid, wide), 0) - SUBS + place_ref[0] * rows
     spot = iota((mid, wide), 1)
     spot = jnp.where(spot < cols + half, spot, spot - wide) + place_ref[1] * cols
@@ -641,10 +640,10 @@
             coef_ref[spot_at : spot_at + rows, :] = dot(
                 down_back, jnp.concatenate([high, rest, high], axis=0)
             )
+    high, rest = two_pieces(coef_ref[...])
+    backs = dot(jnp.concatenate([high, rest, high], axis=1), across_back_ref[...])
     for channel in range(3):
-        at = channel * 3 * rows
-        high, rest = two_pieces(coef_ref[at : at + 3 * rows, :])
-        back = dot(jnp.concatenate([high, rest, high], axis=1), across_back_ref[...])
+        back = backs[channel * 3 * rows : (channel + 1) * 3 * rows]
         shown = image_ref[channel]
         wanted = target_ref[channel]
         gap = shown - wanted
@@ -773,11 +772,11 @@
             mask_ref[part, at : at + peers, :] = jnp.where(hit, piece.astype(F32), 0.0).astype(BF16)
         return dot_nt(mask_ref[part], hot)
 
-    def collect_two(index, carry):
-        sum_ref[...] += collect(2 * index, 0) + collect(2 * index + 1, 1)
+    def collect_some(index, carry):
+        sum_ref[...] += sum(collect(UNROLL * index + part, part) for part in range(UNROLL))
         return carry
 
-    lax.fori_loop(0, entries // (2 * chunk), collect_two, 0)
+    lax.fori_loop(0, entries // (UNROLL * chunk), collect_some, 0)
     lane_low = iota((SUBS, LANES), 1) < half
     for place in range(peers):
         at = place * SUBS
@@ -832,11 +831,11 @@
             mask_ref[part, at : at + high, :] = jnp.where(hit, piece.astype(F32), 0.0).astype(BF16)
         return dot_nt(mask_ref[part], hot)
 
-    def collect_two(index, carry):
-        sum_ref[...] += collect(2 * index, 0) + collect(2 * index + 1, 1)
+    def collect_some(index, carry):
+        sum_ref[...] += sum(collect(UNROLL * index + part, part) for part in range(UNROLL))
         return carry
 
-    lax.fori_loop(0, devices * half // (2 * chunk), collect_two, 0)
+    lax.fori_loop(0, devices * half // (UNROLL * chunk), collect_some, 0)
     jac_copy.wait()
 
     def grad_copy(index):
@@ -1026,14 +1025,14 @@
         jax.ShapeDtypeStruct((devices, SUBS, LANES), F32),
         [
             pltpu.VMEM((1, slots), jnp.int32),
-            pltpu.VMEM((2, high * (SUBS + 1), 2 * LANES), F32),
+            pltpu.VMEM((UNROLL, high * (SUBS + 1), 2 * LANES), F32),
             pltpu.VMEM((devices, LANES), jnp.int32),
             pltpu.SemaphoreType.DMA((1,)),
         ],
         (0,),
         (place, table, got),
         1 << 24,
-        2 + slots // 128,
+        4 + slots // 128,
         outside=(2,),
     )
     arrived = exchange(reply)
@@ -1061,15 +1060,15 @@
             strip,
         ),
         [
-            pltpu.VMEM((2, devices * (SUBS + 1), 512), F32),
-            pltpu.VMEM((2, 32, 512), F32),
+            pltpu.VMEM((UNROLL, devices * (SUBS + 1), 512), F32),
+            pltpu.VMEM((UNROLL, 32, 512), F32),
             pltpu.VMEM((devices, SUBS, LANES), F32),
             pltpu.SemaphoreType.DMA((1,)),
         ],
         (0,),
         (place, arrived, entry, bias, target, mono),
         1 << 26,
-        16 + devices // 8,
+        18 + devices // 6,
         outside=(1,),
     )
     got_a, got_b = swap(send_a, send_b, "cell")
@@ -1112,7 +1111,7 @@
             pltpu.VMEM((entries, 2 * pixels), BF16),
             pltpu.VMEM((groups * 6 * GROUP, 2 * pixels), F32),
             pltpu.VMEM((2 * SUBS, entries), F32),
-            pltpu.VMEM((2, 2 * devices * (SUBS + 1), 512), BF16),
+            pltpu.VMEM((UNROLL, 2 * devices * (SUBS + 1), 512), BF16),
             pltpu.VMEM((2 * devices * (SUBS + 1), LANES), F32),
             pltpu.VMEM(((SUBS + 1) * SUBS, cols), F32),
             pltpu.VMEM(((SUBS + 1) * SUBS, cols), F32),
@@ -1133,7 +1132,7 @@
         jax.ShapeDtypeStruct((count, own), F32),
         [
             pltpu.VMEM((1, slots), jnp.int32),
-            pltpu.VMEM((2, 2 * high * (SUBS + 1), 4 * LANES), BF16),
+            pltpu.VMEM((UNROLL, 2 * high * (SUBS + 1), 4 * LANES), BF16),
             pltpu.VMEM((2 * high * (SUBS + 1), LANES), F32),
             pltpu.VMEM((count * SUBS, LANES), F32),
             pltpu.VMEM((JAC_ROWS * high, LANES), F32),
@@ -1144,7 +1143,7 @@
         (0, 4),
         (place, returned, got, jac, camera),
         1 << 26,
-        12,
+        15,
         outside=(3,),
         outs_outside=(0,),
     )

time: 76.5 us -> 75.1 us (0.982)
  Pallas kernels: 29 us -> 27.4 us
    pallas_call x7, Pallas kernels: 29 us -> 27.4 us  [call(): pl.pallas_call(body, out_shape=out_shape, in_specs=in_specs, out_specs=ou...]
where the time goes in v5:
time: 75.1 us; the launch traced here: 74.8 us
  Pallas kernels  27.4 us (36%)
  blocking collectives  18 us (24%)
  starting transfers between devices  14.9 us (20%)
  waiting for transfers between devices  10.5 us (14%)
  local copies, waits for them, and re-layouts  3.56 us (5%)
    pallas_call x7, Pallas kernels, call(): pl.pallas_call(body, out_shape=out_shape, in_specs=in_specs, out_specs=ou...  27.4 us
    all_to_all x1, blocking collectives, exchange(): lax.all_to_all(payload, ('img', 'cell'), split_axis=0, concat_axis=0, til...  18 us
    all_to_all x2, starting transfers between devices, exchange(): lax.all_to_all(payload, ('img', 'cell'), split_axis=0, concat_axis=0, til...  12 us
    all_to_all x2, waiting for transfers between devices, exchange(): lax.all_to_all(payload, ('img', 'cell'), split_axis=0, concat_axis=0, til...  8.27 us
    unnamed x24, local copies, waits for them, and re-layouts  3.02 us
    ppermute x2, waiting for transfers between devices, swap(): got_a = lax.ppermute(value_a, axis, swap_pairs(count, 0))  2.21 us
  transfers between devices with their start and end apart: 6, of which 4 were waited for; matrix products, arithmetic and copies ran while one was open for 1% of the time, Pallas kernels for 5%

profile of v5, /device:TPU:0, one launch (start us, length us, event | category | flops | bytes accessed | tf_op | source)
XLA Modules:
  0.0 74.8 jit_solution(2052656903505577385)
XLA Ops:
  0.0 0.0 copy-start.4
  0.0 0.0 copy-start.9
  0.0 0.7 copy-done.9
  0.7 0.0 copy-start.11
  0.7 0.0 copy-start.10
  0.7 0.6 shard_map.110
  1.3 7.3 %all-to-all-start = ((s32[32,1,128]{2,1,0:T(1,128)}), s32[32,1,128]{2,1,0:T(1,128)S(1)}, u32[]{:S(2)}, u32[]{:S(2)}) async-start(s32[32,1,128]{2,1,0:T(1,128)} %bitcast.3), calls=%async_computation | async-start | bytes 32768 | tf_op jit(solution)/shard_map/all_to_all | solution.py:974
  8.6 0.1 pad_add_fusion.place_ref
  8.7 0.0 copy-start
  8.7 1.6 %copy-done = f32[59,8192]{1,0:T(8,128)S(1)} copy-done((f32[59,8192]{1,0:T(8,128)S(1)}, f32[59,8192]{1,0:T(8,128)}, u32[]{:S(2)}) %copy-start) | copy-done | bytes 1933336
  10.3 0.0 copy-start.7
  10.3 0.7 copy-done.7
  11.0 0.0 copy-start.1
  11.0 0.0 copy-start.2
  11.0 0.0 copy-start.3
  11.0 0.0 copy-start.5
  11.0 0.0 copy-start.6
  11.0 3.5 %shard_map.109 = (bf16[576,256]{1,0:T(8,128)(2,1)S(1)}, f32[3264,128]{1,0:T(8,128)S(1)}) custom-call(f32[59,8192]{1,0:T(8,128)S(1)} %copy-done, f32[3,3]{1,0:T(4,128)S(1)} %copy-done.7), custom_call_target="tpu_custom_call" | custom-call | flops 16777216 | bytes 1048576 | tf_op jit(solution)/shard_map/pallas_call | solution.py:948
  14.5 1.1 %all-to-all-done = s32[32,1,128]{2,1,0:T(1,128)S(1)} async-done(((s32[32,1,128]{2,1,0:T(1,128)}), s32[32,1,128]{2,1,0:T(1,128)S(1)}, u32[]{:S(2)}, u32[]{:S(2)}) %all-to-all-start) | async-done | bytes 16416 | tf_op jit(solution)/shard_map/all_to_all | solution.py:974
  15.7 2.5 %shard_map.111 = f32[32,8,128]{2,1,0:T(8,128)} custom-call(s32[4]{0:T(128)S(1)} %pad_add_fusion.place_ref, bf16[576,256]{1,0:T(8,128)(2,1)S(1)} %get-tuple-element.16.table_ref, s32[32,128]{1,0:T(8,128)S(1)} %bitcast.12), custom_call_target="tpu_custom_call" | custom-call | flops 16777216 | bytes 1048576 | tf_op jit(solution)/shard_map/pallas_call | solution.py:948
  18.2 4.7 %all-to-all-start.1 = ((f32[32,8,128]{2,1,0:T(8,128)}), f32[32,8,128]{2,1,0:T(8,128)S(1)}, u32[]{:S(2)}, u32[]{:S(2)}) async-start(f32[32,8,128]{2,1,0:T(8,128)} %shard_map.111), calls=%async_computation.1 | async-start | bytes 262144 | tf_op jit(solution)/shard_map/all_to_all | solution.py:974
  22.9 0.0 copy-done.11
  22.9 0.1 lt.24
  23.0 0.2 select_n.15.bias_ref
  23.2 0.0 copy-done.10
  23.2 0.1 copy.15
  23.3 0.2 reshape.40.entry_ref
  23.5 7.1 %all-to-all-done.1.arrived_in = f32[32,8,128]{2,1,0:T(8,128)S(1)} async-done(((f32[32,8,128]{2,1,0:T(8,128)}), f32[32,8,128]{2,1,0:T(8,128)S(1)}, u32[]{:S(2)}, u32[]{:S(2)}) %all-to-all-start.1) | async-done | bytes 131104 | tf_op jit(solution)/shard_map/all_to_all | solution.py:974
  30.6 0.0 copy-done.4
  30.6 0.0 copy-done.1
  30.6 4.9 %shard_map.112 = (f32[3,32,256]{2,1,0:T(8,128)S(1)}, f32[16,4096]{1,0:T(8,128)S(1)}, f32[4096,256]{1,0:T(8,128)S(1)}, bf16[4096,512]{1,0:T(8,128)(2,1)S(1)}, f32...) custom-call(s32[4]{0:T(128)S(1)} %pad_add_fusion.place_ref, f32[32,8,128]{2,1,0:T(8,128)S(1)} %all-to-all-done.1.arrived_in, ...), custom_call_target="tpu_custom_call" | custom-call | flops 67108864 | bytes 1048576 | tf_op jit(solution)/shard_map/pallas_call | solution.py:948
  35.5 1.3 %collective-permute-start = (f32[24,128]{1,0:T(8,128)S(1)}, f32[24,128]{1,0:T(8,128)S(1)}, u32[]{:S(2)}, u32[]{:S(2)}) collective-permute-start(f32[24,128]{1,0:T(8,128)S(1)} %get-tuple-element.17), channel_id=1, source_target_pairs={{0,1},{1,0},{2,3},{3,2},{4,5},{5,4},{6,7},{7,6},{8,9},{9,8},{10,11... | collective-permute-start | bytes 36872 | tf_op jit(solution)/shard_map/ppermute | solution.py:969
  36.8 0.7 collective-permute-start.1
  37.4 1.8 %collective-permute-done.got_a_in = f32[24,128]{1,0:T(8,128)S(1)} collective-permute-done((f32[24,128]{1,0:T(8,128)S(1)}, f32[24,128]{1,0:T(8,128)S(1)}, u32[]{:S(2)}, u32[]{:S(2)}) %collective-permute-start) | collective-permute-done | bytes 12320 | tf_op jit(solution)/shard_map/ppermute | solution.py:969
  39.3 0.0 collective-permute-done.1.got_b_in
  39.3 0.8 %shard_map.113 = (f32[6,32,128]{2,1,0:T(8,128)S(1)}, f32[72,256]{1,0:T(8,128)S(1)}, f32[72,256]{1,0:T(8,128)S(1)}) custom-call(s32[4]{0:T(128)S(1)} %pad_add_fusion.place_ref, f32[24,128]{1,0:T(8,128)S(1)} %collective-permute-done.got_a_in, f32[24,128]{1,0:T(8,128)S(1)} %collective-permute-done.1.got_b_in, f32[3,32,256]{2,1,0:T(8,128)S(1)} %get-tuple-element.19.image_ref, ...), custom_call_target="tpu_custom_call" | custom-call | flops 1048576 | bytes 1048576 | tf_op jit(solution)/shard_map/pallas_call | solution.py:948
  40.1 0.1 collective-permute-start.2
  40.1 0.8 %collective-permute-start.3 = (f32[72,256]{1,0:T(8,128)S(1)}, f32[72,256]{1,0:T(8,128)S(1)}, u32[]{:S(2)}, u32[]{:S(2)}) collective-permute-start(f32[72,256]{1,0:T(8,128)S(1)} %get-tuple-element.21), channel_id=1, source_target_pairs={{8,16},{16,8},{9,17},{17,9},{10,18},{18,10},{11,19},{19,11},{12,20... | collective-permute-start | bytes 221192 | tf_op jit(solution)/shard_map/ppermute | solution.py:968
  41.0 0.4 collective-permute-done.2.got_a_in
  41.4 0.0 collective-permute-done.3.got_b_in
  41.4 0.0 copy-done.2
  41.4 0.0 copy-done.3
  41.4 0.0 copy-done.5
  41.4 0.0 copy-done.6
  41.4 0.0 copy-start.8
  41.4 11.4 %shard_map.114 = f32[32,8,128]{2,1,0:T(8,128)S(1)} custom-call(s32[4]{0:T(128)S(1)} %pad_add_fusion.place_ref, f32[72,256]{1,0:T(8,128)S(1)} %collective-permute-done.2.got_a_in, f32[72,256]{1,0:T(8,128)S(1)} %collective-permute-done.3.got_b_in, f32[3,32,256]{2,1,0:T(8,128)S(1)} %get-tuple-element.19.image_ref, f32[3,32,256]{2,1,0:T(8,128)S(1)} %copy-done.1, ...), custom_call_target="tpu_custom_call" | custom-call | flops 134217728 | bytes 1048576 | tf_op jit(solution)/shard_map/pallas_call | solution.py:948
  52.8 18.0 %all_to_all.21.returned_ref = f32[32,8,128]{2,1,0:T(8,128)S(1)} all-to-all(f32[32,8,128]{2,1,0:T(8,128)S(1)} %shard_map.114), channel_id=1, replica_groups=mesh['img'=4,'cell'=8] {'img','cell'}, dimensions={0} | all-to-all | bytes 262144 | tf_op jit(solution)/shard_map/all_to_all | solution.py:974
  70.8 0.0 copy-done.8
  70.8 3.8 %shard_map.115 = f32[59,8192]{1,0:T(8,128)} custom-call(s32[4]{0:T(128)S(1)} %pad_add_fusion.place_ref, f32[32,8,128]{2,1,0:T(8,128)S(1)} %all_to_all.21.returned_ref, s32[32,128]{1,0:T(8,128)S(1)} %bitcast.13, f32[3264,128]{1,0:T(8,128)S(1)} %get-tuple-element.26.jac_in, f32[3,3]{1,0:T(4,128)S(1)} %copy-done.8), custom_call_target="tpu_custom_call" | custom-call | flops 67108864 | bytes 1048576 | tf_op jit(solution)/shard_map/pallas_call | solution.py:948
  (1 shorter events, 0.0 us)
Async XLA Ops:
  0.0 30.6 %copy-start.4 = (bf16[32,256]{1,0:T(8,128)(2,1)S(1)}, bf16[32,256]{1,0:T(8,128)(2,1)}, u32[]{:S(2)}) copy-start(bf16[32,256]{1,0:T(8,128)(2,1)} %constant.34.mono_ref) | copy-start | bytes 49156
  0.0 0.7 copy-start.9
  0.7 22.2 %copy-start.11 = (s32[2,16]{1,0:T(2,128)S(1)}, s32[2,16]{1,0:T(2,128)}, u32[]{:S(2)}) copy-start(s32[2,16]{1,0:T(2,128)} %param.16) | copy-start | bytes 388
  0.7 22.5 %copy-start.10 = (s32[2,16,128]{2,1,0:T(8,128)S(1)}, s32[2,16,128]{2,1,0:T(8,128)}, u32[]{:S(2)}) copy-start(s32[2,16,128]{2,1,0:T(8,128)} %param.15) | copy-start | bytes 49156
  1.3 14.3 %all-to-all-start = ((s32[32,1,128]{2,1,0:T(1,128)}), s32[32,1,128]{2,1,0:T(1,128)S(1)}, u32[]{:S(2)}, u32[]{:S(2)}) async-start(s32[32,1,128]{2,1,0:T(1,128)} %bitcast.3), calls=%async_computation | async-start | bytes 32768 | tf_op jit(solution)/shard_map/all_to_all | solution.py:974
  8.7 1.6 %copy-start = (f32[59,8192]{1,0:T(8,128)S(1)}, f32[59,8192]{1,0:T(8,128)}, u32[]{:S(2)}) copy-start(f32[59,8192]{1,0:T(8,128)} %attr_ref.1) | copy-start | bytes 5799940
  10.3 0.7 copy-start.7
  11.0 19.6 %copy-start.1 = (f32[3,32,256]{2,1,0:T(8,128)S(1)}, f32[3,32,256]{2,1,0:T(8,128)}, u32[]{:S(2)}) copy-start(f32[3,32,256]{2,1,0:T(8,128)} %target_ref.5) | copy-start | bytes 294916
  11.0 30.4 %copy-start.2 = (bf16[1152,256]{1,0:T(8,128)(2,1)S(1)}, bf16[1152,256]{1,0:T(8,128)(2,1)}, u32[]{:S(2)}) copy-start(bf16[1152,256]{1,0:T(8,128)(2,1)} %constant.30.clone.across_back_ref) | copy-start | bytes 1769476
  11.0 30.4 %copy-start.3 = (f32[384,384]{1,0:T(8,128)S(1)}, f32[384,384]{1,0:T(8,128)}, u32[]{:S(2)}) copy-start(f32[384,384]{1,0:T(8,128)} %constant.29.clone.across_ref) | copy-start | bytes 1769476
  11.0 30.4 %copy-start.5 = (f32[48,64]{1,0:T(8,128)S(1)}, f32[48,64]{1,0:T(8,128)}, u32[]{:S(2)}) copy-start(f32[48,64]{1,0:T(8,128)} %constant.27.clone.down_ref) | copy-start | bytes 36868
  11.0 30.4 %copy-start.6 = (bf16[32,144]{1,0:T(8,128)(2,1)S(1)}, bf16[32,144]{1,0:T(8,128)(2,1)}, u32[]{:S(2)}) copy-start(bf16[32,144]{1,0:T(8,128)(2,1)} %constant.28.clone.down_back_ref) | copy-start | bytes 27652
  18.2 12.4 %all-to-all-start.1 = ((f32[32,8,128]{2,1,0:T(8,128)}), f32[32,8,128]{2,1,0:T(8,128)S(1)}, u32[]{:S(2)}, u32[]{:S(2)}) async-start(f32[32,8,128]{2,1,0:T(8,128)} %shard_map.111), calls=%async_computation.1 | async-start | bytes 262144 | tf_op jit(solution)/shard_map/all_to_all | solution.py:974
  35.5 3.8 %collective-permute-start = (f32[24,128]{1,0:T(8,128)S(1)}, f32[24,128]{1,0:T(8,128)S(1)}, u32[]{:S(2)}, u32[]{:S(2)}) collective-permute-start(f32[24,128]{1,0:T(8,128)S(1)} %get-tuple-element.17), channel_id=1, source_target_pairs={{0,1},{1,0},{2,3},{3,2},{4,5},{5,4},{6,7},{7,6},{8,9},{9,8},{10,11... | collective-permute-start | bytes 36872 | tf_op jit(solution)/shard_map/ppermute | solution.py:969
  36.8 2.5 %collective-permute-start.1 = (f32[24,128]{1,0:T(8,128)S(1)}, f32[24,128]{1,0:T(8,128)S(1)}, u32[]{:S(2)}, u32[]{:S(2)}) collective-permute-start(f32[24,128]{1,0:T(8,128)S(1)} %get-tuple-element.18), channel_id=1, source_target_pairs={{1,2},{2,1},{3,4},{4,3},{5,6},{6,5},{9,10},{10,9},{11,12},{12,11},... | collective-permute-start | bytes 36872 | tf_op jit(solution)/shard_map/ppermute | solution.py:968
  40.1 1.3 %collective-permute-start.2 = (f32[72,256]{1,0:T(8,128)S(1)}, f32[72,256]{1,0:T(8,128)S(1)}, u32[]{:S(2)}, u32[]{:S(2)}) collective-permute-start(f32[72,256]{1,0:T(8,128)S(1)} %get-tuple-element.20), channel_id=1, source_target_pairs={{0,8},{8,0},{16,24},{24,16},{1,9},{9,1},{17,25},{25,17},{2,10},{10... | collective-permute-start | bytes 221192 | tf_op jit(solution)/shard_map/ppermute | solution.py:969
  40.1 1.3 %collective-permute-start.3 = (f32[72,256]{1,0:T(8,128)S(1)}, f32[72,256]{1,0:T(8,128)S(1)}, u32[]{:S(2)}, u32[]{:S(2)}) collective-permute-start(f32[72,256]{1,0:T(8,128)S(1)} %get-tuple-element.21), channel_id=1, source_target_pairs={{8,16},{16,8},{9,17},{17,9},{10,18},{18,10},{11,19},{19,11},{12,20... | collective-permute-start | bytes 221192 | tf_op jit(solution)/shard_map/ppermute | solution.py:968
  41.4 29.4 %copy-start.8 = (f32[3,3]{1,0:T(4,128)S(1)}, f32[3,3]{1,0:T(4,128)}, u32[]{:S(2)}) copy-start(f32[3,3]{1,0:T(4,128)} %cam_ref.3) | copy-start | bytes 112

commit v6 on v5

--- a/solution.py
+++ b/solution.py
@@ -605,7 +605,10 @@
             [shown, wanted, shown * shown + wanted * wanted, shown * wanted]
         ):
             at = (channel * 4 + number) * mid
-            vert_ref[at : at + mid, :] = dot_full(down, value)
+            one, two, three = three_pieces(value)
+            vert_ref[at : at + mid, :] = dot(
+                down, jnp.concatenate([one, two, three, one, two, one], axis=0)
+            )
     blur_ref[...] = dot_full(vert_ref[...], across_ref[...])
     line = iota((mid, wide), 0) - SUBS + place_ref[0] * rows
     spot = iota((mid, wide), 1)
@@ -919,6 +922,14 @@
     return [high, high, rest]
 
 
+def band_six(values):
+    one = values.astype(ml_dtypes.bfloat16)
+    rest = values - one.astype(np.float32)
+    two = rest.astype(ml_dtypes.bfloat16)
+    three = (rest - two.astype(np.float32)).astype(ml_dtypes.bfloat16)
+    return np.concatenate([one, one, one, two, two, three], axis=1)
+
+
 def monomials():
     pixel = np.arange(TILE * TILE)
     x = (pixel % TILE) - 7.5
@@ -1094,7 +1105,7 @@
     mid_at = np.arange(mid) - SUBS
     wide_at = np.arange(wide)
     wide_at = np.where(wide_at < cols + LANES // 2, wide_at, wide_at - wide)
-    down = jnp.asarray(band(mid_at, tall_at))
+    down = jnp.asarray(band_six(band(mid_at, tall_at)))
     down_back = jnp.asarray(np.concatenate(band_pieces(band(np.arange(rows), mid_at)), axis=1))
     across = jnp.asarray(band(wide_at, wide_at))
     across_back = jnp.asarray(np.concatenate(band_pieces(band(wide_at, np.arange(cols))), axis=0))

time: 75.1 us -> 74.8 us (level)
  no operation moved by 1% of the time
where the time goes in v6:
time: 74.8 us; the launch traced here: 74.4 us
  Pallas kernels  27.2 us (36%)
  blocking collectives  18 us (24%)
  starting transfers between devices  14.7 us (20%)
  waiting for transfers between devices  10.7 us (14%)
  local copies, waits for them, and re-layouts  3.56 us (5%)
    pallas_call x7, Pallas kernels, call(): pl.pallas_call(body, out_shape=out_shape, in_specs=in_specs, out_specs=ou...  27.2 us
    all_to_all x1, blocking collectives, exchange(): lax.all_to_all(payload, ('img', 'cell'), split_axis=0, concat_axis=0, til...  18 us
    all_to_all x2, starting transfers between devices, exchange(): lax.all_to_all(payload, ('img', 'cell'), split_axis=0, concat_axis=0, til...  12 us
    all_to_all x2, waiting for transfers between devices, exchange(): lax.all_to_all(payload, ('img', 'cell'), split_axis=0, concat_axis=0, til...  8.27 us
    unnamed x24, local copies, waits for them, and re-layouts  3.02 us
    ppermute x2, waiting for transfers between devices, swap(): got_a = lax.ppermute(value_a, axis, swap_pairs(count, 0))  2.39 us
  transfers between devices with their start and end apart: 6, of which 4 were waited for; matrix products, arithmetic and copies ran while one was open for 1% of the time, Pallas kernels for 5%

profile of v6, /device:TPU:0, one launch (start us, length us, event | category | flops | bytes accessed | tf_op | source)
XLA Modules:
  0.0 74.4 jit_solution(8235597179122083381)
XLA Ops:
  0.0 0.0 copy-start.4
  0.0 0.0 copy-start.9
  0.0 0.7 copy-done.9
  0.7 0.0 copy-start.11
  0.7 0.0 copy-start.10
  0.7 0.6 shard_map.110
  1.3 7.3 %all-to-all-start = ((s32[32,1,128]{2,1,0:T(1,128)}), s32[32,1,128]{2,1,0:T(1,128)S(1)}, u32[]{:S(2)}, u32[]{:S(2)}) async-start(s32[32,1,128]{2,1,0:T(1,128)} %bitcast.3), calls=%async_computation | async-start | bytes 32768 | tf_op jit(solution)/shard_map/all_to_all | solution.py:985
  8.6 0.1 pad_add_fusion.place_ref
  8.7 0.0 copy-start
  8.7 1.6 %copy-done = f32[59,8192]{1,0:T(8,128)S(1)} copy-done((f32[59,8192]{1,0:T(8,128)S(1)}, f32[59,8192]{1,0:T(8,128)}, u32[]{:S(2)}) %copy-start) | copy-done | bytes 1933336
  10.3 0.0 copy-start.7
  10.3 0.7 copy-done.7
  11.0 0.0 copy-start.1
  11.0 0.0 copy-start.2
  11.0 0.0 copy-start.3
  11.0 0.0 copy-start.5
  11.0 0.0 copy-start.6
  11.0 3.5 %shard_map.109 = (bf16[576,256]{1,0:T(8,128)(2,1)S(1)}, f32[3264,128]{1,0:T(8,128)S(1)}) custom-call(f32[59,8192]{1,0:T(8,128)S(1)} %copy-done, f32[3,3]{1,0:T(4,128)S(1)} %copy-done.7), custom_call_target="tpu_custom_call" | custom-call | flops 16777216 | bytes 1048576 | tf_op jit(solution)/shard_map/pallas_call | solution.py:959
  14.5 1.1 %all-to-all-done = s32[32,1,128]{2,1,0:T(1,128)S(1)} async-done(((s32[32,1,128]{2,1,0:T(1,128)}), s32[32,1,128]{2,1,0:T(1,128)S(1)}, u32[]{:S(2)}, u32[]{:S(2)}) %all-to-all-start) | async-done | bytes 16416 | tf_op jit(solution)/shard_map/all_to_all | solution.py:985
  15.7 2.5 %shard_map.111 = f32[32,8,128]{2,1,0:T(8,128)} custom-call(s32[4]{0:T(128)S(1)} %pad_add_fusion.place_ref, bf16[576,256]{1,0:T(8,128)(2,1)S(1)} %get-tuple-element.16.table_ref, s32[32,128]{1,0:T(8,128)S(1)} %bitcast.12), custom_call_target="tpu_custom_call" | custom-call | flops 16777216 | bytes 1048576 | tf_op jit(solution)/shard_map/pallas_call | solution.py:959
  18.2 4.7 %all-to-all-start.1 = ((f32[32,8,128]{2,1,0:T(8,128)}), f32[32,8,128]{2,1,0:T(8,128)S(1)}, u32[]{:S(2)}, u32[]{:S(2)}) async-start(f32[32,8,128]{2,1,0:T(8,128)} %shard_map.111), calls=%async_computation.1 | async-start | bytes 262144 | tf_op jit(solution)/shard_map/all_to_all | solution.py:985
  22.9 0.0 copy-done.11
  22.9 0.1 lt.24
  23.0 0.2 select_n.15.bias_ref
  23.2 0.0 copy-done.10
  23.2 0.1 copy.15
  23.3 0.2 reshape.40.entry_ref
  23.5 7.1 %all-to-all-done.1.arrived_in = f32[32,8,128]{2,1,0:T(8,128)S(1)} async-done(((f32[32,8,128]{2,1,0:T(8,128)}), f32[32,8,128]{2,1,0:T(8,128)S(1)}, u32[]{:S(2)}, u32[]{:S(2)}) %all-to-all-start.1) | async-done | bytes 131104 | tf_op jit(solution)/shard_map/all_to_all | solution.py:985
  30.6 0.0 copy-done.4
  30.6 0.0 copy-done.1
  30.6 4.9 %shard_map.112 = (f32[3,32,256]{2,1,0:T(8,128)S(1)}, f32[16,4096]{1,0:T(8,128)S(1)}, f32[4096,256]{1,0:T(8,128)S(1)}, bf16[4096,512]{1,0:T(8,128)(2,1)S(1)}, f32...) custom-call(s32[4]{0:T(128)S(1)} %pad_add_fusion.place_ref, f32[32,8,128]{2,1,0:T(8,128)S(1)} %all-to-all-done.1.arrived_in, ...), custom_call_target="tpu_custom_call" | custom-call | flops 67108864 | bytes 1048576 | tf_op jit(solution)/shard_map/pallas_call | solution.py:959
  35.5 1.3 %collective-permute-start = (f32[24,128]{1,0:T(8,128)S(1)}, f32[24,128]{1,0:T(8,128)S(1)}, u32[]{:S(2)}, u32[]{:S(2)}) collective-permute-start(f32[24,128]{1,0:T(8,128)S(1)} %get-tuple-element.17), channel_id=1, source_target_pairs={{0,1},{1,0},{2,3},{3,2},{4,5},{5,4},{6,7},{7,6},{8,9},{9,8},{10,11... | collective-permute-start | bytes 36872 | tf_op jit(solution)/shard_map/ppermute | solution.py:980
  36.8 0.7 collective-permute-start.1
  37.4 1.8 %collective-permute-done.got_a_in = f32[24,128]{1,0:T(8,128)S(1)} collective-permute-done((f32[24,128]{1,0:T(8,128)S(1)}, f32[24,128]{1,0:T(8,128)S(1)}, u32[]{:S(2)}, u32[]{:S(2)}) %collective-permute-start) | collective-permute-done | bytes 12320 | tf_op jit(solution)/shard_map/ppermute | solution.py:980
  39.3 0.0 collective-permute-done.1.got_b_in
  39.3 0.8 %shard_map.113 = (f32[6,32,128]{2,1,0:T(8,128)S(1)}, f32[72,256]{1,0:T(8,128)S(1)}, f32[72,256]{1,0:T(8,128)S(1)}) custom-call(s32[4]{0:T(128)S(1)} %pad_add_fusion.place_ref, f32[24,128]{1,0:T(8,128)S(1)} %collective-permute-done.got_a_in, f32[24,128]{1,0:T(8,128)S(1)} %collective-permute-done.1.got_b_in, f32[3,32,256]{2,1,0:T(8,128)S(1)} %get-tuple-element.19.image_ref, ...), custom_call_target="tpu_custom_call" | custom-call | flops 1048576 | bytes 1048576 | tf_op jit(solution)/shard_map/pallas_call | solution.py:959
  40.1 0.1 collective-permute-start.2
  40.1 0.7 collective-permute-start.3
  40.8 0.6 collective-permute-done.2.got_a_in
  41.4 0.0 collective-permute-done.3.got_b_in
  41.4 0.0 copy-done.2
  41.4 0.0 copy-done.3
  41.4 0.0 copy-done.5
  41.4 0.0 copy-done.6
  41.4 0.0 copy-start.8
  41.4 11.2 %shard_map.114 = f32[32,8,128]{2,1,0:T(8,128)S(1)} custom-call(s32[4]{0:T(128)S(1)} %pad_add_fusion.place_ref, f32[72,256]{1,0:T(8,128)S(1)} %collective-permute-done.2.got_a_in, f32[72,256]{1,0:T(8,128)S(1)} %collective-permute-done.3.got_b_in, f32[3,32,256]{2,1,0:T(8,128)S(1)} %get-tuple-element.19.image_ref, f32[3,32,256]{2,1,0:T(8,128)S(1)} %copy-done.1, ...), custom_call_target="tpu_custom_call" | custom-call | flops 134217728 | bytes 1048576 | tf_op jit(solution)/shard_map/pallas_call | solution.py:959
  52.6 18.0 %all_to_all.21.returned_ref = f32[32,8,128]{2,1,0:T(8,128)S(1)} all-to-all(f32[32,8,128]{2,1,0:T(8,128)S(1)} %shard_map.114), channel_id=1, replica_groups=mesh['img'=4,'cell'=8] {'img','cell'}, dimensions={0} | all-to-all | bytes 262144 | tf_op jit(solution)/shard_map/all_to_all | solution.py:985
  70.6 0.0 copy-done.8
  70.6 3.8 %shard_map.115 = f32[59,8192]{1,0:T(8,128)} custom-call(s32[4]{0:T(128)S(1)} %pad_add_fusion.place_ref, f32[32,8,128]{2,1,0:T(8,128)S(1)} %all_to_all.21.returned_ref, s32[32,128]{1,0:T(8,128)S(1)} %bitcast.13, f32[3264,128]{1,0:T(8,128)S(1)} %get-tuple-element.26.jac_in, f32[3,3]{1,0:T(4,128)S(1)} %copy-done.8), custom_call_target="tpu_custom_call" | custom-call | flops 67108864 | bytes 1048576 | tf_op jit(solution)/shard_map/pallas_call | solution.py:959
  (1 shorter events, 0.0 us)
Async XLA Ops:
  0.0 30.6 %copy-start.4 = (bf16[32,256]{1,0:T(8,128)(2,1)S(1)}, bf16[32,256]{1,0:T(8,128)(2,1)}, u32[]{:S(2)}) copy-start(bf16[32,256]{1,0:T(8,128)(2,1)} %constant.34.mono_ref) | copy-start | bytes 49156
  0.0 0.7 copy-start.9
  0.7 22.2 %copy-start.11 = (s32[2,16]{1,0:T(2,128)S(1)}, s32[2,16]{1,0:T(2,128)}, u32[]{:S(2)}) copy-start(s32[2,16]{1,0:T(2,128)} %param.16) | copy-start | bytes 388
  0.7 22.5 %copy-start.10 = (s32[2,16,128]{2,1,0:T(8,128)S(1)}, s32[2,16,128]{2,1,0:T(8,128)}, u32[]{:S(2)}) copy-start(s32[2,16,128]{2,1,0:T(8,128)} %param.15) | copy-start | bytes 49156
  1.3 14.3 %all-to-all-start = ((s32[32,1,128]{2,1,0:T(1,128)}), s32[32,1,128]{2,1,0:T(1,128)S(1)}, u32[]{:S(2)}, u32[]{:S(2)}) async-start(s32[32,1,128]{2,1,0:T(1,128)} %bitcast.3), calls=%async_computation | async-start | bytes 32768 | tf_op jit(solution)/shard_map/all_to_all | solution.py:985
  8.7 1.6 %copy-start = (f32[59,8192]{1,0:T(8,128)S(1)}, f32[59,8192]{1,0:T(8,128)}, u32[]{:S(2)}) copy-start(f32[59,8192]{1,0:T(8,128)} %attr_ref.1) | copy-start | bytes 5799940
  10.3 0.7 copy-start.7
  11.0 19.6 %copy-start.1 = (f32[3,32,256]{2,1,0:T(8,128)S(1)}, f32[3,32,256]{2,1,0:T(8,128)}, u32[]{:S(2)}) copy-start(f32[3,32,256]{2,1,0:T(8,128)} %target_ref.5) | copy-start | bytes 294916
  11.0 30.4 %copy-start.2 = (bf16[1152,256]{1,0:T(8,128)(2,1)S(1)}, bf16[1152,256]{1,0:T(8,128)(2,1)}, u32[]{:S(2)}) copy-start(bf16[1152,256]{1,0:T(8,128)(2,1)} %constant.30.clone.across_back_ref) | copy-start | bytes 1769476
  11.0 30.4 %copy-start.3 = (f32[384,384]{1,0:T(8,128)S(1)}, f32[384,384]{1,0:T(8,128)}, u32[]{:S(2)}) copy-start(f32[384,384]{1,0:T(8,128)} %constant.29.clone.across_ref) | copy-start | bytes 1769476
  11.0 30.4 %copy-start.5 = (bf16[48,384]{1,0:T(8,128)(2,1)S(1)}, bf16[48,384]{1,0:T(8,128)(2,1)}, u32[]{:S(2)}) copy-start(bf16[48,384]{1,0:T(8,128)(2,1)} %constant.27.clone.down_ref) | copy-start | bytes 110596
  11.0 30.4 %copy-start.6 = (bf16[32,144]{1,0:T(8,128)(2,1)S(1)}, bf16[32,144]{1,0:T(8,128)(2,1)}, u32[]{:S(2)}) copy-start(bf16[32,144]{1,0:T(8,128)(2,1)} %constant.28.clone.down_back_ref) | copy-start | bytes 27652
  18.2 12.5 %all-to-all-start.1 = ((f32[32,8,128]{2,1,0:T(8,128)}), f32[32,8,128]{2,1,0:T(8,128)S(1)}, u32[]{:S(2)}, u32[]{:S(2)}) async-start(f32[32,8,128]{2,1,0:T(8,128)} %shard_map.111), calls=%async_computation.1 | async-start | bytes 262144 | tf_op jit(solution)/shard_map/all_to_all | solution.py:985
  35.5 3.8 %collective-permute-start = (f32[24,128]{1,0:T(8,128)S(1)}, f32[24,128]{1,0:T(8,128)S(1)}, u32[]{:S(2)}, u32[]{:S(2)}) collective-permute-start(f32[24,128]{1,0:T(8,128)S(1)} %get-tuple-element.17), channel_id=1, source_target_pairs={{0,1},{1,0},{2,3},{3,2},{4,5},{5,4},{6,7},{7,6},{8,9},{9,8},{10,11... | collective-permute-start | bytes 36872 | tf_op jit(solution)/shard_map/ppermute | solution.py:980
  36.8 2.5 %collective-permute-start.1 = (f32[24,128]{1,0:T(8,128)S(1)}, f32[24,128]{1,0:T(8,128)S(1)}, u32[]{:S(2)}, u32[]{:S(2)}) collective-permute-start(f32[24,128]{1,0:T(8,128)S(1)} %get-tuple-element.18), channel_id=1, source_target_pairs={{1,2},{2,1},{3,4},{4,3},{5,6},{6,5},{9,10},{10,9},{11,12},{12,11},... | collective-permute-start | bytes 36872 | tf_op jit(solution)/shard_map/ppermute | solution.py:979
  40.1 1.3 %collective-permute-start.2 = (f32[72,256]{1,0:T(8,128)S(1)}, f32[72,256]{1,0:T(8,128)S(1)}, u32[]{:S(2)}, u32[]{:S(2)}) collective-permute-start(f32[72,256]{1,0:T(8,128)S(1)} %get-tuple-element.20), channel_id=1, source_target_pairs={{0,8},{8,0},{16,24},{24,16},{1,9},{9,1},{17,25},{25,17},{2,10},{10... | collective-permute-start | bytes 221192 | tf_op jit(solution)/shard_map/ppermute | solution.py:980
  40.1 1.3 %collective-permute-start.3 = (f32[72,256]{1,0:T(8,128)S(1)}, f32[72,256]{1,0:T(8,128)S(1)}, u32[]{:S(2)}, u32[]{:S(2)}) collective-permute-start(f32[72,256]{1,0:T(8,128)S(1)} %get-tuple-element.21), channel_id=1, source_target_pairs={{8,16},{16,8},{9,17},{17,9},{10,18},{18,10},{11,19},{19,11},{12,20... | collective-permute-start | bytes 221192 | tf_op jit(solution)/shard_map/ppermute | solution.py:979
  41.4 29.2 %copy-start.8 = (f32[3,3]{1,0:T(4,128)S(1)}, f32[3,3]{1,0:T(4,128)}, u32[]{:S(2)}) copy-start(f32[3,3]{1,0:T(4,128)} %cam_ref.3) | copy-start | bytes 112
